TPU v7x, 32 devices: a whole 2x2x4 slice. The times are simulated.
32 devices in a mesh: row: 8 (over y, x, core), col: 4 (over z).
Axes of the slice: x: 2, y: 2, z: 4, core: 2. Of those that a mesh axis runs over, the one named last changes fastest.
Arguments:
- features: bfloat16 [16384, 512], P(('col', 'row')), may hold values from -6 to 6
- tile_values: bfloat16 [8, 4, 6, 256, 256], P('row', 'col'), may hold values from -0.21875 to 0.21875
- tile_index: int32 [8, 4, 6], P('row', 'col'), may hold values from 0 to 127, as said below
- tile_count: int32 [8, 4], P('row', 'col'), may hold values from 1 to 6, as said below
- weight: bfloat16 [512, 512], replicated, may hold values from -0.25 to 0.25
- cotangent: bfloat16 [16384, 512], P(('row', 'col')), may hold values from -6 to 6
Outputs:
- output: bfloat16 [16384, 512], P(('row', 'col'))
- weight_grad: float32 [512, 512], replicated
Inputs may be any that keep to these rules, and one draw needn't show every extreme that they name: `tile_index`: on each device the 6 slots hold different tile numbers. `tile_count`: some device has all 6 slots live.
All inputs are finite; a program needn't handle non-finite values.
Results may differ from a plain program's by a relative error of at most 0.024.
Values may be sent and summed in bfloat16 or wider, within the bound.
No kernel may reach another device: no remote copies, remote signals or barrier semaphores. Data moves between devices by JAX's collectives and lax.ppermute only.
A program may use at most 64 MiB of HBM per device.

v0:
```python
import math

import jax
import jax.numpy as jnp
from jax import lax
from jax.sharding import PartitionSpec as P

F = 512
BLK = 256
RBG = 8
KMAX = 6


def local(features, tile_values, tile_index, tile_count, weight, cotangent):
    gathered = lax.all_gather(features, "row", axis=0, tiled=True)
    col_groups = gathered.shape[0] // BLK
    blocks = gathered.reshape(col_groups, BLK, F)
    tile_vals = tile_values[0, 0]
    tile_ids = tile_index[0, 0]
    live_count = tile_count[0, 0]
    row_slot = tile_ids // col_groups
    col_slot = tile_ids % col_groups
    is_live = jnp.arange(KMAX, dtype=jnp.int32) < live_count
    picked = blocks[col_slot]
    products = jnp.einsum("kab,kbf->kaf", tile_vals, picked, preferred_element_type=jnp.float32)
    placing = (
        (row_slot[:, None] == jnp.arange(RBG, dtype=jnp.int32)[None, :]) & is_live[:, None]
    ).astype(jnp.float32)
    partial_value = jnp.einsum("kr,kaf->raf", placing, products)
    rounded = partial_value.reshape(RBG * BLK, F).astype(jnp.bfloat16)
    summed = lax.psum_scatter(rounded, "col", scatter_dimension=0, tiled=True).astype(jnp.float32)
    aggregated = summed.astype(jnp.bfloat16)
    preact = jnp.dot(aggregated, weight, preferred_element_type=jnp.float32)
    output = jnp.where(preact > 0, preact, jnp.expm1(jnp.minimum(preact, 0.0))).astype(jnp.bfloat16)
    slope = jnp.where(preact > 0, 1.0, jnp.exp(jnp.minimum(preact, 0.0)))
    grad_pre = (cotangent.astype(jnp.float32) * slope).astype(jnp.bfloat16)
    grad_scale = 1.0 / math.sqrt(RBG * BLK * lax.axis_size("row"))
    local_grad = jnp.dot(aggregated.T, grad_pre, preferred_element_type=jnp.float32) * grad_scale
    weight_grad = lax.psum(local_grad, ("row", "col"))
    return (output, weight_grad)


def solution(mesh):
    placed = (
        P(("col", "row"), None),
        P("row", "col", None, None, None),
        P("row", "col", None),
        P("row", "col"),
        P(),
        P(("row", "col"), None),
    )
    return jax.shard_map(
        local, mesh=mesh, in_specs=placed, out_specs=(P(("row", "col"), None), P()), check_vma=False
    )
```

profile of v0, /device:TPU:0, one launch (start us, length us, event | category | flops | bytes accessed | tf_op | source)
XLA Modules:
  0.0 248.7 jit_solution(15301075794862174197)
XLA Ops:
  7.2 0.0 copy-start
  7.2 0.0 all-gather.2.cloned.1.call-start
  7.2 0.7 all-gather.2.cloned.1.call-update
  7.9 0.0 reduce-scatter.2.cloned.1.call-start
  8.6 0.7 fusion.19
  9.3 0.7 and_select_fusion.1
  10.0 39.4 %all-gather.2.cloned.1.call-done = bf16[4096,512]{1,0:T(8,128)(2,1)} async-done(((bf16[512,512]{1,0:T(8,128)(2,1)}), bf16[4096,512]{1,0:T(8,128)(2,1)}) %all-gather.2.cloned.1.call-update) | async-done | bytes 4194320 | tf_op jit(solution)/shard_map/all_gather | solution.py:15
  49.4 2.8 %gather_fusion = bf16[6,256,512]{2,1,0:T(8,128)(2,1)S(1)} fusion(bf16[16,256,512]{2,1,0:T(8,128)(2,1)} %bitcast.32, s32[1024]{0:T(1024)S(1)} %pad_clamp_fusion), kind=kCustom, calls=%fused_computation | custom fusion | bytes 3145752 | tf_op jit(solution)/shard_map/gather | solution.py:24
  52.2 0.0 copy-done
  52.2 1.9 fusion.8
  54.1 3.2 %copy.9 = bf16[6,512,256]{1,0,2:T(8,128)(2,1)S(1)} copy(bf16[6,512,256]{2,1,0:T(8,128)(2,1)} %fusion.8) | data formatting | bytes 3145728 | tf_op jit(solution)/shard_map/kab,kbf->kaf/dot_general | solution.py:25
  57.3 0.7 fusion.2
  58.0 2.0 copy.8
  60.1 0.0 reduce-scatter.2.cloned.1.call-update
  60.1 0.0 all-reduce.2.cloned.1.call-start
  60.1 44.0 %reduce-scatter.2.cloned.1.call-done = bf16[512,512]{1,0:T(8,128)(2,1)} async-done(((bf16[2048,512]{1,0:T(8,128)(2,1)}), bf16[512,512]{1,0:T(8,128)(2,1)}) %reduce-scatter.2.cloned.1.call-update) | async-done | bytes 524304 | tf_op jit(solution)/shard_map/reduce_scatter | solution.py:31
  104.1 0.0 copy-done.1
  104.1 2.6 %fusion.5 = (bf16[512,512]{1,0:T(8,128)(2,1)}, f32[512,512]{1,0:T(8,128)S(1)}) fusion(bf16[512,512]{1,0:T(8,128)(2,1)} %reduce-scatter.2.cloned.1.call-done, bf16[512,512]{1,0:T(8,128)(2,1)S(1)} %copy-done.1), kind=kOutput, calls=%fused_computation.7 | convolution fusion | flops 269484032 | bytes 2621440 | tf_op jit(solution)/shard_map/dot_general | solution.py:33
  106.7 0.0 copy-done.2
  106.7 0.0 copy-done.3
  106.7 1.5 convolution_multiply_fusion
  108.2 0.0 all-reduce.2.cloned.1.call-update
  108.2 131.6 %all-reduce.2.cloned.1.call-done = f32[512,512]{1,0:T(8,128)} async-done(((f32[512,512]{1,0:T(8,128)}), f32[512,512]{1,0:T(8,128)}) %all-reduce.2.cloned.1.call-update) | async-done | bytes 1048592 | tf_op jit(solution)/shard_map/psum | solution.py:39
  239.9 2.3 copy.12
  (5 shorter events, 0.0 us)
Async XLA Ops:
  7.2 45.0 %copy-start = (bf16[1,1,6,256,256]{4,3,2,1,0:T(8,128)(2,1)S(1)}, bf16[1,1,6,256,256]{4,3,2,1,0:T(8,128)(2,1)}, u32[]{:S(2)}) copy-start(bf16[1,1,6,256,256]{4,3,2,1,0:T(8,128)(2,1)} %param.7) | copy-start | bytes 2359300
  7.2 42.2 %all-gather.2.cloned.1.call-start = ((), (), s32[]{:S(2)}) async-start(), calls=%async_computation.1 | async-start | bytes 4718592 | tf_op jit(solution)/shard_map/all_gather | solution.py:15
  7.9 96.2 %reduce-scatter.2.cloned.1.call-start = ((), (), s32[]{:S(2)}) async-start(), calls=%async_computation.2 | async-start | bytes 2621440 | tf_op jit(solution)/shard_map/reduce_scatter | solution.py:31
  60.0 44.0 %copy-start.1 = (bf16[512,512]{1,0:T(8,128)(2,1)S(1)}, bf16[512,512]{1,0:T(8,128)(2,1)}, u32[]{:S(2)}) copy-start(bf16[512,512]{1,0:T(8,128)(2,1)} %param.10) | copy-start | bytes 1572868
  60.0 46.6 %copy-start.2 = (bf16[512,512]{1,0:T(8,128)(2,1)S(1)}, bf16[512,512]{1,0:T(8,128)(2,1)}, u32[]{:S(2)}) copy-start(bf16[512,512]{1,0:T(8,128)(2,1)} %param.11) | copy-start | bytes 1572868
  60.1 179.8 %all-reduce.2.cloned.1.call-start = ((), (), s32[]{:S(2)}) async-start(), calls=%async_computation.3 | async-start | bytes 2097152 | tf_op jit(solution)/shard_map/psum | solution.py:39
  104.1 2.6 %copy-start.3 = (bf16[512,512]{1,0:T(8,128)(2,1)S(1)}, bf16[512,512]{1,0:T(8,128)(2,1)}, u32[]{:S(2)}) copy-start(bf16[512,512]{1,0:T(8,128)(2,1)} %reduce-scatter.2.cloned.1.call-done) | copy-start | bytes 1572868
Sparse Core Ops, SparseCore 0:
  9.9 39.4 all-gather.1
  60.2 43.8 reduce-scatter.1
  110.7 129.1 all-reduce.1
where the time goes:
time: 249 us
  waiting for transfers between devices  216 us (87%)
  between operations  14.4 us (6%)
  local copies, waits for them, and re-layouts  10.4 us (4%)
  matrix products  6.67 us (3%)
    psum x1, waiting for transfers between devices, local(): weight_grad = lax.psum(local_grad, ('row', 'col'))  132 us
    reduce_scatter x1, waiting for transfers between devices, local(): lax.psum_scatter(rounded, 'col', scatter_dimension=0, tiled=True)  44 us
    all_gather x1, waiting for transfers between devices, local(): gathered = lax.all_gather(features, 'row', axis=0, tiled=True)  39.4 us
  transfers between devices with their start and end apart: 3, of which 3 were waited for; matrix products, arithmetic and copies ran while one was open for 1% of the time, Pallas kernels for 0%

commit v1 on v0

v1 whole, which is shorter than its diff:
```python
import functools
import math

import jax
import jax.numpy as jnp
from jax import lax
from jax.experimental import pallas as pl
from jax.experimental.pallas import tpu as pltpu
from jax.sharding import PartitionSpec as P

BLK = 256
RBG = 8
CHUNKS = (256, 256)
VMEM_LIMIT = 48 * 1024 * 1024
F32, BF16 = jnp.float32, jnp.bfloat16


def swap(x, axis, mask):
    return lax.ppermute(x, axis, [(i, i ^ mask) for i in range(lax.axis_size(axis))])


def bit_reversed(i, bits):
    out = 0 * i
    for b in range(bits):
        out = out + (((i >> b) & 1) << (bits - 1 - b))
    return out


def gather_row(x):
    n = lax.axis_size("row")
    half = x.shape[0] // 2
    got = {0: x}
    for k in sorted(range(2, n, 2), key=lambda k: (bin(k).count("1"), k)):
        low, high = k & -k, 1 << (k.bit_length() - 1)
        if low == high:
            got[k] = swap(x, "row", k)
        else:
            top = swap(got[k ^ high][:half], "row", high)
            bottom = swap(got[k ^ low][half:], "row", low)
            got[k] = jnp.concatenate([top, bottom])
    for k in range(0, n, 2):
        got[k + 1] = swap(got[k], "row", 1)
    return [got[k] for k in range(n)]


def tiles_kernel(me_ref, index_ref, count_ref, tiles_ref, *refs, n_row, n_col):
    pieces, (low_ref, high_ref, picked, total) = refs[:n_row], refs[n_row:]
    kmax = tiles_ref.shape[0]
    rows = pieces[0].shape[0]
    part = min(BLK, rows)
    own = RBG * BLK // n_col
    step = min(BLK, own)
    bits = n_col.bit_length() - 1
    col_groups = rows * n_row // BLK
    me_row, me_col = me_ref[0], me_ref[1]
    total[...] = jnp.zeros_like(total)
    for k in range(kmax):
        number = index_ref[k]
        row_slot, col_slot = number // col_groups, number % col_groups
        live = k < count_ref[0]

        @pl.when(live)
        def _(k=k, row_slot=row_slot, col_slot=col_slot):
            for j in range(BLK // part):
                first = col_slot * BLK + j * part
                owner = (first // rows) ^ me_row
                offset = pl.multiple_of(first % rows, part)
                for p in range(n_row):
                    @pl.when(owner == p)
                    def _(p=p):
                        picked[j * part:(j + 1) * part, :] = pieces[p][pl.ds(offset, part), :]
            product = jnp.dot(tiles_ref[k], picked[...], preferred_element_type=F32)
            for j in range(BLK // step):
                first = row_slot * BLK + j * step
                place = bit_reversed((first // own) ^ me_col, bits) * own + first % own
                place = pl.ds(pl.multiple_of(place, step), step)
                total[place, :] += product[j * step:(j + 1) * step, :]
    middle = total.shape[0] // 2
    low_ref[...] = total[:middle, :].astype(BF16)
    high_ref[...] = total[middle:, :].astype(BF16)


def tile_products(me, index, count, tiles, pieces):
    n_row, n_col = lax.axis_size("row"), lax.axis_size("col")
    wide = pieces[0].shape[1]
    half = jax.ShapeDtypeStruct((RBG * BLK // 2, wide), BF16)
    smem, vmem = pl.BlockSpec(memory_space=pltpu.SMEM), pl.BlockSpec(memory_space=pltpu.VMEM)
    return pl.pallas_call(
        functools.partial(tiles_kernel, n_row=n_row, n_col=n_col),
        out_shape=(half, half),
        in_specs=[smem] * 3 + [vmem] * (1 + n_row),
        out_specs=(vmem, vmem),
        scratch_shapes=[pltpu.VMEM((BLK, wide), BF16), pltpu.VMEM((RBG * BLK, wide), F32)],
        compiler_params=pltpu.CompilerParams(vmem_limit_bytes=VMEM_LIMIT),
        cost_estimate=pl.CostEstimate(
            flops=2 * tiles.shape[0] * BLK * BLK * wide, bytes_accessed=6 * 1024 * 1024, transcendentals=0),
    )(me, index, count, tiles, *pieces)


def vertex_kernel(me_ref, weight_ref, cot_ref, *refs, n_row, n_chunk, scale):
    sums, (out_ref, keep_ref, send_ref, agg, grad) = refs[:3 * n_chunk], refs[3 * n_chunk:]
    me_row = me_ref[0]
    at = 0
    for j in range(n_chunk):
        a, b, c = sums[3 * j:3 * j + 3]
        wide = a.shape[1]
        agg[:, at:at + wide] = (a[...].astype(F32) + b[...].astype(F32) + c[...].astype(F32)).astype(BF16)
        at += wide
    aggregated = agg[...]
    preact = jnp.dot(aggregated, weight_ref[...], preferred_element_type=F32)
    power = jnp.exp(jnp.minimum(preact, 0.0))
    positive = preact > 0
    out_ref[...] = jnp.where(positive, preact, power - 1.0).astype(BF16)
    grad_pre = (cot_ref[...].astype(F32) * jnp.where(positive, 1.0, power)).astype(BF16)
    grad[...] = lax.dot_general(aggregated, grad_pre, (((0,), (0,)), ((), ())), preferred_element_type=F32) * scale
    part = grad.shape[0] // n_row
    for k in range(n_row):
        rows = grad[pl.ds(pl.multiple_of((me_row ^ k) * part, part), part), :].astype(BF16)
        target = send_ref if k % 2 else keep_ref
        target[(k // 2) * part:(k // 2 + 1) * part, :] = rows


def vertex_step(me, weight, cotangent, sums, scale):
    n_row = lax.axis_size("row")
    n, f = cotangent.shape
    half = jax.ShapeDtypeStruct((f // 2, f), BF16)
    smem, vmem = pl.BlockSpec(memory_space=pltpu.SMEM), pl.BlockSpec(memory_space=pltpu.VMEM)
    return pl.pallas_call(
        functools.partial(vertex_kernel, n_row=n_row, n_chunk=len(sums) // 3, scale=scale),
        out_shape=(jax.ShapeDtypeStruct((n, f), BF16), half, half),
        in_specs=[smem] + [vmem] * (2 + len(sums)),
        out_specs=(vmem,) * 3,
        scratch_shapes=[pltpu.VMEM((n, f), BF16), pltpu.VMEM((f, f), F32)],
        compiler_params=pltpu.CompilerParams(vmem_limit_bytes=VMEM_LIMIT),
        cost_estimate=pl.CostEstimate(
            flops=4 * n * f * f, bytes_accessed=4 * 1024 * 1024, transcendentals=n * f),
    )(me, weight, cotangent, *sums)


def join(me, pieces):
    n = len(pieces)
    part, f = pieces[0].shape

    def kernel(me_ref, *refs):
        out_ref = refs[-1]
        for k in range(n):
            at = pl.multiple_of((me_ref[0] ^ k) * part, part)
            out_ref[pl.ds(at, part), :] = refs[k][...].astype(F32)

    smem, vmem = pl.BlockSpec(memory_space=pltpu.SMEM), pl.BlockSpec(memory_space=pltpu.VMEM)
    return pl.pallas_call(
        kernel,
        out_shape=jax.ShapeDtypeStruct((n * part, f), F32),
        in_specs=[smem] + [vmem] * n,
        out_specs=vmem,
        compiler_params=pltpu.CompilerParams(vmem_limit_bytes=VMEM_LIMIT),
    )(me, *pieces)


def reduce_gradient(me, keep, send):
    n_row, n_col = lax.axis_size("row"), lax.axis_size("col")
    part = keep.shape[0] // (n_row // 2)
    chip = keep.astype(F32) + swap(send, "row", 1).astype(F32)
    mine = chip[:part]
    for k in range(1, n_row // 2):
        mine = mine + swap(chip[k * part:(k + 1) * part].astype(BF16), "row", 2 * k).astype(F32)
    bit = 1
    while bit < n_col:
        rounded = mine.astype(BF16)
        if 2 * bit < n_col:
            others = [swap(rounded, "col", m * bit).astype(F32) for m in (1, 2, 3)]
            mine = (rounded.astype(F32) + others[0]) + (others[1] + others[2])
            bit *= 4
        else:
            mine = rounded.astype(F32) + swap(rounded, "col", bit).astype(F32)
            bit *= 2
    rounded = mine.astype(BF16)
    even = [rounded] + [swap(rounded, "row", 2 * k) for k in range(1, n_row // 2)]
    pieces = []
    for p in even:
        pieces += [p, swap(p, "row", 1)]
    return join(me, pieces)


def local(features, tile_values, tile_index, tile_count, weight, cotangent):
    n_row, n_col = lax.axis_size("row"), lax.axis_size("col")
    me = jnp.stack([lax.axis_index("row"), lax.axis_index("col")]).astype(jnp.int32)
    tiles, index, count = tile_values[0, 0], tile_index[0, 0], tile_count[0]
    sums, at = [], 0
    for wide in CHUNKS:
        pieces = gather_row(features[:, at:at + wide])
        at += wide
        keep, send = tile_products(me, index, count, tiles, pieces)
        terms, bit = [], 1
        while bit < n_col:
            got = swap(send, "col", bit)
            bit *= 2
            if bit < n_col:
                half = keep.shape[0] // 2
                send = (keep[half:].astype(F32) + got[half:].astype(F32)).astype(BF16)
                if 2 * bit < n_col:
                    keep = (keep[:half].astype(F32) + got[:half].astype(F32)).astype(BF16)
                else:
                    keep, terms = keep[:half], terms + [got[:half]]
            else:
                terms += [got]
        sums += [keep] + terms
    scale = 1.0 / math.sqrt(cotangent.shape[0] * n_row * n_col)
    output, grad_keep, grad_send = vertex_step(me, weight, cotangent, sums, scale)
    return output, reduce_gradient(me, grad_keep, grad_send)


def solution(mesh):
    placed = (
        P(("col", "row"), None),
        P("row", "col", None, None, None),
        P("row", "col", None),
        P("row", "col"),
        P(),
        P(("row", "col"), None),
    )
    return jax.shard_map(
        local, mesh=mesh, in_specs=placed, out_specs=(P(("row", "col"), None), P()), check_vma=False
    )
```

time: 249 us -> 103 us (0.41)
  waiting for transfers between devices: 216 us -> 61.7 us
  starting transfers between devices: 0.12 us -> 32 us
  between operations: 14.4 us -> 1.5 us
  local copies, waits for them, and re-layouts: 10.4 us -> 1.89 us
  matrix products: 6.67 us -> 0 us
  Pallas kernels: 0 us -> 5.78 us
    psum x1 -> x0, waiting for transfers between devices: 132 us -> none  [local(): weight_grad = lax.psum(local_grad, ('row', 'col'))]
    ppermute x0 -> x34, waiting for transfers between devices: none -> 61.7 us  [swap(): lax.ppermute(x, axis, [(i, i ^ mask) for i in range(lax.axis_size(axis))])]
    reduce_scatter x1 -> x0, waiting for transfers between devices: 44 us -> none  [local(): lax.psum_scatter(rounded, 'col', scatter_dimension=0, tiled=True)]
    all_gather x1 -> x0, waiting for transfers between devices: 39.4 us -> none  [local(): gathered = lax.all_gather(features, 'row', axis=0, tiled=True)]
    ppermute x0 -> x34, starting transfers between devices: none -> 32 us  [swap(): lax.ppermute(x, axis, [(i, i ^ mask) for i in range(lax.axis_size(axis))])]
    dot_general x4 -> x0, matrix products: 6.67 us -> none  [the longest x1 2.6 us: local(): preact = jnp.dot(aggregated, weight, preferred_element_type=jnp.float32)]
    pallas_call x0 -> x4, Pallas kernels: none -> 5.78 us  [the longest x2 2.16 us: tile_products(): pl.pallas_call(functools.partial(tiles_kernel, n_row=n_row, n_col=n_col),...]
    dot_general x1 -> x0, local copies, waits for them, and re-layouts: 3.25 us -> none  [local(): jnp.einsum('kab,kbf->kaf', tile_vals, picked, preferred_element_type=jnp....]
  transfers between devices with their start and end apart: 3 -> 34, of which waited for: 3 -> 19; matrix products, arithmetic and copies ran while one was open for 1% -> 0% of each run, Pallas kernels for 0% -> 2%
where the time goes in v1:
time: 103 us
  waiting for transfers between devices  61.7 us (60%)
  starting transfers between devices  32 us (31%)
  Pallas kernels  5.78 us (6%)
  local copies, waits for them, and re-layouts  1.89 us (2%)
  between operations  1.5 us (1%)
    ppermute x34, waiting for transfers between devices, swap(): lax.ppermute(x, axis, [(i, i ^ mask) for i in range(lax.axis_size(axis))])  61.7 us
    ppermute x34, starting transfers between devices, swap(): lax.ppermute(x, axis, [(i, i ^ mask) for i in range(lax.axis_size(axis))])  32 us
    pallas_call x2, Pallas kernels, tile_products(): pl.pallas_call(functools.partial(tiles_kernel, n_row=n_row, n_col=n_col),...  2.16 us
  transfers between devices with their start and end apart: 34, of which 19 were waited for; matrix products, arithmetic and copies ran while one was open for 0% of the time, Pallas kernels for 2%

profile of v1, /device:TPU:0, one launch (start us, length us, event | category | flops | bytes accessed | tf_op | source)
XLA Modules:
  0.0 103.2 jit_solution(377424973724103581)
XLA Ops:
  1.7 3.0 %collective-permute-start.1 = (bf16[512,256]{1,0:T(8,128)(2,1)S(1)}, bf16[512,256]{1,0:T(8,128)(2,1)S(1)}, u32[]{:S(2)}, u32[]{:S(2)}) collective-permute-start(bf16[512,256]{1,0:T(8,128)(2,1)S(1)} %get-tuple-element.19.refs_0_), channel_id=1, source_target_pairs={{0,8},{4,12},{8,0},{12,4},{16,24},{20,28},{24,16},{28,20},{1,9},{5... | collective-permute-start | bytes 786440 | tf_op jit(solution)/shard_map/ppermute | solution.py:19
  4.7 1.5 %collective-permute-start.3 = (bf16[512,256]{1,0:T(8,128)(2,1)S(1)}, bf16[512,256]{1,0:T(8,128)(2,1)S(1)}, u32[]{:S(2)}, u32[]{:S(2)}) collective-permute-start(bf16[512,256]{1,0:T(8,128)(2,1)S(1)} %get-tuple-element.19.refs_0_), channel_id=1, source_target_pairs={{0,16},{4,20},{8,24},{12,28},{16,0},{20,4},{24,8},{28,12},{1,17},{... | collective-permute-start | bytes 786440 | tf_op jit(solution)/shard_map/ppermute | solution.py:19
  6.8 5.0 %collective-permute-done.1.refs_2_ = bf16[512,256]{1,0:T(8,128)(2,1)S(1)} collective-permute-done((bf16[512,256]{1,0:T(8,128)(2,1)S(1)}, bf16[512,256]{1,0:T(8,128)(2,1)S(1)}, u32[]{:S(2)}, u32[]{:S(2)}) %collective-permute-start.1) | collective-permute-done | bytes 262176 | tf_op jit(solution)/shard_map/ppermute | solution.py:19
  11.8 2.2 %collective-permute-start.5 = (bf16[256,256]{1,0:T(8,128)(2,1)S(1)}, bf16[256,256]{1,0:T(8,128)(2,1)S(1)}, u32[]{:S(2)}, u32[]{:S(2)}) collective-permute-start(bf16[256,256]{1,0:T(8,128)(2,1)S(1)} %slice.75), channel_id=1, source_target_pairs={{0,16},{4,20},{8,24},{12,28},{16,0},{20,4},{24,8},{28,12},{1,17},{... | collective-permute-start | bytes 393224 | tf_op jit(solution)/shard_map/ppermute | solution.py:19
  14.0 1.6 %collective-permute-start.6 = (bf16[256,256]{1,0:T(8,128)(2,1)S(1)}, bf16[256,256]{1,0:T(8,128)(2,1)S(1)}, u32[]{:S(2)}, u32[]{:S(2)}) collective-permute-start(bf16[256,256]{1,0:T(8,128)(2,1)S(1)} %slice.76), channel_id=1, source_target_pairs={{0,8},{4,12},{8,0},{12,4},{16,24},{20,28},{24,16},{28,20},{1,9},{5... | collective-permute-start | bytes 393224 | tf_op jit(solution)/shard_map/ppermute | solution.py:19
  15.6 1.9 %collective-permute-done.11.refs_2_ = bf16[512,256]{1,0:T(8,128)(2,1)S(1)} collective-permute-done((bf16[512,256]{1,0:T(8,128)(2,1)S(1)}, bf16[512,256]{1,0:T(8,128)(2,1)S(1)}, u32[]{:S(2)}, u32[]{:S(2)}) %collective-permute-start.11) | collective-permute-done | bytes 262176 | tf_op jit(solution)/shard_map/ppermute | solution.py:19
  17.5 2.2 %collective-permute-start.15 = (bf16[256,256]{1,0:T(8,128)(2,1)S(1)}, bf16[256,256]{1,0:T(8,128)(2,1)S(1)}, u32[]{:S(2)}, u32[]{:S(2)}) collective-permute-start(bf16[256,256]{1,0:T(8,128)(2,1)S(1)} %slice.79), channel_id=1, source_target_pairs={{0,16},{4,20},{8,24},{12,28},{16,0},{20,4},{24,8},{28,12},{1,17},{... | collective-permute-start | bytes 393224 | tf_op jit(solution)/shard_map/ppermute | solution.py:19
  19.6 1.6 %collective-permute-start.16 = (bf16[256,256]{1,0:T(8,128)(2,1)S(1)}, bf16[256,256]{1,0:T(8,128)(2,1)S(1)}, u32[]{:S(2)}, u32[]{:S(2)}) collective-permute-start(bf16[256,256]{1,0:T(8,128)(2,1)S(1)} %slice.80), channel_id=1, source_target_pairs={{0,8},{4,12},{8,0},{12,4},{16,24},{20,28},{24,16},{28,20},{1,9},{5... | collective-permute-start | bytes 393224 | tf_op jit(solution)/shard_map/ppermute | solution.py:19
  28.3 1.9 %collective-permute-start.8 = (bf16[1024,256]{1,0:T(8,128)(2,1)S(1)}, bf16[1024,256]{1,0:T(8,128)(2,1)S(1)}, u32[]{:S(2)}, u32[]{:S(2)}) collective-permute-start(bf16[1024,256]{1,0:T(8,128)(2,1)S(1)} %get-tuple-element.10), channel_id=1, source_target_pairs={{0,1},{1,0},{2,3},{3,2},{4,5},{5,4},{6,7},{7,6},{8,9},{9,8},{10,11... | collective-permute-start | bytes 1572872 | tf_op jit(solution)/shard_map/ppermute | solution.py:19
  31.8 11.4 %collective-permute-done.8 = bf16[1024,256]{1,0:T(8,128)(2,1)S(1)} collective-permute-done((bf16[1024,256]{1,0:T(8,128)(2,1)S(1)}, bf16[1024,256]{1,0:T(8,128)(2,1)S(1)}, u32[]{:S(2)}, u32[]{:S(2)}) %collective-permute-start.8) | collective-permute-done | bytes 524320 | tf_op jit(solution)/shard_map/ppermute | solution.py:19
  43.2 2.3 %collective-permute-start.9 = (bf16[512,256]{1,0:T(8,128)(2,1)S(1)}, bf16[512,256]{1,0:T(8,128)(2,1)S(1)}, u32[]{:S(2)}, u32[]{:S(2)}) collective-permute-start(bf16[512,256]{1,0:T(8,128)(2,1)S(1)} %add_convert_fusion.1), channel_id=1, source_target_pairs={{0,2},{1,3},{2,0},{3,1},{4,6},{5,7},{6,4},{7,5},{8,10},{9,11},{10,... | collective-permute-start | bytes 786440 | tf_op jit(solution)/shard_map/ppermute | solution.py:19
  45.5 14.3 %collective-permute-done.18 = bf16[1024,256]{1,0:T(8,128)(2,1)S(1)} collective-permute-done((bf16[1024,256]{1,0:T(8,128)(2,1)S(1)}, bf16[1024,256]{1,0:T(8,128)(2,1)S(1)}, u32[]{:S(2)}, u32[]{:S(2)}) %collective-permute-start.18) | collective-permute-done | bytes 524320 | tf_op jit(solution)/shard_map/ppermute | solution.py:19
  59.9 1.5 %collective-permute-start.19 = (bf16[512,256]{1,0:T(8,128)(2,1)S(1)}, bf16[512,256]{1,0:T(8,128)(2,1)S(1)}, u32[]{:S(2)}, u32[]{:S(2)}) collective-permute-start(bf16[512,256]{1,0:T(8,128)(2,1)S(1)} %add_convert_fusion), channel_id=1, source_target_pairs={{0,2},{1,3},{2,0},{3,1},{4,6},{5,7},{6,4},{7,5},{8,10},{9,11},{10,... | collective-permute-start | bytes 786440 | tf_op jit(solution)/shard_map/ppermute | solution.py:19
  61.5 13.1 %collective-permute-done.19.refs_5_ = bf16[512,256]{1,0:T(8,128)(2,1)S(1)} collective-permute-done((bf16[512,256]{1,0:T(8,128)(2,1)S(1)}, bf16[512,256]{1,0:T(8,128)(2,1)S(1)}, u32[]{:S(2)}, u32[]{:S(2)}) %collective-permute-start.19) | collective-permute-done | bytes 262176 | tf_op jit(solution)/shard_map/ppermute | solution.py:19
  74.6 2.0 %shard_map.79 = (bf16[512,512]{1,0:T(8,128)(2,1)}, bf16[256,512]{1,0:T(8,128)(2,1)S(1)}, bf16[256,512]{1,0:T(8,128)(2,1)S(1)}) custom-call(s32[2]{0:T(128)S(1)} %pad_add_fusion.me_ref, bf16[512,512]{1,0:T(8,128)(2,1)S(1)} %copy-done.1, bf16[512,512]{1,0:T(8,128)(2,1)S(1)} %copy-done.2, bf16[512,256]{1,0:T(8,128)(2,1)S(1)} %slice.60.refs_0_, ...), custom_call_target="tpu_custom_call" | custom-call | flops 536870912 | bytes 4194304 | tf_op jit(solution)/shard_map/pallas_call | solution.py:128
  76.7 1.5 %collective-permute-done.20 = bf16[256,512]{1,0:T(8,128)(2,1)S(1)} collective-permute-done((bf16[256,512]{1,0:T(8,128)(2,1)S(1)}, bf16[256,512]{1,0:T(8,128)(2,1)S(1)}, u32[]{:S(2)}, u32[]{:S(2)}) %collective-permute-start.20) | collective-permute-done | bytes 262176 | tf_op jit(solution)/shard_map/ppermute | solution.py:19
  81.9 2.3 %collective-permute-done.23 = bf16[64,512]{1,0:T(8,128)(2,1)S(1)} collective-permute-done((bf16[64,512]{1,0:T(8,128)(2,1)S(1)}, bf16[64,512]{1,0:T(8,128)(2,1)S(1)}, u32[]{:S(2)}, u32[]{:S(2)}) %collective-permute-start.23) | collective-permute-done | bytes 65568 | tf_op jit(solution)/shard_map/ppermute | solution.py:19
  84.9 2.2 %collective-permute-start.26 = (bf16[64,512]{1,0:T(8,128)(2,1)S(1)}, bf16[64,512]{1,0:T(8,128)(2,1)S(1)}, u32[]{:S(2)}, u32[]{:S(2)}) collective-permute-start(bf16[64,512]{1,0:T(8,128)(2,1)S(1)} %fusion.2), channel_id=1, source_target_pairs={{0,3},{1,2},{2,1},{3,0},{4,7},{5,6},{6,5},{7,4},{8,11},{9,10},{10,... | collective-permute-start | bytes 196616 | tf_op jit(solution)/shard_map/ppermute | solution.py:19
  87.2 2.2 %collective-permute-start.24 = (bf16[64,512]{1,0:T(8,128)(2,1)S(1)}, bf16[64,512]{1,0:T(8,128)(2,1)S(1)}, u32[]{:S(2)}, u32[]{:S(2)}) collective-permute-start(bf16[64,512]{1,0:T(8,128)(2,1)S(1)} %fusion.2), channel_id=1, source_target_pairs={{0,1},{1,0},{2,3},{3,2},{4,5},{5,4},{6,7},{7,6},{8,9},{9,8},{10,11... | collective-permute-start | bytes 196616 | tf_op jit(solution)/shard_map/ppermute | solution.py:19
  89.4 1.8 %collective-permute-done.26 = bf16[64,512]{1,0:T(8,128)(2,1)S(1)} collective-permute-done((bf16[64,512]{1,0:T(8,128)(2,1)S(1)}, bf16[64,512]{1,0:T(8,128)(2,1)S(1)}, u32[]{:S(2)}, u32[]{:S(2)}) %collective-permute-start.26) | collective-permute-done | bytes 65568 | tf_op jit(solution)/shard_map/ppermute | solution.py:19
  91.2 1.9 %collective-permute-done.25 = bf16[64,512]{1,0:T(8,128)(2,1)S(1)} collective-permute-done((bf16[64,512]{1,0:T(8,128)(2,1)S(1)}, bf16[64,512]{1,0:T(8,128)(2,1)S(1)}, u32[]{:S(2)}, u32[]{:S(2)}) %collective-permute-start.25) | collective-permute-done | bytes 65568 | tf_op jit(solution)/shard_map/ppermute | solution.py:19
  95.2 1.5 %collective-permute-start.32 = (bf16[64,512]{1,0:T(8,128)(2,1)S(1)}, bf16[64,512]{1,0:T(8,128)(2,1)S(1)}, u32[]{:S(2)}, u32[]{:S(2)}) collective-permute-start(bf16[64,512]{1,0:T(8,128)(2,1)S(1)} %add_convert_fusion.2.refs_0_), channel_id=1, source_target_pairs={{0,24},{4,28},{8,16},{12,20},{16,8},{20,12},{24,0},{28,4},{1,25},{... | collective-permute-start | bytes 196616 | tf_op jit(solution)/shard_map/ppermute | solution.py:19
  97.9 1.4 %collective-permute-done.30.refs_4_ = bf16[64,512]{1,0:T(8,128)(2,1)S(1)} collective-permute-done((bf16[64,512]{1,0:T(8,128)(2,1)S(1)}, bf16[64,512]{1,0:T(8,128)(2,1)S(1)}, u32[]{:S(2)}, u32[]{:S(2)}) %collective-permute-start.30) | collective-permute-done | bytes 65568 | tf_op jit(solution)/shard_map/ppermute | solution.py:19
  101.6 1.6 %shard_map.80 = f32[512,512]{1,0:T(8,128)} custom-call(s32[2]{0:T(128)S(1)} %pad_add_fusion.me_ref, bf16[64,512]{1,0:T(8,128)(2,1)S(1)} %add_convert_fusion.2.refs_0_, bf16[64,512]{1,0:T(8,128)(2,1)S(1)} %collective-permute-done.27.refs_1_, bf16[64,512]{1,0:T(8,128)(2,1)S(1)} %collective-permute-done.28.refs_2_, ...), custom_call_target="tpu_custom_call" | custom-call | tf_op jit(solution)/shard_map/pallas_call | solution.py:151
  (76 shorter events, 19.9 us)
Async XLA Ops:
  1.7 10.1 %collective-permute-start.1 = (bf16[512,256]{1,0:T(8,128)(2,1)S(1)}, bf16[512,256]{1,0:T(8,128)(2,1)S(1)}, u32[]{:S(2)}, u32[]{:S(2)}) collective-permute-start(bf16[512,256]{1,0:T(8,128)(2,1)S(1)} %get-tuple-element.19.refs_0_), channel_id=1, source_target_pairs={{0,8},{4,12},{8,0},{12,4},{16,24},{20,28},{24,16},{28,20},{1,9},{5... | collective-permute-start | bytes 786440 | tf_op jit(solution)/shard_map/ppermute | solution.py:19
  4.7 9.3 %collective-permute-start.3 = (bf16[512,256]{1,0:T(8,128)(2,1)S(1)}, bf16[512,256]{1,0:T(8,128)(2,1)S(1)}, u32[]{:S(2)}, u32[]{:S(2)}) collective-permute-start(bf16[512,256]{1,0:T(8,128)(2,1)S(1)} %get-tuple-element.19.refs_0_), channel_id=1, source_target_pairs={{0,16},{4,20},{8,24},{12,28},{16,0},{20,4},{24,8},{28,12},{1,17},{... | collective-permute-start | bytes 786440 | tf_op jit(solution)/shard_map/ppermute | solution.py:19
  6.2 11.2 %collective-permute-start.11 = (bf16[512,256]{1,0:T(8,128)(2,1)S(1)}, bf16[512,256]{1,0:T(8,128)(2,1)S(1)}, u32[]{:S(2)}, u32[]{:S(2)}) collective-permute-start(bf16[512,256]{1,0:T(8,128)(2,1)S(1)} %get-tuple-element.18.refs_0_), channel_id=1, source_target_pairs={{0,8},{4,12},{8,0},{12,4},{16,24},{20,28},{24,16},{28,20},{1,9},{5... | collective-permute-start | bytes 786440 | tf_op jit(solution)/shard_map/ppermute | solution.py:19
  6.8 12.9 %collective-permute-start.13 = (bf16[512,256]{1,0:T(8,128)(2,1)S(1)}, bf16[512,256]{1,0:T(8,128)(2,1)S(1)}, u32[]{:S(2)}, u32[]{:S(2)}) collective-permute-start(bf16[512,256]{1,0:T(8,128)(2,1)S(1)} %get-tuple-element.18.refs_0_), channel_id=1, source_target_pairs={{0,16},{4,20},{8,24},{12,28},{16,0},{20,4},{24,8},{28,12},{1,17},{... | collective-permute-start | bytes 786440 | tf_op jit(solution)/shard_map/ppermute | solution.py:19
  11.8 10.4 %collective-permute-start.5 = (bf16[256,256]{1,0:T(8,128)(2,1)S(1)}, bf16[256,256]{1,0:T(8,128)(2,1)S(1)}, u32[]{:S(2)}, u32[]{:S(2)}) collective-permute-start(bf16[256,256]{1,0:T(8,128)(2,1)S(1)} %slice.75), channel_id=1, source_target_pairs={{0,16},{4,20},{8,24},{12,28},{16,0},{20,4},{24,8},{28,12},{1,17},{... | collective-permute-start | bytes 393224 | tf_op jit(solution)/shard_map/ppermute | solution.py:19
  14.0 8.3 %collective-permute-start.6 = (bf16[256,256]{1,0:T(8,128)(2,1)S(1)}, bf16[256,256]{1,0:T(8,128)(2,1)S(1)}, u32[]{:S(2)}, u32[]{:S(2)}) collective-permute-start(bf16[256,256]{1,0:T(8,128)(2,1)S(1)} %slice.76), channel_id=1, source_target_pairs={{0,8},{4,12},{8,0},{12,4},{16,24},{20,28},{24,16},{28,20},{1,9},{5... | collective-permute-start | bytes 393224 | tf_op jit(solution)/shard_map/ppermute | solution.py:19
  15.6 9.1 %collective-permute-start = (bf16[512,256]{1,0:T(8,128)(2,1)S(1)}, bf16[512,256]{1,0:T(8,128)(2,1)S(1)}, u32[]{:S(2)}, u32[]{:S(2)}) collective-permute-start(bf16[512,256]{1,0:T(8,128)(2,1)S(1)} %get-tuple-element.19.refs_0_), channel_id=1, source_target_pairs={{0,4},{4,0},{8,12},{12,8},{16,20},{20,16},{24,28},{28,24},{1,5},{5... | collective-permute-start | bytes 786440 | tf_op jit(solution)/shard_map/ppermute | solution.py:19
  17.5 6.2 %collective-permute-start.15 = (bf16[256,256]{1,0:T(8,128)(2,1)S(1)}, bf16[256,256]{1,0:T(8,128)(2,1)S(1)}, u32[]{:S(2)}, u32[]{:S(2)}) collective-permute-start(bf16[256,256]{1,0:T(8,128)(2,1)S(1)} %slice.79), channel_id=1, source_target_pairs={{0,16},{4,20},{8,24},{12,28},{16,0},{20,4},{24,8},{28,12},{1,17},{... | collective-permute-start | bytes 393224 | tf_op jit(solution)/shard_map/ppermute | solution.py:19
  19.6 5.0 %collective-permute-start.16 = (bf16[256,256]{1,0:T(8,128)(2,1)S(1)}, bf16[256,256]{1,0:T(8,128)(2,1)S(1)}, u32[]{:S(2)}, u32[]{:S(2)}) collective-permute-start(bf16[256,256]{1,0:T(8,128)(2,1)S(1)} %slice.80), channel_id=1, source_target_pairs={{0,8},{4,12},{8,0},{12,4},{16,24},{20,28},{24,16},{28,20},{1,9},{5... | collective-permute-start | bytes 393224 | tf_op jit(solution)/shard_map/ppermute | solution.py:19
  24.7 5.5 %collective-permute-start.10 = (bf16[512,256]{1,0:T(8,128)(2,1)S(1)}, bf16[512,256]{1,0:T(8,128)(2,1)S(1)}, u32[]{:S(2)}, u32[]{:S(2)}) collective-permute-start(bf16[512,256]{1,0:T(8,128)(2,1)S(1)} %get-tuple-element.18.refs_0_), channel_id=1, source_target_pairs={{0,4},{4,0},{8,12},{12,8},{16,20},{20,16},{24,28},{28,24},{1,5},{5... | collective-permute-start | bytes 786440 | tf_op jit(solution)/shard_map/ppermute | solution.py:19
  24.7 5.5 %collective-permute-start.12 = (bf16[512,256]{1,0:T(8,128)(2,1)S(1)}, bf16[512,256]{1,0:T(8,128)(2,1)S(1)}, u32[]{:S(2)}, u32[]{:S(2)}) collective-permute-start(bf16[512,256]{1,0:T(8,128)(2,1)S(1)} %collective-permute-done.11.refs_2_), channel_id=1, source_target_pairs={{0,4},{4,0},{8,12},{12,8},{16,20},{20,16},{24,28},{28,24},{1,5},{5... | collective-permute-start | bytes 786440 | tf_op jit(solution)/shard_map/ppermute | solution.py:19
  25.3 4.9 %collective-permute-start.14 = (bf16[512,256]{1,0:T(8,128)(2,1)S(1)}, bf16[512,256]{1,0:T(8,128)(2,1)S(1)}, u32[]{:S(2)}, u32[]{:S(2)}) collective-permute-start(bf16[512,256]{1,0:T(8,128)(2,1)S(1)} %collective-permute-done.13.refs_4_), channel_id=1, source_target_pairs={{0,4},{4,0},{8,12},{12,8},{16,20},{20,16},{24,28},{28,24},{1,5},{5... | collective-permute-start | bytes 786440 | tf_op jit(solution)/shard_map/ppermute | solution.py:19
  25.4 4.8 %collective-permute-start.17 = (bf16[512,256]{1,0:T(8,128)(2,1)S(1)}, bf16[512,256]{1,0:T(8,128)(2,1)S(1)}, u32[]{:S(2)}, u32[]{:S(2)}) collective-permute-start(bf16[512,256]{1,0:T(8,128)(2,1)S(1)} %constant_dynamic-update-slice_fusion.2.refs_6_), channel_id=1, source_target_pairs={{0,4},{4,0},{8,12},{12,8},{16,20},{20,16},{24,28},{28,24},{1,5},{5... | collective-permute-start | bytes 786440 | tf_op jit(solution)/shard_map/ppermute | solution.py:19
  28.3 14.9 %collective-permute-start.8 = (bf16[1024,256]{1,0:T(8,128)(2,1)S(1)}, bf16[1024,256]{1,0:T(8,128)(2,1)S(1)}, u32[]{:S(2)}, u32[]{:S(2)}) collective-permute-start(bf16[1024,256]{1,0:T(8,128)(2,1)S(1)} %get-tuple-element.10), channel_id=1, source_target_pairs={{0,1},{1,0},{2,3},{3,2},{4,5},{5,4},{6,7},{7,6},{8,9},{9,8},{10,11... | collective-permute-start | bytes 1572872 | tf_op jit(solution)/shard_map/ppermute | solution.py:19
  31.3 28.6 %collective-permute-start.18 = (bf16[1024,256]{1,0:T(8,128)(2,1)S(1)}, bf16[1024,256]{1,0:T(8,128)(2,1)S(1)}, u32[]{:S(2)}, u32[]{:S(2)}) collective-permute-start(bf16[1024,256]{1,0:T(8,128)(2,1)S(1)} %get-tuple-element.12), channel_id=1, source_target_pairs={{0,1},{1,0},{2,3},{3,2},{4,5},{5,4},{6,7},{7,6},{8,9},{9,8},{10,11... | collective-permute-start | bytes 1572872 | tf_op jit(solution)/shard_map/ppermute | solution.py:19
  43.2 18.3 %collective-permute-start.9 = (bf16[512,256]{1,0:T(8,128)(2,1)S(1)}, bf16[512,256]{1,0:T(8,128)(2,1)S(1)}, u32[]{:S(2)}, u32[]{:S(2)}) collective-permute-start(bf16[512,256]{1,0:T(8,128)(2,1)S(1)} %add_convert_fusion.1), channel_id=1, source_target_pairs={{0,2},{1,3},{2,0},{3,1},{4,6},{5,7},{6,4},{7,5},{8,10},{9,11},{10,... | collective-permute-start | bytes 786440 | tf_op jit(solution)/shard_map/ppermute | solution.py:19
  59.9 14.7 %collective-permute-start.19 = (bf16[512,256]{1,0:T(8,128)(2,1)S(1)}, bf16[512,256]{1,0:T(8,128)(2,1)S(1)}, u32[]{:S(2)}, u32[]{:S(2)}) collective-permute-start(bf16[512,256]{1,0:T(8,128)(2,1)S(1)} %add_convert_fusion), channel_id=1, source_target_pairs={{0,2},{1,3},{2,0},{3,1},{4,6},{5,7},{6,4},{7,5},{8,10},{9,11},{10,... | collective-permute-start | bytes 786440 | tf_op jit(solution)/shard_map/ppermute | solution.py:19
  78.4 5.9 %collective-permute-start.23 = (bf16[64,512]{1,0:T(8,128)(2,1)S(1)}, bf16[64,512]{1,0:T(8,128)(2,1)S(1)}, u32[]{:S(2)}, u32[]{:S(2)}) collective-permute-start(bf16[64,512]{1,0:T(8,128)(2,1)S(1)} %get-tuple-element.21), channel_id=1, source_target_pairs={{0,24},{4,28},{8,16},{12,20},{16,8},{20,12},{24,0},{28,4},{1,25},{... | collective-permute-start | bytes 196616 | tf_op jit(solution)/shard_map/ppermute | solution.py:19
  79.3 5.3 %collective-permute-start.22 = (bf16[64,512]{1,0:T(8,128)(2,1)S(1)}, bf16[64,512]{1,0:T(8,128)(2,1)S(1)}, u32[]{:S(2)}, u32[]{:S(2)}) collective-permute-start(bf16[64,512]{1,0:T(8,128)(2,1)S(1)} %get-tuple-element.22), channel_id=1, source_target_pairs={{0,16},{4,20},{8,24},{12,28},{16,0},{20,4},{24,8},{28,12},{1,17},{... | collective-permute-start | bytes 196616 | tf_op jit(solution)/shard_map/ppermute | solution.py:19
  84.9 6.3 %collective-permute-start.26 = (bf16[64,512]{1,0:T(8,128)(2,1)S(1)}, bf16[64,512]{1,0:T(8,128)(2,1)S(1)}, u32[]{:S(2)}, u32[]{:S(2)}) collective-permute-start(bf16[64,512]{1,0:T(8,128)(2,1)S(1)} %fusion.2), channel_id=1, source_target_pairs={{0,3},{1,2},{2,1},{3,0},{4,7},{5,6},{6,5},{7,4},{8,11},{9,10},{10,... | collective-permute-start | bytes 196616 | tf_op jit(solution)/shard_map/ppermute | solution.py:19
  87.2 6.0 %collective-permute-start.25 = (bf16[64,512]{1,0:T(8,128)(2,1)S(1)}, bf16[64,512]{1,0:T(8,128)(2,1)S(1)}, u32[]{:S(2)}, u32[]{:S(2)}) collective-permute-start(bf16[64,512]{1,0:T(8,128)(2,1)S(1)} %fusion.2), channel_id=1, source_target_pairs={{0,2},{1,3},{2,0},{3,1},{4,6},{5,7},{6,4},{7,5},{8,10},{9,11},{10,... | collective-permute-start | bytes 196616 | tf_op jit(solution)/shard_map/ppermute | solution.py:19
  87.2 6.0 %collective-permute-start.24 = (bf16[64,512]{1,0:T(8,128)(2,1)S(1)}, bf16[64,512]{1,0:T(8,128)(2,1)S(1)}, u32[]{:S(2)}, u32[]{:S(2)}) collective-permute-start(bf16[64,512]{1,0:T(8,128)(2,1)S(1)} %fusion.2), channel_id=1, source_target_pairs={{0,1},{1,0},{2,3},{3,2},{4,5},{5,4},{6,7},{7,6},{8,9},{9,8},{10,11... | collective-permute-start | bytes 196616 | tf_op jit(solution)/shard_map/ppermute | solution.py:19
  94.3 5.0 %collective-permute-start.30 = (bf16[64,512]{1,0:T(8,128)(2,1)S(1)}, bf16[64,512]{1,0:T(8,128)(2,1)S(1)}, u32[]{:S(2)}, u32[]{:S(2)}) collective-permute-start(bf16[64,512]{1,0:T(8,128)(2,1)S(1)} %add_convert_fusion.2.refs_0_), channel_id=1, source_target_pairs={{0,16},{4,20},{8,24},{12,28},{16,0},{20,4},{24,8},{28,12},{1,17},{... | collective-permute-start | bytes 196616 | tf_op jit(solution)/shard_map/ppermute | solution.py:19
  95.2 5.2 %collective-permute-start.32 = (bf16[64,512]{1,0:T(8,128)(2,1)S(1)}, bf16[64,512]{1,0:T(8,128)(2,1)S(1)}, u32[]{:S(2)}, u32[]{:S(2)}) collective-permute-start(bf16[64,512]{1,0:T(8,128)(2,1)S(1)} %add_convert_fusion.2.refs_0_), channel_id=1, source_target_pairs={{0,24},{4,28},{8,16},{12,20},{16,8},{20,12},{24,0},{28,4},{1,25},{... | collective-permute-start | bytes 196616 | tf_op jit(solution)/shard_map/ppermute | solution.py:19
  (14 other events, 66.1 us)

commit v2 on v1

v2 whole, which is shorter than its diff:
```python
import functools
import math

import jax
import jax.numpy as jnp
from jax import lax
from jax.experimental import pallas as pl
from jax.experimental.pallas import tpu as pltpu
from jax.sharding import PartitionSpec as P

BLK = 256
RBG = 8
CHUNKS = (256, 256)
COST = 15 * 10**9
VMEM_LIMIT = 48 * 1024 * 1024
F32, BF16 = jnp.float32, jnp.bfloat16


def swap(x, axis, mask):
    return lax.ppermute(x, axis, [(i, i ^ mask) for i in range(lax.axis_size(axis))])


def bit_reversed(i, bits):
    out = 0 * i
    for b in range(bits):
        out = out + (((i >> b) & 1) << (bits - 1 - b))
    return out


def gather_chips(x):
    return [swap(x, "row", k) for k in range(2, lax.axis_size("row"), 2)]


def stage(x):
    def kernel(x_ref, out_ref, sem):
        copy = pltpu.make_async_copy(x_ref, out_ref, sem)
        copy.start()
        copy.wait()

    return pl.pallas_call(
        kernel,
        out_shape=jax.ShapeDtypeStruct(x.shape, x.dtype),
        in_specs=[pl.BlockSpec(memory_space=pl.ANY)],
        out_specs=pl.BlockSpec(memory_space=pltpu.VMEM),
        scratch_shapes=[pltpu.SemaphoreType.DMA],
        compiler_params=pltpu.CompilerParams(vmem_limit_bytes=VMEM_LIMIT),
    )(x)


def tiles_kernel(scalars_ref, tiles_ref, *refs, at, n_row, n_col):
    pieces, out_refs, (picked, total) = refs[:n_row], refs[n_row:-2], refs[-2:]
    rows, wide = pieces[0].shape[0], total.shape[1]
    part = min(BLK, rows)
    own = RBG * BLK // n_col
    step = min(BLK, own)
    bits = n_col.bit_length() - 1
    col_groups = rows * n_row // BLK
    me_row, me_col, count = scalars_ref[0], scalars_ref[1], scalars_ref[2]
    total[...] = jnp.zeros_like(total)
    for k in range(tiles_ref.shape[0]):
        number = scalars_ref[3 + k]
        row_slot, col_slot = number // col_groups, number % col_groups

        @pl.when(k < count)
        def _(k=k, row_slot=row_slot, col_slot=col_slot):
            for j in range(BLK // part):
                first = col_slot * BLK + j * part
                owner = (first // rows) ^ me_row
                block = pl.ds(pl.multiple_of(first % rows, part), part)
                for p in range(n_row):
                    columns = slice(at, at + wide) if p < 2 else slice(None)

                    @pl.when(owner == p)
                    def _(p=p, j=j, block=block, columns=columns):
                        picked[j * part:(j + 1) * part, :] = pieces[p][block, columns]

            product = jnp.dot(tiles_ref[k], picked[...], preferred_element_type=F32)
            for j in range(BLK // step):
                first = row_slot * BLK + j * step
                place = bit_reversed((first // own) ^ me_col, bits) * own + first % own
                place = pl.ds(pl.multiple_of(place, step), step)
                total[place, :] += product[j * step:(j + 1) * step, :]

    quarter = total.shape[0] // 4
    for q, out_ref in enumerate(out_refs):
        out_ref[...] = total[q * quarter:(q + 1) * quarter, :].astype(BF16)


def tile_products(scalars, tiles, pieces, at):
    n_row, n_col = lax.axis_size("row"), lax.axis_size("col")
    wide = pieces[-1].shape[1]
    quarter = jax.ShapeDtypeStruct((RBG * BLK // 4, wide), BF16)
    smem, vmem = pl.BlockSpec(memory_space=pltpu.SMEM), pl.BlockSpec(memory_space=pltpu.VMEM)
    return pl.pallas_call(
        functools.partial(tiles_kernel, at=at, n_row=n_row, n_col=n_col),
        out_shape=(quarter,) * 4,
        in_specs=[smem] + [vmem] * (1 + n_row),
        out_specs=(vmem,) * 4,
        scratch_shapes=[
            pltpu.VMEM((BLK, wide), BF16),
            pltpu.VMEM((RBG * BLK, wide), F32),
        ],
        compiler_params=pltpu.CompilerParams(vmem_limit_bytes=VMEM_LIMIT),
        cost_estimate=pl.CostEstimate(
            flops=2 * tiles.shape[0] * BLK * BLK * wide, bytes_accessed=6 * 1024 * 1024, transcendentals=0),
    )(scalars, tiles, *pieces)


def vertex_kernel(me_ref, weight_ref, cot_ref, *refs, n_row, places, scale):
    *terms, out_ref, keep_ref, send_ref, total, agg, grad = refs
    me_row = me_ref[0]
    total[...] = jnp.zeros_like(total)
    for term, at in zip(terms, places):
        total[:, at:at + term.shape[1]] += term[...].astype(F32)
    agg[...] = total[...].astype(BF16)
    aggregated = agg[...]
    preact = jnp.dot(aggregated, weight_ref[...], preferred_element_type=F32)
    power = jnp.exp(jnp.minimum(preact, 0.0))
    positive = preact > 0
    out_ref[...] = jnp.where(positive, preact, power - 1.0).astype(BF16)
    grad_pre = (cot_ref[...].astype(F32) * jnp.where(positive, 1.0, power)).astype(BF16)
    grad[...] = lax.dot_general(aggregated, grad_pre, (((0,), (0,)), ((), ())), preferred_element_type=F32) * scale
    part = grad.shape[0] // n_row
    for k in range(n_row):
        rows = grad[pl.ds(pl.multiple_of((me_row ^ k) * part, part), part), :].astype(BF16)
        target = send_ref if k % 2 else keep_ref
        target[(k // 2) * part:(k // 2 + 1) * part, :] = rows


def vertex_step(me, weight, cotangent, terms, places, scale):
    n_row = lax.axis_size("row")
    n, f = cotangent.shape
    half = jax.ShapeDtypeStruct((f // 2, f), BF16)
    smem, vmem = pl.BlockSpec(memory_space=pltpu.SMEM), pl.BlockSpec(memory_space=pltpu.VMEM)
    return pl.pallas_call(
        functools.partial(vertex_kernel, n_row=n_row, places=places, scale=scale),
        out_shape=(jax.ShapeDtypeStruct((n, f), BF16), half, half),
        in_specs=[smem] + [vmem] * (2 + len(terms)),
        out_specs=(vmem,) * 3,
        scratch_shapes=[pltpu.VMEM((n, f), F32), pltpu.VMEM((n, f), BF16), pltpu.VMEM((f, f), F32)],
        compiler_params=pltpu.CompilerParams(vmem_limit_bytes=VMEM_LIMIT),
        cost_estimate=pl.CostEstimate(
            flops=4 * n * f * f, bytes_accessed=4 * 1024 * 1024, transcendentals=n * f),
    )(me, weight, cotangent, *terms)


def join(me, pieces):
    n = len(pieces)
    part, f = pieces[0].shape

    def kernel(me_ref, *refs):
        out_ref = refs[-1]
        for k in range(n):
            at = pl.multiple_of((me_ref[0] ^ k) * part, part)
            out_ref[pl.ds(at, part), :] = refs[k][...].astype(F32)

    smem, vmem = pl.BlockSpec(memory_space=pltpu.SMEM), pl.BlockSpec(memory_space=pltpu.VMEM)
    return pl.pallas_call(
        kernel,
        out_shape=jax.ShapeDtypeStruct((n * part, f), F32),
        in_specs=[smem] + [vmem] * n,
        out_specs=vmem,
        compiler_params=pltpu.CompilerParams(vmem_limit_bytes=VMEM_LIMIT),
    )(me, *pieces)


def reduce_gradient(me, keep, send):
    n_row, n_col = lax.axis_size("row"), lax.axis_size("col")
    part = keep.shape[0] // (n_row // 2)
    chip = keep.astype(F32) + swap(send, "row", 1).astype(F32)
    mine = chip[:part]
    for k in range(1, n_row // 2):
        mine = mine + swap(chip[k * part:(k + 1) * part].astype(BF16), "row", 2 * k).astype(F32)
    bit = 1
    while bit < n_col:
        rounded = mine.astype(BF16)
        if 2 * bit < n_col:
            others = [swap(rounded, "col", m * bit).astype(F32) for m in (1, 2, 3)]
            mine = (rounded.astype(F32) + others[0]) + (others[1] + others[2])
            bit *= 4
        else:
            mine = rounded.astype(F32) + swap(rounded, "col", bit).astype(F32)
            bit *= 2
    rounded = mine.astype(BF16)
    even = [rounded] + [swap(rounded, "row", 2 * k) for k in range(1, n_row // 2)]
    pieces = []
    for p in even:
        pieces += [p, swap(p, "row", 1)]
    return join(me, pieces)


def plus(*terms):
    return sum((t.astype(F32) for t in terms[1:]), terms[0].astype(F32)).astype(BF16)


def sum_terms(*terms):
    def kernel(*refs):
        total = refs[0][...].astype(F32)
        for ref in refs[1:-1]:
            total += ref[...].astype(F32)
        refs[-1][...] = total.astype(BF16)

    vmem = pl.BlockSpec(memory_space=pltpu.VMEM)
    return pl.pallas_call(
        kernel,
        out_shape=jax.ShapeDtypeStruct(terms[0].shape, BF16),
        in_specs=[vmem] * len(terms),
        out_specs=vmem,
        compiler_params=pltpu.CompilerParams(vmem_limit_bytes=VMEM_LIMIT),
        cost_estimate=pl.CostEstimate(flops=COST, bytes_accessed=4 * terms[0].size * 2, transcendentals=0),
    )(*terms)


def local(features, tile_values, tile_index, tile_count, weight, cotangent):
    n_row, n_col = lax.axis_size("row"), lax.axis_size("col")
    me = jnp.stack([lax.axis_index("row"), lax.axis_index("col")]).astype(jnp.int32)
    tiles = stage(tile_values[0, 0])
    scalars = jnp.concatenate([me, tile_count[0], tile_index[0, 0]])
    starts = [sum(CHUNKS[:j]) for j in range(len(CHUNKS))]
    parts = [features[:, at:at + wide] for at, wide in zip(starts, CHUNKS)]
    own, tiles, scalars = lax.optimization_barrier((features, tiles, scalars))
    core = swap(own, "row", 1)
    keep, terms = (), []
    for part, at in zip(parts, starts):
        part, *keep = lax.optimization_barrier((part, *keep))
        pieces = [features, core]
        for block in gather_chips(part):
            pieces += [block, swap(block, "row", 1)]
        *keep, near, away = tile_products(scalars, tiles, pieces, at)
        if terms:
            stay, far, got_near = terms
            before = sum_terms(stay, got_near)
            away, before = lax.optimization_barrier((away, before))
        got = swap(away, "col", 1)
        send = plus(keep[1], got)
        if terms:
            before = sum_terms(before, far)
            send, before = lax.optimization_barrier((send, before))
            near, got = lax.optimization_barrier((near, got))
        terms = [keep[0], swap(send, "col", 2), swap(near, "col", 1)]
    terms = [(before, 0)] + [(t, at) for t in terms]
    if n_col > 4:
        bit = 4
        mine = jnp.concatenate([plus(*(t for t, place in terms if place == at)) for at in starts], axis=1)
        while bit < n_col:
            half = mine.shape[0] // 2
            mine = plus(mine[:half], swap(mine[half:], "col", bit))
            bit *= 2
        terms = [(mine, 0)]
    terms, places = zip(*terms)
    scale = 1.0 / math.sqrt(cotangent.shape[0] * n_row * n_col)
    output, grad_keep, grad_send = vertex_step(me, weight, cotangent, terms, places, scale)
    return output, reduce_gradient(me, grad_keep, grad_send)


def solution(mesh):
    placed = (
        P(("col", "row"), None),
        P("row", "col", None, None, None),
        P("row", "col", None),
        P("row", "col"),
        P(),
        P(("row", "col"), None),
    )
    return jax.shard_map(
        local, mesh=mesh, in_specs=placed, out_specs=(P(("row", "col"), None), P()), check_vma=False
    )
```

time: 103 us -> 95.6 us (0.928)
  waiting for transfers between devices: 61.7 us -> 53.2 us
  starting transfers between devices: 32 us -> 30.8 us
    ppermute x34 -> x33, waiting for transfers between devices: 61.7 us -> 53.2 us  [swap(): lax.ppermute(x, axis, [(i, i ^ mask) for i in range(lax.axis_size(axis))])]
    ppermute x34 -> x33, starting transfers between devices: 32 us -> 30.8 us  [swap(): lax.ppermute(x, axis, [(i, i ^ mask) for i in range(lax.axis_size(axis))])]
    pallas_call x3 -> x6, Pallas kernels: 4.2 us -> 4.85 us  [the longest x2 2.63 us: tile_products(): pl.pallas_call(functools.partial(tiles_kernel, at=at, n_row=n_row, n_col=...]
  transfers between devices with their start and end apart: 34 -> 33, of which waited for: 19 -> 23; matrix products, arithmetic and copies ran while one was open for 0% -> 0% of each run, Pallas kernels for 2% -> 2%
where the time goes in v2:
time: 95.6 us; the launch traced here: 95.2 us
  waiting for transfers between devices  53.2 us (56%)
  starting transfers between devices  30.8 us (32%)
  Pallas kernels  6.43 us (7%)
  local copies, waits for them, and re-layouts  2.79 us (3%)
  between operations  1.43 us (1%)
    ppermute x33, waiting for transfers between devices, swap(): lax.ppermute(x, axis, [(i, i ^ mask) for i in range(lax.axis_size(axis))])  53.2 us
    ppermute x33, starting transfers between devices, swap(): lax.ppermute(x, axis, [(i, i ^ mask) for i in range(lax.axis_size(axis))])  30.8 us
    pallas_call x2, Pallas kernels, tile_products(): pl.pallas_call(functools.partial(tiles_kernel, at=at, n_row=n_row, n_col=...  2.63 us
    pallas_call x1, Pallas kernels, vertex_step(): pl.pallas_call(functools.partial(vertex_kernel, n_row=n_row, places=place...  2.02 us
  transfers between devices with their start and end apart: 33, of which 23 were waited for; matrix products, arithmetic and copies ran while one was open for 0% of the time, Pallas kernels for 2%

profile of v2, /device:TPU:0, one launch (start us, length us, event | category | flops | bytes accessed | tf_op | source)
XLA Modules:
  0.0 95.2 jit_solution(6483604615258409399)
XLA Ops:
  1.8 4.0 %collective-permute-start.5 = (bf16[512,256]{1,0:T(8,128)(2,1)S(1)}, bf16[512,256]{1,0:T(8,128)(2,1)S(1)}, u32[]{:S(2)}, u32[]{:S(2)}) collective-permute-start(bf16[512,256]{1,0:T(8,128)(2,1)S(1)} %get-tuple-element.44), channel_id=1, source_target_pairs={{0,24},{4,28},{8,16},{12,20},{16,8},{20,12},{24,0},{28,4},{1,25},{... | collective-permute-start | bytes 786440 | tf_op jit(solution)/shard_map/ppermute | solution.py:20
  8.8 4.1 %collective-permute-done.5.refs_6_ = bf16[512,256]{1,0:T(8,128)(2,1)S(1)} collective-permute-done((bf16[512,256]{1,0:T(8,128)(2,1)S(1)}, bf16[512,256]{1,0:T(8,128)(2,1)S(1)}, u32[]{:S(2)}, u32[]{:S(2)}) %collective-permute-start.5) | collective-permute-done | bytes 262176 | tf_op jit(solution)/shard_map/ppermute | solution.py:20
  12.9 4.7 %collective-permute-done.3.refs_4_ = bf16[512,256]{1,0:T(8,128)(2,1)S(1)} collective-permute-done((bf16[512,256]{1,0:T(8,128)(2,1)S(1)}, bf16[512,256]{1,0:T(8,128)(2,1)S(1)}, u32[]{:S(2)}, u32[]{:S(2)}) %collective-permute-start.3) | collective-permute-done | bytes 262176 | tf_op jit(solution)/shard_map/ppermute | solution.py:20
  20.9 1.6 %collective-permute-start.15 = (bf16[512,256]{1,0:T(8,128)(2,1)S(1)}, bf16[512,256]{1,0:T(8,128)(2,1)S(1)}, u32[]{:S(2)}, u32[]{:S(2)}) collective-permute-start(bf16[512,256]{1,0:T(8,128)(2,1)S(1)} %get-tuple-element.33), channel_id=1, source_target_pairs={{0,1},{1,0},{2,3},{3,2},{4,5},{5,4},{6,7},{7,6},{8,9},{9,8},{10,11... | collective-permute-start | bytes 786440 | tf_op jit(solution)/shard_map/ppermute | solution.py:20
  22.5 3.0 %collective-permute-start.11 = (bf16[512,256]{1,0:T(8,128)(2,1)S(1)}, bf16[512,256]{1,0:T(8,128)(2,1)S(1)}, u32[]{:S(2)}, u32[]{:S(2)}) collective-permute-start(bf16[512,256]{1,0:T(8,128)(2,1)S(1)} %get-tuple-element.27), channel_id=1, source_target_pairs={{0,24},{4,28},{8,16},{12,20},{16,8},{20,12},{24,0},{28,4},{1,25},{... | collective-permute-start | bytes 786440 | tf_op jit(solution)/shard_map/ppermute | solution.py:20
  27.1 2.9 %collective-permute-done.15 = bf16[512,256]{1,0:T(8,128)(2,1)S(1)} collective-permute-done((bf16[512,256]{1,0:T(8,128)(2,1)S(1)}, bf16[512,256]{1,0:T(8,128)(2,1)S(1)}, u32[]{:S(2)}, u32[]{:S(2)}) %collective-permute-start.15) | collective-permute-done | bytes 262176 | tf_op jit(solution)/shard_map/ppermute | solution.py:20
  30.2 2.7 %collective-permute-start.16 = (bf16[512,256]{1,0:T(8,128)(2,1)S(1)}, bf16[512,256]{1,0:T(8,128)(2,1)S(1)}, u32[]{:S(2)}, u32[]{:S(2)}) collective-permute-start(bf16[512,256]{1,0:T(8,128)(2,1)S(1)} %add_convert_fusion), channel_id=1, source_target_pairs={{0,2},{1,3},{2,0},{3,1},{4,6},{5,7},{6,4},{7,5},{8,10},{9,11},{10,... | collective-permute-start | bytes 786440 | tf_op jit(solution)/shard_map/ppermute | solution.py:20
  32.8 4.7 %collective-permute-done.9.refs_4_ = bf16[512,256]{1,0:T(8,128)(2,1)S(1)} collective-permute-done((bf16[512,256]{1,0:T(8,128)(2,1)S(1)}, bf16[512,256]{1,0:T(8,128)(2,1)S(1)}, u32[]{:S(2)}, u32[]{:S(2)}) %collective-permute-start.9) | collective-permute-done | bytes 262176 | tf_op jit(solution)/shard_map/ppermute | solution.py:20
  38.1 1.4 %collective-permute-done.13.refs_1_ = bf16[512,256]{1,0:T(8,128)(2,1)S(1)} collective-permute-done((bf16[512,256]{1,0:T(8,128)(2,1)S(1)}, bf16[512,256]{1,0:T(8,128)(2,1)S(1)}, u32[]{:S(2)}, u32[]{:S(2)}) %collective-permute-start.13) | collective-permute-done | bytes 262176 | tf_op jit(solution)/shard_map/ppermute | solution.py:20
  41.5 3.1 %collective-permute-done.16.refs_1_ = bf16[512,256]{1,0:T(8,128)(2,1)S(1)} collective-permute-done((bf16[512,256]{1,0:T(8,128)(2,1)S(1)}, bf16[512,256]{1,0:T(8,128)(2,1)S(1)}, u32[]{:S(2)}, u32[]{:S(2)}) %collective-permute-start.16) | collective-permute-done | bytes 262176 | tf_op jit(solution)/shard_map/ppermute | solution.py:20
  44.7 5.4 %collective-permute-done.14 = bf16[512,256]{1,0:T(8,128)(2,1)S(1)} collective-permute-done((bf16[512,256]{1,0:T(8,128)(2,1)S(1)}, bf16[512,256]{1,0:T(8,128)(2,1)S(1)}, u32[]{:S(2)}, u32[]{:S(2)}) %collective-permute-start.14) | collective-permute-done | bytes 262176 | tf_op jit(solution)/shard_map/ppermute | solution.py:20
  50.4 4.2 %collective-permute-start.17 = (bf16[512,256]{1,0:T(8,128)(2,1)S(1)}, bf16[512,256]{1,0:T(8,128)(2,1)S(1)}, u32[]{:S(2)}, u32[]{:S(2)}) collective-permute-start(bf16[512,256]{1,0:T(8,128)(2,1)S(1)} %add_convert_fusion.1), channel_id=1, source_target_pairs={{0,2},{1,3},{2,0},{3,1},{4,6},{5,7},{6,4},{7,5},{8,10},{9,11},{10,... | collective-permute-start | bytes 786440 | tf_op jit(solution)/shard_map/ppermute | solution.py:20
  54.7 8.9 %collective-permute-done.18.refs_3_ = bf16[512,256]{1,0:T(8,128)(2,1)S(1)} collective-permute-done((bf16[512,256]{1,0:T(8,128)(2,1)S(1)}, bf16[512,256]{1,0:T(8,128)(2,1)S(1)}, u32[]{:S(2)}, u32[]{:S(2)}) %collective-permute-start.18) | collective-permute-done | bytes 262176 | tf_op jit(solution)/shard_map/ppermute | solution.py:20
  63.6 2.9 %collective-permute-done.17.refs_2_ = bf16[512,256]{1,0:T(8,128)(2,1)S(1)} collective-permute-done((bf16[512,256]{1,0:T(8,128)(2,1)S(1)}, bf16[512,256]{1,0:T(8,128)(2,1)S(1)}, u32[]{:S(2)}, u32[]{:S(2)}) %collective-permute-start.17) | collective-permute-done | bytes 262176 | tf_op jit(solution)/shard_map/ppermute | solution.py:20
  66.5 2.0 %shard_map.82 = (bf16[512,512]{1,0:T(8,128)(2,1)}, bf16[256,512]{1,0:T(8,128)(2,1)S(1)}, bf16[256,512]{1,0:T(8,128)(2,1)S(1)}) custom-call(s32[2]{0:T(128)S(1)} %pad_add_fusion.me_ref, bf16[512,512]{1,0:T(8,128)(2,1)S(1)} %copy-done.2, bf16[512,512]{1,0:T(8,128)(2,1)S(1)} %copy-done.3, bf16[512,256]{1,0:T(8,128)(2,1)S(1)} %shard_map.81.refs_0_, ...), custom_call_target="tpu_custom_call" | custom-call | flops 536870912 | bytes 4194304 | tf_op jit(solution)/shard_map/pallas_call | solution.py:135
  68.6 1.5 %collective-permute-done.19 = bf16[256,512]{1,0:T(8,128)(2,1)S(1)} collective-permute-done((bf16[256,512]{1,0:T(8,128)(2,1)S(1)}, bf16[256,512]{1,0:T(8,128)(2,1)S(1)}, u32[]{:S(2)}, u32[]{:S(2)}) %collective-permute-start.19) | collective-permute-done | bytes 262176 | tf_op jit(solution)/shard_map/ppermute | solution.py:20
  71.3 2.4 %collective-permute-start.21 = (bf16[64,512]{1,0:T(8,128)(2,1)S(1)}, bf16[64,512]{1,0:T(8,128)(2,1)S(1)}, u32[]{:S(2)}, u32[]{:S(2)}) collective-permute-start(bf16[64,512]{1,0:T(8,128)(2,1)S(1)} %get-tuple-element.48), channel_id=1, source_target_pairs={{0,16},{4,20},{8,24},{12,28},{16,0},{20,4},{24,8},{28,12},{1,17},{... | collective-permute-start | bytes 196616 | tf_op jit(solution)/shard_map/ppermute | solution.py:20
  77.0 2.4 %collective-permute-start.25 = (bf16[64,512]{1,0:T(8,128)(2,1)S(1)}, bf16[64,512]{1,0:T(8,128)(2,1)S(1)}, u32[]{:S(2)}, u32[]{:S(2)}) collective-permute-start(bf16[64,512]{1,0:T(8,128)(2,1)S(1)} %fusion.2), channel_id=1, source_target_pairs={{0,3},{1,2},{2,1},{3,0},{4,7},{5,6},{6,5},{7,4},{8,11},{9,10},{10,... | collective-permute-start | bytes 196616 | tf_op jit(solution)/shard_map/ppermute | solution.py:20
  79.5 2.0 %collective-permute-start.23 = (bf16[64,512]{1,0:T(8,128)(2,1)S(1)}, bf16[64,512]{1,0:T(8,128)(2,1)S(1)}, u32[]{:S(2)}, u32[]{:S(2)}) collective-permute-start(bf16[64,512]{1,0:T(8,128)(2,1)S(1)} %fusion.2), channel_id=1, source_target_pairs={{0,1},{1,0},{2,3},{3,2},{4,5},{5,4},{6,7},{7,6},{8,9},{9,8},{10,11... | collective-permute-start | bytes 196616 | tf_op jit(solution)/shard_map/ppermute | solution.py:20
  81.5 1.9 %collective-permute-done.25 = bf16[64,512]{1,0:T(8,128)(2,1)S(1)} collective-permute-done((bf16[64,512]{1,0:T(8,128)(2,1)S(1)}, bf16[64,512]{1,0:T(8,128)(2,1)S(1)}, u32[]{:S(2)}, u32[]{:S(2)}) %collective-permute-start.25) | collective-permute-done | bytes 65568 | tf_op jit(solution)/shard_map/ppermute | solution.py:20
  83.4 2.0 %collective-permute-done.24 = bf16[64,512]{1,0:T(8,128)(2,1)S(1)} collective-permute-done((bf16[64,512]{1,0:T(8,128)(2,1)S(1)}, bf16[64,512]{1,0:T(8,128)(2,1)S(1)}, u32[]{:S(2)}, u32[]{:S(2)}) %collective-permute-start.24) | collective-permute-done | bytes 65568 | tf_op jit(solution)/shard_map/ppermute | solution.py:20
  85.4 1.5 %collective-permute-start.31 = (bf16[64,512]{1,0:T(8,128)(2,1)S(1)}, bf16[64,512]{1,0:T(8,128)(2,1)S(1)}, u32[]{:S(2)}, u32[]{:S(2)}) collective-permute-start(bf16[64,512]{1,0:T(8,128)(2,1)S(1)} %add_convert_fusion.2.refs_0_), channel_id=1, source_target_pairs={{0,24},{4,28},{8,16},{12,20},{16,8},{20,12},{24,0},{28,4},{1,25},{... | collective-permute-start | bytes 196616 | tf_op jit(solution)/shard_map/ppermute | solution.py:20
  89.0 2.1 %collective-permute-done.31.refs_6_ = bf16[64,512]{1,0:T(8,128)(2,1)S(1)} collective-permute-done((bf16[64,512]{1,0:T(8,128)(2,1)S(1)}, bf16[64,512]{1,0:T(8,128)(2,1)S(1)}, u32[]{:S(2)}, u32[]{:S(2)}) %collective-permute-start.31) | collective-permute-done | bytes 65568 | tf_op jit(solution)/shard_map/ppermute | solution.py:20
  93.6 1.6 %shard_map.83 = f32[512,512]{1,0:T(8,128)} custom-call(s32[2]{0:T(128)S(1)} %pad_add_fusion.me_ref, bf16[64,512]{1,0:T(8,128)(2,1)S(1)} %add_convert_fusion.2.refs_0_, bf16[64,512]{1,0:T(8,128)(2,1)S(1)} %collective-permute-done.26.refs_1_, bf16[64,512]{1,0:T(8,128)(2,1)S(1)} %collective-permute-done.27.refs_2_, ...), custom_call_target="tpu_custom_call" | custom-call | tf_op jit(solution)/shard_map/pallas_call | solution.py:158
  (68 shorter events, 20.6 us)
Async XLA Ops:
  1.8 11.1 %collective-permute-start.5 = (bf16[512,256]{1,0:T(8,128)(2,1)S(1)}, bf16[512,256]{1,0:T(8,128)(2,1)S(1)}, u32[]{:S(2)}, u32[]{:S(2)}) collective-permute-start(bf16[512,256]{1,0:T(8,128)(2,1)S(1)} %get-tuple-element.44), channel_id=1, source_target_pairs={{0,24},{4,28},{8,16},{12,20},{16,8},{20,12},{24,0},{28,4},{1,25},{... | collective-permute-start | bytes 786440 | tf_op jit(solution)/shard_map/ppermute | solution.py:20
  5.7 11.9 %collective-permute-start.3 = (bf16[512,256]{1,0:T(8,128)(2,1)S(1)}, bf16[512,256]{1,0:T(8,128)(2,1)S(1)}, u32[]{:S(2)}, u32[]{:S(2)}) collective-permute-start(bf16[512,256]{1,0:T(8,128)(2,1)S(1)} %get-tuple-element.44), channel_id=1, source_target_pairs={{0,16},{4,20},{8,24},{12,28},{16,0},{20,4},{24,8},{28,12},{1,17},{... | collective-permute-start | bytes 786440 | tf_op jit(solution)/shard_map/ppermute | solution.py:20
  6.2 11.7 %collective-permute-start.1 = (bf16[512,256]{1,0:T(8,128)(2,1)S(1)}, bf16[512,256]{1,0:T(8,128)(2,1)S(1)}, u32[]{:S(2)}, u32[]{:S(2)}) collective-permute-start(bf16[512,256]{1,0:T(8,128)(2,1)S(1)} %get-tuple-element.44), channel_id=1, source_target_pairs={{0,8},{4,12},{8,0},{12,4},{16,24},{20,28},{24,16},{28,20},{1,9},{5... | collective-permute-start | bytes 786440 | tf_op jit(solution)/shard_map/ppermute | solution.py:20
  8.8 10.8 %collective-permute-start = (bf16[512,512]{1,0:T(8,128)(2,1)S(1)}, bf16[512,512]{1,0:T(8,128)(2,1)S(1)}, u32[]{:S(2)}, u32[]{:S(2)}) collective-permute-start(bf16[512,512]{1,0:T(8,128)(2,1)S(1)} %copy-done), channel_id=1, source_target_pairs={{0,4},{4,0},{8,12},{12,8},{16,20},{20,16},{24,28},{28,24},{1,5},{5... | collective-permute-start | bytes 1572872 | tf_op jit(solution)/shard_map/ppermute | solution.py:20
  12.9 5.3 %collective-permute-start.6 = (bf16[512,256]{1,0:T(8,128)(2,1)S(1)}, bf16[512,256]{1,0:T(8,128)(2,1)S(1)}, u32[]{:S(2)}, u32[]{:S(2)}) collective-permute-start(bf16[512,256]{1,0:T(8,128)(2,1)S(1)} %collective-permute-done.5.refs_6_), channel_id=1, source_target_pairs={{0,4},{4,0},{8,12},{12,8},{16,20},{20,16},{24,28},{28,24},{1,5},{5... | collective-permute-start | bytes 786440 | tf_op jit(solution)/shard_map/ppermute | solution.py:20
  20.9 9.2 %collective-permute-start.15 = (bf16[512,256]{1,0:T(8,128)(2,1)S(1)}, bf16[512,256]{1,0:T(8,128)(2,1)S(1)}, u32[]{:S(2)}, u32[]{:S(2)}) collective-permute-start(bf16[512,256]{1,0:T(8,128)(2,1)S(1)} %get-tuple-element.33), channel_id=1, source_target_pairs={{0,1},{1,0},{2,3},{3,2},{4,5},{5,4},{6,7},{7,6},{8,9},{9,8},{10,11... | collective-permute-start | bytes 786440 | tf_op jit(solution)/shard_map/ppermute | solution.py:20
  22.5 10.3 %collective-permute-start.11 = (bf16[512,256]{1,0:T(8,128)(2,1)S(1)}, bf16[512,256]{1,0:T(8,128)(2,1)S(1)}, u32[]{:S(2)}, u32[]{:S(2)}) collective-permute-start(bf16[512,256]{1,0:T(8,128)(2,1)S(1)} %get-tuple-element.27), channel_id=1, source_target_pairs={{0,24},{4,28},{8,16},{12,20},{16,8},{20,12},{24,0},{28,4},{1,25},{... | collective-permute-start | bytes 786440 | tf_op jit(solution)/shard_map/ppermute | solution.py:20
  25.5 12.1 %collective-permute-start.9 = (bf16[512,256]{1,0:T(8,128)(2,1)S(1)}, bf16[512,256]{1,0:T(8,128)(2,1)S(1)}, u32[]{:S(2)}, u32[]{:S(2)}) collective-permute-start(bf16[512,256]{1,0:T(8,128)(2,1)S(1)} %get-tuple-element.27), channel_id=1, source_target_pairs={{0,16},{4,20},{8,24},{12,28},{16,0},{20,4},{24,8},{28,12},{1,17},{... | collective-permute-start | bytes 786440 | tf_op jit(solution)/shard_map/ppermute | solution.py:20
  25.9 11.7 %collective-permute-start.7 = (bf16[512,256]{1,0:T(8,128)(2,1)S(1)}, bf16[512,256]{1,0:T(8,128)(2,1)S(1)}, u32[]{:S(2)}, u32[]{:S(2)}) collective-permute-start(bf16[512,256]{1,0:T(8,128)(2,1)S(1)} %get-tuple-element.27), channel_id=1, source_target_pairs={{0,8},{4,12},{8,0},{12,4},{16,24},{20,28},{24,16},{28,20},{1,9},{5... | collective-permute-start | bytes 786440 | tf_op jit(solution)/shard_map/ppermute | solution.py:20
  26.0 13.5 %collective-permute-start.13 = (bf16[512,256]{1,0:T(8,128)(2,1)S(1)}, bf16[512,256]{1,0:T(8,128)(2,1)S(1)}, u32[]{:S(2)}, u32[]{:S(2)}) collective-permute-start(bf16[512,256]{1,0:T(8,128)(2,1)S(1)} %get-tuple-element.30), channel_id=1, source_target_pairs={{0,1},{1,0},{2,3},{3,2},{4,5},{5,4},{6,7},{7,6},{8,9},{9,8},{10,11... | collective-permute-start | bytes 786440 | tf_op jit(solution)/shard_map/ppermute | solution.py:20
  30.2 14.5 %collective-permute-start.16 = (bf16[512,256]{1,0:T(8,128)(2,1)S(1)}, bf16[512,256]{1,0:T(8,128)(2,1)S(1)}, u32[]{:S(2)}, u32[]{:S(2)}) collective-permute-start(bf16[512,256]{1,0:T(8,128)(2,1)S(1)} %add_convert_fusion), channel_id=1, source_target_pairs={{0,2},{1,3},{2,0},{3,1},{4,6},{5,7},{6,4},{7,5},{8,10},{9,11},{10,... | collective-permute-start | bytes 786440 | tf_op jit(solution)/shard_map/ppermute | solution.py:20
  32.8 6.7 %collective-permute-start.12 = (bf16[512,256]{1,0:T(8,128)(2,1)S(1)}, bf16[512,256]{1,0:T(8,128)(2,1)S(1)}, u32[]{:S(2)}, u32[]{:S(2)}) collective-permute-start(bf16[512,256]{1,0:T(8,128)(2,1)S(1)} %collective-permute-done.11.refs_6_), channel_id=1, source_target_pairs={{0,4},{4,0},{8,12},{12,8},{16,20},{20,16},{24,28},{28,24},{1,5},{5... | collective-permute-start | bytes 786440 | tf_op jit(solution)/shard_map/ppermute | solution.py:20
  40.9 9.2 %collective-permute-start.14 = (bf16[512,256]{1,0:T(8,128)(2,1)S(1)}, bf16[512,256]{1,0:T(8,128)(2,1)S(1)}, u32[]{:S(2)}, u32[]{:S(2)}) collective-permute-start(bf16[512,256]{1,0:T(8,128)(2,1)S(1)} %get-tuple-element.31), channel_id=1, source_target_pairs={{0,1},{1,0},{2,3},{3,2},{4,5},{5,4},{6,7},{7,6},{8,9},{9,8},{10,11... | collective-permute-start | bytes 786440 | tf_op jit(solution)/shard_map/ppermute | solution.py:20
  50.1 13.5 %collective-permute-start.18 = (bf16[512,256]{1,0:T(8,128)(2,1)S(1)}, bf16[512,256]{1,0:T(8,128)(2,1)S(1)}, u32[]{:S(2)}, u32[]{:S(2)}) collective-permute-start(bf16[512,256]{1,0:T(8,128)(2,1)S(1)} %get-tuple-element.38), channel_id=1, source_target_pairs={{0,1},{1,0},{2,3},{3,2},{4,5},{5,4},{6,7},{7,6},{8,9},{9,8},{10,11... | collective-permute-start | bytes 786440 | tf_op jit(solution)/shard_map/ppermute | solution.py:20
  50.4 16.1 %collective-permute-start.17 = (bf16[512,256]{1,0:T(8,128)(2,1)S(1)}, bf16[512,256]{1,0:T(8,128)(2,1)S(1)}, u32[]{:S(2)}, u32[]{:S(2)}) collective-permute-start(bf16[512,256]{1,0:T(8,128)(2,1)S(1)} %add_convert_fusion.1), channel_id=1, source_target_pairs={{0,2},{1,3},{2,0},{3,1},{4,6},{5,7},{6,4},{7,5},{8,10},{9,11},{10,... | collective-permute-start | bytes 786440 | tf_op jit(solution)/shard_map/ppermute | solution.py:20
  70.2 4.9 %collective-permute-start.20 = (bf16[64,512]{1,0:T(8,128)(2,1)S(1)}, bf16[64,512]{1,0:T(8,128)(2,1)S(1)}, u32[]{:S(2)}, u32[]{:S(2)}) collective-permute-start(bf16[64,512]{1,0:T(8,128)(2,1)S(1)} %get-tuple-element.46), channel_id=1, source_target_pairs={{0,8},{4,12},{8,0},{12,4},{16,24},{20,28},{24,16},{28,20},{1,9},{5... | collective-permute-start | bytes 196616 | tf_op jit(solution)/shard_map/ppermute | solution.py:20
  71.0 5.2 %collective-permute-start.22 = (bf16[64,512]{1,0:T(8,128)(2,1)S(1)}, bf16[64,512]{1,0:T(8,128)(2,1)S(1)}, u32[]{:S(2)}, u32[]{:S(2)}) collective-permute-start(bf16[64,512]{1,0:T(8,128)(2,1)S(1)} %get-tuple-element.47), channel_id=1, source_target_pairs={{0,24},{4,28},{8,16},{12,20},{16,8},{20,12},{24,0},{28,4},{1,25},{... | collective-permute-start | bytes 196616 | tf_op jit(solution)/shard_map/ppermute | solution.py:20
  71.3 5.7 %collective-permute-start.21 = (bf16[64,512]{1,0:T(8,128)(2,1)S(1)}, bf16[64,512]{1,0:T(8,128)(2,1)S(1)}, u32[]{:S(2)}, u32[]{:S(2)}) collective-permute-start(bf16[64,512]{1,0:T(8,128)(2,1)S(1)} %get-tuple-element.48), channel_id=1, source_target_pairs={{0,16},{4,20},{8,24},{12,28},{16,0},{20,4},{24,8},{28,12},{1,17},{... | collective-permute-start | bytes 196616 | tf_op jit(solution)/shard_map/ppermute | solution.py:20
  77.0 6.4 %collective-permute-start.25 = (bf16[64,512]{1,0:T(8,128)(2,1)S(1)}, bf16[64,512]{1,0:T(8,128)(2,1)S(1)}, u32[]{:S(2)}, u32[]{:S(2)}) collective-permute-start(bf16[64,512]{1,0:T(8,128)(2,1)S(1)} %fusion.2), channel_id=1, source_target_pairs={{0,3},{1,2},{2,1},{3,0},{4,7},{5,6},{6,5},{7,4},{8,11},{9,10},{10,... | collective-permute-start | bytes 196616 | tf_op jit(solution)/shard_map/ppermute | solution.py:20
  79.5 5.9 %collective-permute-start.24 = (bf16[64,512]{1,0:T(8,128)(2,1)S(1)}, bf16[64,512]{1,0:T(8,128)(2,1)S(1)}, u32[]{:S(2)}, u32[]{:S(2)}) collective-permute-start(bf16[64,512]{1,0:T(8,128)(2,1)S(1)} %fusion.2), channel_id=1, source_target_pairs={{0,2},{1,3},{2,0},{3,1},{4,6},{5,7},{6,4},{7,5},{8,10},{9,11},{10,... | collective-permute-start | bytes 196616 | tf_op jit(solution)/shard_map/ppermute | solution.py:20
  79.5 5.9 %collective-permute-start.23 = (bf16[64,512]{1,0:T(8,128)(2,1)S(1)}, bf16[64,512]{1,0:T(8,128)(2,1)S(1)}, u32[]{:S(2)}, u32[]{:S(2)}) collective-permute-start(bf16[64,512]{1,0:T(8,128)(2,1)S(1)} %fusion.2), channel_id=1, source_target_pairs={{0,1},{1,0},{2,3},{3,2},{4,5},{5,4},{6,7},{7,6},{8,9},{9,8},{10,11... | collective-permute-start | bytes 196616 | tf_op jit(solution)/shard_map/ppermute | solution.py:20
  85.4 5.6 %collective-permute-start.31 = (bf16[64,512]{1,0:T(8,128)(2,1)S(1)}, bf16[64,512]{1,0:T(8,128)(2,1)S(1)}, u32[]{:S(2)}, u32[]{:S(2)}) collective-permute-start(bf16[64,512]{1,0:T(8,128)(2,1)S(1)} %add_convert_fusion.2.refs_0_), channel_id=1, source_target_pairs={{0,24},{4,28},{8,16},{12,20},{16,8},{20,12},{24,0},{28,4},{1,25},{... | collective-permute-start | bytes 196616 | tf_op jit(solution)/shard_map/ppermute | solution.py:20
  86.9 4.8 %collective-permute-start.29 = (bf16[64,512]{1,0:T(8,128)(2,1)S(1)}, bf16[64,512]{1,0:T(8,128)(2,1)S(1)}, u32[]{:S(2)}, u32[]{:S(2)}) collective-permute-start(bf16[64,512]{1,0:T(8,128)(2,1)S(1)} %add_convert_fusion.2.refs_0_), channel_id=1, source_target_pairs={{0,16},{4,20},{8,24},{12,28},{16,0},{20,4},{24,8},{28,12},{1,17},{... | collective-permute-start | bytes 196616 | tf_op jit(solution)/shard_map/ppermute | solution.py:20
  88.1 4.3 %collective-permute-start.27 = (bf16[64,512]{1,0:T(8,128)(2,1)S(1)}, bf16[64,512]{1,0:T(8,128)(2,1)S(1)}, u32[]{:S(2)}, u32[]{:S(2)}) collective-permute-start(bf16[64,512]{1,0:T(8,128)(2,1)S(1)} %add_convert_fusion.2.refs_0_), channel_id=1, source_target_pairs={{0,8},{4,12},{8,0},{12,4},{16,24},{20,28},{24,16},{28,20},{1,9},{5... | collective-permute-start | bytes 196616 | tf_op jit(solution)/shard_map/ppermute | solution.py:20
  (14 other events, 68.4 us)

commit v3 on v2

v3 whole, which is shorter than its diff:
```python
import functools
import math

import jax
import jax.numpy as jnp
from jax import lax
from jax.experimental import pallas as pl
from jax.experimental.pallas import tpu as pltpu
from jax.sharding import PartitionSpec as P

BLK = 256
RBG = 8
CHUNKS = (256, 256)
FIELD = 256
COST = 15 * 10**9
VMEM_LIMIT = 48 * 1024 * 1024
F32, BF16 = jnp.float32, jnp.bfloat16


def swap(x, axis, mask):
    return lax.ppermute(x, axis, [(i, i ^ mask) for i in range(lax.axis_size(axis))])


def bit_reversed(i, bits):
    out = 0 * i
    for b in range(bits):
        out = out + (((i >> b) & 1) << (bits - 1 - b))
    return out


def gather_chips(early, late):
    return [swap(early if k & (k - 1) == 0 else late, "row", k) for k in range(2, lax.axis_size("row"), 2)]


def relay_chips(x, *later):
    half = x.shape[0] // 2
    masks = sorted(range(2, lax.axis_size("row"), 2), key=lambda k: (bin(k).count("1"), k))
    near = [k for k in masks if k & (k - 1) == 0]
    halves = {}
    for early in (True, False):
        for k in near:
            h = int((k != near[0]) == early)
            halves[k, h] = swap(x[h * half:(h + 1) * half], "row", k)
    first = [(k, int(k != near[0])) for k in near]
    arrived, later = lax.optimization_barrier(([halves[key] for key in first], later))
    halves.update(zip(first, arrived))
    for k in masks[len(near):]:
        low, high = k & -k, 1 << (k.bit_length() - 1)
        halves[k, 0] = swap(halves[k ^ high, 0], "row", high)
        halves[k, 1] = swap(halves[k ^ low, 1], "row", low)
    return [jnp.concatenate([halves[k, 0], halves[k, 1]]) for k in sorted(masks)], *later


def stage(x):
    def kernel(x_ref, out_ref, sem):
        copy = pltpu.make_async_copy(x_ref, out_ref, sem)
        copy.start()
        copy.wait()

    return pl.pallas_call(
        kernel,
        out_shape=jax.ShapeDtypeStruct(x.shape, x.dtype),
        in_specs=[pl.BlockSpec(memory_space=pl.ANY)],
        out_specs=pl.BlockSpec(memory_space=pltpu.VMEM),
        scratch_shapes=[pltpu.SemaphoreType.DMA],
        compiler_params=pltpu.CompilerParams(vmem_limit_bytes=VMEM_LIMIT),
    )(x)


def slot_numbers(index, count, rows):
    n_row, n_col = lax.axis_size("row"), lax.axis_size("col")
    own = RBG * BLK // n_col
    part, bits = min(BLK, rows, own), n_col.bit_length() - 1
    col_groups = rows * n_row // BLK
    live = jnp.arange(index.shape[0]) < count
    along = jnp.arange(0, BLK, part)
    first = (index % col_groups * BLK)[:, None] + along
    source = jnp.where(live[:, None], (first // rows) ^ lax.axis_index("row"), n_row)
    target = (index // col_groups * BLK)[:, None] + along
    place = bit_reversed((target // own) ^ lax.axis_index("col"), bits) * own + target % own
    numbers = (source + FIELD * (first % rows // part) + FIELD * FIELD * (place // part)).reshape(-1)
    return jnp.broadcast_to(jnp.pad(numbers.astype(jnp.int32), (0, 128 - numbers.size)), (8, 128))


def tiles_kernel(numbers_ref, tiles_ref, *refs, at, n_row, part):
    pieces, out_refs, (picked, total) = refs[:n_row], refs[n_row:-2], refs[-2:]
    kmax = tiles_ref.shape[0]
    wide = total.shape[1]
    parts = BLK // part
    total[...] = jnp.zeros_like(total)
    places = []
    for i in range(kmax * parts):
        k, to = i // parts, pl.ds(i % parts * part, part)
        number = numbers_ref[0, i]
        source, row = number & (FIELD - 1), (number // FIELD) & (FIELD - 1)
        places.append(pl.ds(pl.multiple_of(number // (FIELD * FIELD) * part, part), part))
        block = pl.ds(pl.multiple_of(row * part, part), part)

        @pl.when(source == n_row)
        def _(k=k, to=to):
            picked[k, to, :] = jnp.zeros((part, wide), BF16)

        for p in range(n_row):
            columns = slice(at, at + wide) if p < 2 else slice(None)

            @pl.when(source == p)
            def _(k=k, to=to, p=p, block=block, columns=columns):
                picked[k, to, :] = pieces[p][block, columns]

    for k in range(kmax):
        product = jnp.dot(tiles_ref[k], picked[k], preferred_element_type=F32)
        for j in range(parts):
            total[places[k * parts + j], :] += product[j * part:(j + 1) * part, :]

    quarter = total.shape[0] // 4
    for q, out_ref in enumerate(out_refs):
        out_ref[...] = total[q * quarter:(q + 1) * quarter, :].astype(BF16)


def tile_products(numbers, tiles, pieces, at):
    n_row, n_col = lax.axis_size("row"), lax.axis_size("col")
    wide = pieces[-1].shape[1]
    quarter = jax.ShapeDtypeStruct((RBG * BLK // 4, wide), BF16)
    vmem = pl.BlockSpec(memory_space=pltpu.VMEM)
    return pl.pallas_call(
        functools.partial(tiles_kernel, at=at, n_row=n_row, part=min(BLK, pieces[0].shape[0], RBG * BLK // n_col)),
        out_shape=(quarter,) * 4,
        in_specs=[vmem] * (2 + n_row),
        out_specs=(vmem,) * 4,
        scratch_shapes=[
            pltpu.VMEM((tiles.shape[0], BLK, wide), BF16),
            pltpu.VMEM((RBG * BLK, wide), F32),
        ],
        compiler_params=pltpu.CompilerParams(vmem_limit_bytes=VMEM_LIMIT),
        cost_estimate=pl.CostEstimate(
            flops=2 * tiles.shape[0] * BLK * BLK * wide, bytes_accessed=6 * 1024 * 1024, transcendentals=0),
    )(numbers, tiles, *pieces)


def early_part(terms, weight, at, before):
    n, wide = terms[0].shape
    f = weight.shape[1]

    def kernel(weight_ref, *refs):
        *terms, agg_ref, pre_ref = refs
        if before is not None:
            before_ref, *terms = terms
        total = terms[0][...].astype(F32)
        for term in terms[1:]:
            total += term[...].astype(F32)
        agg_ref[...] = total.astype(BF16)
        share = jnp.dot(agg_ref[...], weight_ref[at:at + wide, :], preferred_element_type=F32)
        pre_ref[...] = share if before is None else before_ref[...] + share

    vmem = pl.BlockSpec(memory_space=pltpu.VMEM)
    inputs = (weight, *([] if before is None else [before]), *terms)
    return pl.pallas_call(
        kernel,
        out_shape=(jax.ShapeDtypeStruct((n, wide), BF16), jax.ShapeDtypeStruct((n, f), F32)),
        in_specs=[vmem] * len(inputs),
        out_specs=(vmem,) * 2,
        compiler_params=pltpu.CompilerParams(vmem_limit_bytes=VMEM_LIMIT),
        cost_estimate=pl.CostEstimate(flops=COST, bytes_accessed=4 * n * f, transcendentals=0),
    )(*inputs)


def vertex_kernel(weight_ref, cot_ref, pre_ref, *refs, n_row, n_early, scale):
    early, (*terms, out_ref, keep_ref, send_ref, output, grad, sem) = refs[:n_early], refs[n_early:]
    me_row = lax.axis_index("row")
    cut = grad.shape[0] - terms[0].shape[1]
    total = terms[0][...].astype(F32)
    for term in terms[1:]:
        total += term[...].astype(F32)
    last = total.astype(BF16)
    preact = pre_ref[...] + jnp.dot(last, weight_ref[cut:, :], preferred_element_type=F32)
    power = jnp.exp(jnp.minimum(preact, 0.0))
    positive = preact > 0
    output[...] = jnp.where(positive, preact, power - 1.0).astype(BF16)
    copy = pltpu.make_async_copy(output, out_ref, sem)
    copy.start()
    grad_pre = (cot_ref[...].astype(F32) * jnp.where(positive, 1.0, power)).astype(BF16)
    over_rows = (((0,), (0,)), ((), ()))
    at = 0
    for aggregated in [ref[...] for ref in early] + [last]:
        wide = aggregated.shape[1]
        grad[at:at + wide, :] = lax.dot_general(
            aggregated, grad_pre, over_rows, preferred_element_type=F32) * scale
        at += wide
    part = grad.shape[0] // n_row
    for k in range(n_row):
        rows = grad[pl.ds(pl.multiple_of((me_row ^ k) * part, part), part), :].astype(BF16)
        target = send_ref if k % 2 else keep_ref
        target[(k // 2) * part:(k // 2 + 1) * part, :] = rows
    copy.wait()


def vertex_step(weight, cotangent, pre, early, terms, scale):
    n_row = lax.axis_size("row")
    n, f = cotangent.shape
    half = jax.ShapeDtypeStruct((f // 2, f), BF16)
    vmem = pl.BlockSpec(memory_space=pltpu.VMEM)
    return pl.pallas_call(
        functools.partial(vertex_kernel, n_row=n_row, n_early=len(early), scale=scale),
        out_shape=(jax.ShapeDtypeStruct((n, f), BF16), half, half),
        in_specs=[vmem] * (3 + len(early) + len(terms)),
        out_specs=(pl.BlockSpec(memory_space=pl.ANY), vmem, vmem),
        scratch_shapes=[pltpu.VMEM((n, f), BF16), pltpu.VMEM((f, f), F32), pltpu.SemaphoreType.DMA],
        compiler_params=pltpu.CompilerParams(vmem_limit_bytes=VMEM_LIMIT),
        cost_estimate=pl.CostEstimate(
            flops=4 * n * f * f, bytes_accessed=4 * 1024 * 1024, transcendentals=n * f),
    )(weight, cotangent, pre, *early, *terms)


def join(pieces):
    n = len(pieces)
    part, f = pieces[0].shape

    def kernel(*refs):
        out_ref = refs[-1]
        me_row = lax.axis_index("row")
        for k in range(n):
            at = pl.multiple_of((me_row ^ k) * part, part)
            out_ref[pl.ds(at, part), :] = refs[k][...].astype(F32)

    vmem = pl.BlockSpec(memory_space=pltpu.VMEM)
    return pl.pallas_call(
        kernel,
        out_shape=jax.ShapeDtypeStruct((n * part, f), F32),
        in_specs=[vmem] * n,
        out_specs=vmem,
        compiler_params=pltpu.CompilerParams(vmem_limit_bytes=VMEM_LIMIT),
    )(*pieces)


def reduce_gradient(keep, send):
    n_row, n_col = lax.axis_size("row"), lax.axis_size("col")
    part = keep.shape[0] // (n_row // 2)
    chip = keep.astype(F32) + swap(send, "row", 1).astype(F32)
    mine = chip[:part]
    for k in range(1, n_row // 2):
        mine = mine + swap(chip[k * part:(k + 1) * part].astype(BF16), "row", 2 * k).astype(F32)
    rounded, bit = mine.astype(BF16), 1
    while bit < n_col:
        if 2 * bit < n_col:
            others = [swap(rounded, "col", m * bit) for m in (1, 2, 3)]
            rounded = ((rounded.astype(F32) + others[0].astype(F32)) + (others[1].astype(F32) + others[2].astype(F32))).astype(BF16)
            bit *= 4
        else:
            rounded = plus(rounded, swap(rounded, "col", bit))
            bit *= 2
    pieces = []
    for k in range(0, n_row, 2):
        piece = swap(rounded, "row", k) if k else rounded
        pieces += [piece, swap(piece, "row", 1)]
    return join(pieces)


def plus(*terms):
    return sum((t.astype(F32) for t in terms[1:]), terms[0].astype(F32)).astype(BF16)


def finish(terms):
    n_col, bit = lax.axis_size("col"), 4
    while bit < n_col:
        mine = plus(*terms)
        half = mine.shape[0] // 2
        terms = mine[:half], swap(mine[half:], "col", bit)
        bit *= 2
    return terms


def hold(x):
    def kernel(x_ref, out_ref):
        out_ref[...] = x_ref[...]

    vmem = pl.BlockSpec(memory_space=pltpu.VMEM)
    return pl.pallas_call(
        kernel,
        out_shape=jax.ShapeDtypeStruct(x.shape, x.dtype),
        in_specs=[vmem],
        out_specs=vmem,
        compiler_params=pltpu.CompilerParams(vmem_limit_bytes=VMEM_LIMIT),
        cost_estimate=pl.CostEstimate(flops=COST, bytes_accessed=4 * x.size, transcendentals=0),
    )(x)


def local(features, tile_values, tile_index, tile_count, weight, cotangent):
    n_row, n_col = lax.axis_size("row"), lax.axis_size("col")
    starts = [sum(CHUNKS[:j]) for j in range(len(CHUNKS))]
    blocks, own, tiles, index, count = relay_chips(
        features[:, :CHUNKS[0]], features, tile_values[0, 0], tile_index[0, 0], tile_count[0, 0])
    numbers = slot_numbers(index, count, features.shape[0])
    tiles = stage(tiles)
    core = swap(own, "row", 1)
    keep, summed, pre = (), [], None
    for at, wide in zip(starts, CHUNKS):
        final = at + wide == features.shape[1]
        if at:
            early, *blocks = lax.optimization_barrier((features, *blocks))
            late, *keep = lax.optimization_barrier((features, *keep))
            blocks = gather_chips(early[:, at:at + wide], late[:, at:at + wide])
        pieces = [own, core]
        for block in blocks:
            pieces += [block, swap(block, "row", 1)]
        *keep, near, away = tile_products(numbers, tiles, pieces, at)
        if at:
            away, terms[0] = lax.optimization_barrier((away, hold(terms[0])))
        got = swap(away, "col", 1)
        send = plus(keep[1], got)
        if at:
            aggregated, pre = early_part(finish(terms), weight, done, pre)
            send, aggregated, pre = lax.optimization_barrier((send, aggregated, pre))
            summed.append(aggregated)
        if final:
            near, got = lax.optimization_barrier((near, got))
        cut = near.shape[0] // (2 if final else 1)
        arrived = [swap(near[i:i + cut], "col", 1) for i in range(0, near.shape[0], cut)]
        terms, done = [keep[0], swap(send, "col", 2), jnp.concatenate(arrived)], at
    scale = 1.0 / math.sqrt(cotangent.shape[0] * n_row * n_col)
    output, grad_keep, grad_send = vertex_step(weight, cotangent, pre, summed, finish(terms), scale)
    return output, reduce_gradient(grad_keep, grad_send)


def solution(mesh):
    placed = (
        P(("col", "row"), None),
        P("row", "col", None, None, None),
        P("row", "col", None),
        P("row", "col"),
        P(),
        P(("row", "col"), None),
    )
    return jax.shard_map(
        local, mesh=mesh, in_specs=placed, out_specs=(P(("row", "col"), None), P()), check_vma=False
    )
```

time: 95.6 us -> 92.6 us (0.969)
  waiting for transfers between devices: 53.2 us -> 47.3 us
  starting transfers between devices: 30.8 us -> 35.5 us
  local copies, waits for them, and re-layouts: 2.79 us -> 1.8 us
    ppermute x33 -> x37, waiting for transfers between devices: 53.2 us -> 47.3 us  [swap(): lax.ppermute(x, axis, [(i, i ^ mask) for i in range(lax.axis_size(axis))])]
    ppermute x33 -> x37, starting transfers between devices: 30.8 us -> 35.5 us  [swap(): lax.ppermute(x, axis, [(i, i ^ mask) for i in range(lax.axis_size(axis))])]
  transfers between devices with their start and end apart: 33 -> 37, of which waited for: 23 -> 24; matrix products, arithmetic and copies ran while one was open for 0% -> 0% of each run, Pallas kernels for 2% -> 4%
where the time goes in v3:
time: 92.6 us; the launch traced here: 92.4 us
  waiting for transfers between devices  47.3 us (51%)
  starting transfers between devices  35.5 us (38%)
  Pallas kernels  5.91 us (6%)
  local copies, waits for them, and re-layouts  1.8 us (2%)
  between operations  1.57 us (2%)
    ppermute x37, waiting for transfers between devices, swap(): lax.ppermute(x, axis, [(i, i ^ mask) for i in range(lax.axis_size(axis))])  47.3 us
    ppermute x37, starting transfers between devices, swap(): lax.ppermute(x, axis, [(i, i ^ mask) for i in range(lax.axis_size(axis))])  35.5 us
    pallas_call x2, Pallas kernels, tile_products(): pl.pallas_call(functools.partial(tiles_kernel, at=at, n_row=n_row, part=m...  3.08 us
  transfers between devices with their start and end apart: 37, of which 24 were waited for; matrix products, arithmetic and copies ran while one was open for 0% of the time, Pallas kernels for 4%

profile of v3, /device:TPU:0, one launch (start us, length us, event | category | flops | bytes accessed | tf_op | source)
XLA Modules:
  0.0 92.4 jit_solution(11046586182521497494)
XLA Ops:
  1.6 3.0 %collective-permute-start.1 = (bf16[256,256]{1,0:T(8,128)(2,1)S(1)}, bf16[256,256]{1,0:T(8,128)(2,1)S(1)}, u32[]{:S(2)}, u32[]{:S(2)}) collective-permute-start(bf16[256,256]{1,0:T(8,128)(2,1)S(1)} %get-tuple-element.58), channel_id=1, source_target_pairs={{0,16},{4,20},{8,24},{12,28},{16,0},{20,4},{24,8},{28,12},{1,17},{... | collective-permute-start | bytes 393224 | tf_op jit(solution)/shard_map/ppermute | solution.py:21
  6.8 1.8 %collective-permute-done.1 = bf16[256,256]{1,0:T(8,128)(2,1)S(1)} collective-permute-done((bf16[256,256]{1,0:T(8,128)(2,1)S(1)}, bf16[256,256]{1,0:T(8,128)(2,1)S(1)}, u32[]{:S(2)}, u32[]{:S(2)}) %collective-permute-start.1) | collective-permute-done | bytes 131104 | tf_op jit(solution)/shard_map/ppermute | solution.py:21
  8.6 2.4 %collective-permute-done = bf16[256,256]{1,0:T(8,128)(2,1)S(1)} collective-permute-done((bf16[256,256]{1,0:T(8,128)(2,1)S(1)}, bf16[256,256]{1,0:T(8,128)(2,1)S(1)}, u32[]{:S(2)}, u32[]{:S(2)}) %collective-permute-start) | collective-permute-done | bytes 131104 | tf_op jit(solution)/shard_map/ppermute | solution.py:21
  11.1 1.9 %collective-permute-start.6 = (bf16[256,256]{1,0:T(8,128)(2,1)S(1)}, bf16[256,256]{1,0:T(8,128)(2,1)S(1)}, u32[]{:S(2)}, u32[]{:S(2)}) collective-permute-start(bf16[256,256]{1,0:T(8,128)(2,1)S(1)} %collective-permute-done.1), channel_id=1, source_target_pairs={{0,8},{4,12},{8,0},{12,4},{16,24},{20,28},{24,16},{28,20},{1,9},{5... | collective-permute-start | bytes 393224 | tf_op jit(solution)/shard_map/ppermute | solution.py:21
  14.1 1.8 %collective-permute-done.5 = bf16[256,256]{1,0:T(8,128)(2,1)S(1)} collective-permute-done((bf16[256,256]{1,0:T(8,128)(2,1)S(1)}, bf16[256,256]{1,0:T(8,128)(2,1)S(1)}, u32[]{:S(2)}, u32[]{:S(2)}) %collective-permute-start.5) | collective-permute-done | bytes 131104 | tf_op jit(solution)/shard_map/ppermute | solution.py:21
  17.6 2.0 %collective-permute-start.9 = (bf16[512,256]{1,0:T(8,128)(2,1)S(1)}, bf16[512,256]{1,0:T(8,128)(2,1)S(1)}, u32[]{:S(2)}, u32[]{:S(2)}) collective-permute-start(bf16[512,256]{1,0:T(8,128)(2,1)S(1)} %slice.40), channel_id=1, source_target_pairs={{0,16},{4,20},{8,24},{12,28},{16,0},{20,4},{24,8},{28,12},{1,17},{... | collective-permute-start | bytes 786440 | tf_op jit(solution)/shard_map/ppermute | solution.py:21
  22.7 1.6 %collective-permute-start.17 = (bf16[512,256]{1,0:T(8,128)(2,1)S(1)}, bf16[512,256]{1,0:T(8,128)(2,1)S(1)}, u32[]{:S(2)}, u32[]{:S(2)}) collective-permute-start(bf16[512,256]{1,0:T(8,128)(2,1)S(1)} %get-tuple-element.43), channel_id=1, source_target_pairs={{0,1},{1,0},{2,3},{3,2},{4,5},{5,4},{6,7},{7,6},{8,9},{9,8},{10,11... | collective-permute-start | bytes 786440 | tf_op jit(solution)/shard_map/ppermute | solution.py:21
  24.5 2.1 %collective-permute-done.9.refs_4_ = bf16[512,256]{1,0:T(8,128)(2,1)S(1)} collective-permute-done((bf16[512,256]{1,0:T(8,128)(2,1)S(1)}, bf16[512,256]{1,0:T(8,128)(2,1)S(1)}, u32[]{:S(2)}, u32[]{:S(2)}) %collective-permute-start.9) | collective-permute-done | bytes 262176 | tf_op jit(solution)/shard_map/ppermute | solution.py:21
  26.6 2.2 %collective-permute-done.7.refs_2_ = bf16[512,256]{1,0:T(8,128)(2,1)S(1)} collective-permute-done((bf16[512,256]{1,0:T(8,128)(2,1)S(1)}, bf16[512,256]{1,0:T(8,128)(2,1)S(1)}, u32[]{:S(2)}, u32[]{:S(2)}) %collective-permute-start.7) | collective-permute-done | bytes 262176 | tf_op jit(solution)/shard_map/ppermute | solution.py:21
  31.0 2.7 %collective-permute-start.18 = (bf16[512,256]{1,0:T(8,128)(2,1)S(1)}, bf16[512,256]{1,0:T(8,128)(2,1)S(1)}, u32[]{:S(2)}, u32[]{:S(2)}) collective-permute-start(bf16[512,256]{1,0:T(8,128)(2,1)S(1)} %add_convert_fusion), channel_id=1, source_target_pairs={{0,2},{1,3},{2,0},{3,1},{4,6},{5,7},{6,4},{7,5},{8,10},{9,11},{10,... | collective-permute-start | bytes 786440 | tf_op jit(solution)/shard_map/ppermute | solution.py:21
  36.7 1.6 %collective-permute-start.16 = (bf16[512,256]{1,0:T(8,128)(2,1)S(1)}, bf16[512,256]{1,0:T(8,128)(2,1)S(1)}, u32[]{:S(2)}, u32[]{:S(2)}) collective-permute-start(bf16[512,256]{1,0:T(8,128)(2,1)S(1)} %get-tuple-element.41), channel_id=1, source_target_pairs={{0,1},{1,0},{2,3},{3,2},{4,5},{5,4},{6,7},{7,6},{8,9},{9,8},{10,11... | collective-permute-start | bytes 786440 | tf_op jit(solution)/shard_map/ppermute | solution.py:21
  38.4 4.9 %collective-permute-done.19.refs_2_ = bf16[512,256]{1,0:T(8,128)(2,1)S(1)} collective-permute-done((bf16[512,256]{1,0:T(8,128)(2,1)S(1)}, bf16[512,256]{1,0:T(8,128)(2,1)S(1)}, u32[]{:S(2)}, u32[]{:S(2)}) %collective-permute-start.19) | collective-permute-done | bytes 262176 | tf_op jit(solution)/shard_map/ppermute | solution.py:21
  43.3 2.2 %collective-permute-done.18.refs_1_ = bf16[512,256]{1,0:T(8,128)(2,1)S(1)} collective-permute-done((bf16[512,256]{1,0:T(8,128)(2,1)S(1)}, bf16[512,256]{1,0:T(8,128)(2,1)S(1)}, u32[]{:S(2)}, u32[]{:S(2)}) %collective-permute-start.18) | collective-permute-done | bytes 262176 | tf_op jit(solution)/shard_map/ppermute | solution.py:21
  45.7 3.0 %collective-permute-done.16 = bf16[512,256]{1,0:T(8,128)(2,1)S(1)} collective-permute-done((bf16[512,256]{1,0:T(8,128)(2,1)S(1)}, bf16[512,256]{1,0:T(8,128)(2,1)S(1)}, u32[]{:S(2)}, u32[]{:S(2)}) %collective-permute-start.16) | collective-permute-done | bytes 262176 | tf_op jit(solution)/shard_map/ppermute | solution.py:21
  48.8 2.7 %collective-permute-start.20 = (bf16[512,256]{1,0:T(8,128)(2,1)S(1)}, bf16[512,256]{1,0:T(8,128)(2,1)S(1)}, u32[]{:S(2)}, u32[]{:S(2)}) collective-permute-start(bf16[512,256]{1,0:T(8,128)(2,1)S(1)} %add_convert_fusion.1), channel_id=1, source_target_pairs={{0,2},{1,3},{2,0},{3,1},{4,6},{5,7},{6,4},{7,5},{8,10},{9,11},{10,... | collective-permute-start | bytes 786440 | tf_op jit(solution)/shard_map/ppermute | solution.py:21
  53.6 7.5 %collective-permute-done.21 = bf16[256,256]{1,0:T(8,128)(2,1)S(1)} collective-permute-done((bf16[256,256]{1,0:T(8,128)(2,1)S(1)}, bf16[256,256]{1,0:T(8,128)(2,1)S(1)}, u32[]{:S(2)}, u32[]{:S(2)}) %collective-permute-start.21) | collective-permute-done | bytes 131104 | tf_op jit(solution)/shard_map/ppermute | solution.py:21
  61.1 2.6 %collective-permute-done.22 = bf16[256,256]{1,0:T(8,128)(2,1)S(1)} collective-permute-done((bf16[256,256]{1,0:T(8,128)(2,1)S(1)}, bf16[256,256]{1,0:T(8,128)(2,1)S(1)}, u32[]{:S(2)}, u32[]{:S(2)}) %collective-permute-start.22) | collective-permute-done | bytes 131104 | tf_op jit(solution)/shard_map/ppermute | solution.py:21
  68.5 2.0 %collective-permute-start.25 = (bf16[64,512]{1,0:T(8,128)(2,1)S(1)}, bf16[64,512]{1,0:T(8,128)(2,1)S(1)}, u32[]{:S(2)}, u32[]{:S(2)}) collective-permute-start(bf16[64,512]{1,0:T(8,128)(2,1)S(1)} %get-tuple-element.62), channel_id=1, source_target_pairs={{0,16},{4,20},{8,24},{12,28},{16,0},{20,4},{24,8},{28,12},{1,17},{... | collective-permute-start | bytes 196616 | tf_op jit(solution)/shard_map/ppermute | solution.py:21
  71.6 2.0 %collective-permute-done.26 = bf16[64,512]{1,0:T(8,128)(2,1)S(1)} collective-permute-done((bf16[64,512]{1,0:T(8,128)(2,1)S(1)}, bf16[64,512]{1,0:T(8,128)(2,1)S(1)}, u32[]{:S(2)}, u32[]{:S(2)}) %collective-permute-start.26) | collective-permute-done | bytes 65568 | tf_op jit(solution)/shard_map/ppermute | solution.py:21
  73.9 3.2 %collective-permute-start.29 = (bf16[64,512]{1,0:T(8,128)(2,1)S(1)}, bf16[64,512]{1,0:T(8,128)(2,1)S(1)}, u32[]{:S(2)}, u32[]{:S(2)}) collective-permute-start(bf16[64,512]{1,0:T(8,128)(2,1)S(1)} %fusion.2), channel_id=1, source_target_pairs={{0,3},{1,2},{2,1},{3,0},{4,7},{5,6},{6,5},{7,4},{8,11},{9,10},{10,... | collective-permute-start | bytes 196616 | tf_op jit(solution)/shard_map/ppermute | solution.py:21
  78.4 1.8 %collective-permute-done.29 = bf16[64,512]{1,0:T(8,128)(2,1)S(1)} collective-permute-done((bf16[64,512]{1,0:T(8,128)(2,1)S(1)}, bf16[64,512]{1,0:T(8,128)(2,1)S(1)}, u32[]{:S(2)}, u32[]{:S(2)}) %collective-permute-start.29) | collective-permute-done | bytes 65568 | tf_op jit(solution)/shard_map/ppermute | solution.py:21
  80.2 2.1 %collective-permute-done.28 = bf16[64,512]{1,0:T(8,128)(2,1)S(1)} collective-permute-done((bf16[64,512]{1,0:T(8,128)(2,1)S(1)}, bf16[64,512]{1,0:T(8,128)(2,1)S(1)}, u32[]{:S(2)}, u32[]{:S(2)}) %collective-permute-start.28) | collective-permute-done | bytes 65568 | tf_op jit(solution)/shard_map/ppermute | solution.py:21
  82.3 2.7 %collective-permute-start.35 = (bf16[64,512]{1,0:T(8,128)(2,1)S(1)}, bf16[64,512]{1,0:T(8,128)(2,1)S(1)}, u32[]{:S(2)}, u32[]{:S(2)}) collective-permute-start(bf16[64,512]{1,0:T(8,128)(2,1)S(1)} %add_convert_fusion.2.refs_0_), channel_id=1, source_target_pairs={{0,24},{4,28},{8,16},{12,20},{16,8},{20,12},{24,0},{28,4},{1,25},{... | collective-permute-start | bytes 196616 | tf_op jit(solution)/shard_map/ppermute | solution.py:21
  85.9 1.7 %collective-permute-done.35.refs_6_ = bf16[64,512]{1,0:T(8,128)(2,1)S(1)} collective-permute-done((bf16[64,512]{1,0:T(8,128)(2,1)S(1)}, bf16[64,512]{1,0:T(8,128)(2,1)S(1)}, u32[]{:S(2)}, u32[]{:S(2)}) %collective-permute-start.35) | collective-permute-done | bytes 65568 | tf_op jit(solution)/shard_map/ppermute | solution.py:21
  (87 shorter events, 29.2 us)
Async XLA Ops:
  1.6 6.9 %collective-permute-start.1 = (bf16[256,256]{1,0:T(8,128)(2,1)S(1)}, bf16[256,256]{1,0:T(8,128)(2,1)S(1)}, u32[]{:S(2)}, u32[]{:S(2)}) collective-permute-start(bf16[256,256]{1,0:T(8,128)(2,1)S(1)} %get-tuple-element.58), channel_id=1, source_target_pairs={{0,16},{4,20},{8,24},{12,28},{16,0},{20,4},{24,8},{28,12},{1,17},{... | collective-permute-start | bytes 393224 | tf_op jit(solution)/shard_map/ppermute | solution.py:21
  4.7 6.3 %collective-permute-start = (bf16[256,256]{1,0:T(8,128)(2,1)S(1)}, bf16[256,256]{1,0:T(8,128)(2,1)S(1)}, u32[]{:S(2)}, u32[]{:S(2)}) collective-permute-start(bf16[256,256]{1,0:T(8,128)(2,1)S(1)} %get-tuple-element.59), channel_id=1, source_target_pairs={{0,8},{4,12},{8,0},{12,4},{16,24},{20,28},{24,16},{28,20},{1,9},{5... | collective-permute-start | bytes 393224 | tf_op jit(solution)/shard_map/ppermute | solution.py:21
  6.2 6.8 %collective-permute-start.4 = (bf16[256,256]{1,0:T(8,128)(2,1)S(1)}, bf16[256,256]{1,0:T(8,128)(2,1)S(1)}, u32[]{:S(2)}, u32[]{:S(2)}) collective-permute-start(bf16[256,256]{1,0:T(8,128)(2,1)S(1)} %get-tuple-element.59), channel_id=1, source_target_pairs={{0,16},{4,20},{8,24},{12,28},{16,0},{20,4},{24,8},{28,12},{1,17},{... | collective-permute-start | bytes 393224 | tf_op jit(solution)/shard_map/ppermute | solution.py:21
  6.7 6.9 %collective-permute-start.3 = (bf16[256,256]{1,0:T(8,128)(2,1)S(1)}, bf16[256,256]{1,0:T(8,128)(2,1)S(1)}, u32[]{:S(2)}, u32[]{:S(2)}) collective-permute-start(bf16[256,256]{1,0:T(8,128)(2,1)S(1)} %get-tuple-element.58), channel_id=1, source_target_pairs={{0,8},{4,12},{8,0},{12,4},{16,24},{20,28},{24,16},{28,20},{1,9},{5... | collective-permute-start | bytes 393224 | tf_op jit(solution)/shard_map/ppermute | solution.py:21
  13.0 8.1 %collective-permute-start.2 = (bf16[512,512]{1,0:T(8,128)(2,1)S(1)}, bf16[512,512]{1,0:T(8,128)(2,1)S(1)}, u32[]{:S(2)}, u32[]{:S(2)}) collective-permute-start(bf16[512,512]{1,0:T(8,128)(2,1)S(1)} %copy-done), channel_id=1, source_target_pairs={{0,4},{4,0},{8,12},{12,8},{16,20},{20,16},{24,28},{28,24},{1,5},{5... | collective-permute-start | bytes 1572872 | tf_op jit(solution)/shard_map/ppermute | solution.py:21
  13.6 6.1 %collective-permute-start.11 = (bf16[512,256]{1,0:T(8,128)(2,1)S(1)}, bf16[512,256]{1,0:T(8,128)(2,1)S(1)}, u32[]{:S(2)}, u32[]{:S(2)}) collective-permute-start(bf16[512,256]{1,0:T(8,128)(2,1)S(1)} %constant_dynamic-update-slice_fusion.refs_2_), channel_id=1, source_target_pairs={{0,4},{4,0},{8,12},{12,8},{16,20},{20,16},{24,28},{28,24},{1,5},{5... | collective-permute-start | bytes 786440 | tf_op jit(solution)/shard_map/ppermute | solution.py:21
  13.7 7.5 %collective-permute-start.12 = (bf16[512,256]{1,0:T(8,128)(2,1)S(1)}, bf16[512,256]{1,0:T(8,128)(2,1)S(1)}, u32[]{:S(2)}, u32[]{:S(2)}) collective-permute-start(bf16[512,256]{1,0:T(8,128)(2,1)S(1)} %constant_dynamic-update-slice_fusion.2.refs_4_), channel_id=1, source_target_pairs={{0,4},{4,0},{8,12},{12,8},{16,20},{20,16},{24,28},{28,24},{1,5},{5... | collective-permute-start | bytes 786440 | tf_op jit(solution)/shard_map/ppermute | solution.py:21
  17.6 9.0 %collective-permute-start.9 = (bf16[512,256]{1,0:T(8,128)(2,1)S(1)}, bf16[512,256]{1,0:T(8,128)(2,1)S(1)}, u32[]{:S(2)}, u32[]{:S(2)}) collective-permute-start(bf16[512,256]{1,0:T(8,128)(2,1)S(1)} %slice.40), channel_id=1, source_target_pairs={{0,16},{4,20},{8,24},{12,28},{16,0},{20,4},{24,8},{28,12},{1,17},{... | collective-permute-start | bytes 786440 | tf_op jit(solution)/shard_map/ppermute | solution.py:21
  19.6 9.1 %collective-permute-start.7 = (bf16[512,256]{1,0:T(8,128)(2,1)S(1)}, bf16[512,256]{1,0:T(8,128)(2,1)S(1)}, u32[]{:S(2)}, u32[]{:S(2)}) collective-permute-start(bf16[512,256]{1,0:T(8,128)(2,1)S(1)} %slice.40), channel_id=1, source_target_pairs={{0,8},{4,12},{8,0},{12,4},{16,24},{20,28},{24,16},{28,20},{1,9},{5... | collective-permute-start | bytes 786440 | tf_op jit(solution)/shard_map/ppermute | solution.py:21
  22.7 8.2 %collective-permute-start.17 = (bf16[512,256]{1,0:T(8,128)(2,1)S(1)}, bf16[512,256]{1,0:T(8,128)(2,1)S(1)}, u32[]{:S(2)}, u32[]{:S(2)}) collective-permute-start(bf16[512,256]{1,0:T(8,128)(2,1)S(1)} %get-tuple-element.43), channel_id=1, source_target_pairs={{0,1},{1,0},{2,3},{3,2},{4,5},{5,4},{6,7},{7,6},{8,9},{9,8},{10,11... | collective-permute-start | bytes 786440 | tf_op jit(solution)/shard_map/ppermute | solution.py:21
  24.4 9.3 %collective-permute-start.14 = (bf16[512,256]{1,0:T(8,128)(2,1)S(1)}, bf16[512,256]{1,0:T(8,128)(2,1)S(1)}, u32[]{:S(2)}, u32[]{:S(2)}) collective-permute-start(bf16[512,256]{1,0:T(8,128)(2,1)S(1)} %slice.41), channel_id=1, source_target_pairs={{0,24},{4,28},{8,16},{12,20},{16,8},{20,12},{24,0},{28,4},{1,25},{... | collective-permute-start | bytes 786440 | tf_op jit(solution)/shard_map/ppermute | solution.py:21
  26.6 7.1 %collective-permute-start.10 = (bf16[512,256]{1,0:T(8,128)(2,1)S(1)}, bf16[512,256]{1,0:T(8,128)(2,1)S(1)}, u32[]{:S(2)}, u32[]{:S(2)}) collective-permute-start(bf16[512,256]{1,0:T(8,128)(2,1)S(1)} %collective-permute-done.9.refs_4_), channel_id=1, source_target_pairs={{0,4},{4,0},{8,12},{12,8},{16,20},{20,16},{24,28},{28,24},{1,5},{5... | collective-permute-start | bytes 786440 | tf_op jit(solution)/shard_map/ppermute | solution.py:21
  28.8 14.5 %collective-permute-start.19 = (bf16[512,256]{1,0:T(8,128)(2,1)S(1)}, bf16[512,256]{1,0:T(8,128)(2,1)S(1)}, u32[]{:S(2)}, u32[]{:S(2)}) collective-permute-start(bf16[512,256]{1,0:T(8,128)(2,1)S(1)} %get-tuple-element.44), channel_id=1, source_target_pairs={{0,1},{1,0},{2,3},{3,2},{4,5},{5,4},{6,7},{7,6},{8,9},{9,8},{10,11... | collective-permute-start | bytes 786440 | tf_op jit(solution)/shard_map/ppermute | solution.py:21
  31.0 14.4 %collective-permute-start.18 = (bf16[512,256]{1,0:T(8,128)(2,1)S(1)}, bf16[512,256]{1,0:T(8,128)(2,1)S(1)}, u32[]{:S(2)}, u32[]{:S(2)}) collective-permute-start(bf16[512,256]{1,0:T(8,128)(2,1)S(1)} %add_convert_fusion), channel_id=1, source_target_pairs={{0,2},{1,3},{2,0},{3,1},{4,6},{5,7},{6,4},{7,5},{8,10},{9,11},{10,... | collective-permute-start | bytes 786440 | tf_op jit(solution)/shard_map/ppermute | solution.py:21
  36.7 12.0 %collective-permute-start.16 = (bf16[512,256]{1,0:T(8,128)(2,1)S(1)}, bf16[512,256]{1,0:T(8,128)(2,1)S(1)}, u32[]{:S(2)}, u32[]{:S(2)}) collective-permute-start(bf16[512,256]{1,0:T(8,128)(2,1)S(1)} %get-tuple-element.41), channel_id=1, source_target_pairs={{0,1},{1,0},{2,3},{3,2},{4,5},{5,4},{6,7},{7,6},{8,9},{9,8},{10,11... | collective-permute-start | bytes 786440 | tf_op jit(solution)/shard_map/ppermute | solution.py:21
  48.8 14.9 %collective-permute-start.20 = (bf16[512,256]{1,0:T(8,128)(2,1)S(1)}, bf16[512,256]{1,0:T(8,128)(2,1)S(1)}, u32[]{:S(2)}, u32[]{:S(2)}) collective-permute-start(bf16[512,256]{1,0:T(8,128)(2,1)S(1)} %add_convert_fusion.1), channel_id=1, source_target_pairs={{0,2},{1,3},{2,0},{3,1},{4,6},{5,7},{6,4},{7,5},{8,10},{9,11},{10,... | collective-permute-start | bytes 786440 | tf_op jit(solution)/shard_map/ppermute | solution.py:21
  51.5 9.6 %collective-permute-start.21 = (bf16[256,256]{1,0:T(8,128)(2,1)S(1)}, bf16[256,256]{1,0:T(8,128)(2,1)S(1)}, u32[]{:S(2)}, u32[]{:S(2)}) collective-permute-start(bf16[256,256]{1,0:T(8,128)(2,1)S(1)} %get-tuple-element.63), channel_id=1, source_target_pairs={{0,1},{1,0},{2,3},{3,2},{4,5},{5,4},{6,7},{7,6},{8,9},{9,8},{10,11... | collective-permute-start | bytes 393224 | tf_op jit(solution)/shard_map/ppermute | solution.py:21
  53.1 10.6 %collective-permute-start.22 = (bf16[256,256]{1,0:T(8,128)(2,1)S(1)}, bf16[256,256]{1,0:T(8,128)(2,1)S(1)}, u32[]{:S(2)}, u32[]{:S(2)}) collective-permute-start(bf16[256,256]{1,0:T(8,128)(2,1)S(1)} %get-tuple-element.64), channel_id=1, source_target_pairs={{0,1},{1,0},{2,3},{3,2},{4,5},{5,4},{6,7},{7,6},{8,9},{9,8},{10,11... | collective-permute-start | bytes 393224 | tf_op jit(solution)/shard_map/ppermute | solution.py:21
  68.5 5.2 %collective-permute-start.26 = (bf16[64,512]{1,0:T(8,128)(2,1)S(1)}, bf16[64,512]{1,0:T(8,128)(2,1)S(1)}, u32[]{:S(2)}, u32[]{:S(2)}) collective-permute-start(bf16[64,512]{1,0:T(8,128)(2,1)S(1)} %get-tuple-element.61), channel_id=1, source_target_pairs={{0,24},{4,28},{8,16},{12,20},{16,8},{20,12},{24,0},{28,4},{1,25},{... | collective-permute-start | bytes 196616 | tf_op jit(solution)/shard_map/ppermute | solution.py:21
  68.5 5.5 %collective-permute-start.25 = (bf16[64,512]{1,0:T(8,128)(2,1)S(1)}, bf16[64,512]{1,0:T(8,128)(2,1)S(1)}, u32[]{:S(2)}, u32[]{:S(2)}) collective-permute-start(bf16[64,512]{1,0:T(8,128)(2,1)S(1)} %get-tuple-element.62), channel_id=1, source_target_pairs={{0,16},{4,20},{8,24},{12,28},{16,0},{20,4},{24,8},{28,12},{1,17},{... | collective-permute-start | bytes 196616 | tf_op jit(solution)/shard_map/ppermute | solution.py:21
  73.9 6.3 %collective-permute-start.29 = (bf16[64,512]{1,0:T(8,128)(2,1)S(1)}, bf16[64,512]{1,0:T(8,128)(2,1)S(1)}, u32[]{:S(2)}, u32[]{:S(2)}) collective-permute-start(bf16[64,512]{1,0:T(8,128)(2,1)S(1)} %fusion.2), channel_id=1, source_target_pairs={{0,3},{1,2},{2,1},{3,0},{4,7},{5,6},{6,5},{7,4},{8,11},{9,10},{10,... | collective-permute-start | bytes 196616 | tf_op jit(solution)/shard_map/ppermute | solution.py:21
  77.1 5.2 %collective-permute-start.28 = (bf16[64,512]{1,0:T(8,128)(2,1)S(1)}, bf16[64,512]{1,0:T(8,128)(2,1)S(1)}, u32[]{:S(2)}, u32[]{:S(2)}) collective-permute-start(bf16[64,512]{1,0:T(8,128)(2,1)S(1)} %fusion.2), channel_id=1, source_target_pairs={{0,2},{1,3},{2,0},{3,1},{4,6},{5,7},{6,4},{7,5},{8,10},{9,11},{10,... | collective-permute-start | bytes 196616 | tf_op jit(solution)/shard_map/ppermute | solution.py:21
  77.1 5.2 %collective-permute-start.27 = (bf16[64,512]{1,0:T(8,128)(2,1)S(1)}, bf16[64,512]{1,0:T(8,128)(2,1)S(1)}, u32[]{:S(2)}, u32[]{:S(2)}) collective-permute-start(bf16[64,512]{1,0:T(8,128)(2,1)S(1)} %fusion.2), channel_id=1, source_target_pairs={{0,1},{1,0},{2,3},{3,2},{4,5},{5,4},{6,7},{7,6},{8,9},{9,8},{10,11... | collective-permute-start | bytes 196616 | tf_op jit(solution)/shard_map/ppermute | solution.py:21
  82.3 5.3 %collective-permute-start.35 = (bf16[64,512]{1,0:T(8,128)(2,1)S(1)}, bf16[64,512]{1,0:T(8,128)(2,1)S(1)}, u32[]{:S(2)}, u32[]{:S(2)}) collective-permute-start(bf16[64,512]{1,0:T(8,128)(2,1)S(1)} %add_convert_fusion.2.refs_0_), channel_id=1, source_target_pairs={{0,24},{4,28},{8,16},{12,20},{16,8},{20,12},{24,0},{28,4},{1,25},{... | collective-permute-start | bytes 196616 | tf_op jit(solution)/shard_map/ppermute | solution.py:21
  (18 other events, 90.0 us)

commit v4 on v3

--- a/solution.py
+++ b/solution.py
@@ -311,8 +311,7 @@
             aggregated, pre = early_part(finish(terms), weight, done, pre)
             send, aggregated, pre = lax.optimization_barrier((send, aggregated, pre))
             summed.append(aggregated)
-        if final:
-            near, got = lax.optimization_barrier((near, got))
+        near, got = lax.optimization_barrier((near, got))
         cut = near.shape[0] // (2 if final else 1)
         arrived = [swap(near[i:i + cut], "col", 1) for i in range(0, near.shape[0], cut)]
         terms, done = [keep[0], swap(send, "col", 2), jnp.concatenate(arrived)], at

time: 92.6 us -> 91.3 us (0.986)
  starting transfers between devices: 35.5 us -> 34.4 us
    ppermute x37, starting transfers between devices: 35.5 us -> 34.4 us  [swap(): lax.ppermute(x, axis, [(i, i ^ mask) for i in range(lax.axis_size(axis))])]
where the time goes in v4:
time: 91.3 us; the launch traced here: 91.1 us
  waiting for transfers between devices  47 us (51%)
  starting transfers between devices  34.4 us (38%)
  Pallas kernels  5.92 us (6%)
  local copies, waits for them, and re-layouts  1.8 us (2%)
  between operations  1.57 us (2%)
    ppermute x37, waiting for transfers between devices, swap(): lax.ppermute(x, axis, [(i, i ^ mask) for i in range(lax.axis_size(axis))])  47 us
    ppermute x37, starting transfers between devices, swap(): lax.ppermute(x, axis, [(i, i ^ mask) for i in range(lax.axis_size(axis))])  34.4 us
    pallas_call x2, Pallas kernels, tile_products(): pl.pallas_call(functools.partial(tiles_kernel, at=at, n_row=n_row, part=m...  3.08 us
  transfers between devices with their start and end apart: 37, of which 24 were waited for; matrix products, arithmetic and copies ran while one was open for 0% of the time, Pallas kernels for 4%

profile of v4, /device:TPU:0, one launch (start us, length us, event | category | flops | bytes accessed | tf_op | source)
XLA Modules:
  0.0 91.1 jit_solution(14974512520865645111)
XLA Ops:
  1.6 3.0 %collective-permute-start.1 = (bf16[256,256]{1,0:T(8,128)(2,1)S(1)}, bf16[256,256]{1,0:T(8,128)(2,1)S(1)}, u32[]{:S(2)}, u32[]{:S(2)}) collective-permute-start(bf16[256,256]{1,0:T(8,128)(2,1)S(1)} %get-tuple-element.60), channel_id=1, source_target_pairs={{0,16},{4,20},{8,24},{12,28},{16,0},{20,4},{24,8},{28,12},{1,17},{... | collective-permute-start | bytes 393224 | tf_op jit(solution)/shard_map/ppermute | solution.py:21
  6.8 1.8 %collective-permute-done.1 = bf16[256,256]{1,0:T(8,128)(2,1)S(1)} collective-permute-done((bf16[256,256]{1,0:T(8,128)(2,1)S(1)}, bf16[256,256]{1,0:T(8,128)(2,1)S(1)}, u32[]{:S(2)}, u32[]{:S(2)}) %collective-permute-start.1) | collective-permute-done | bytes 131104 | tf_op jit(solution)/shard_map/ppermute | solution.py:21
  8.6 2.4 %collective-permute-done = bf16[256,256]{1,0:T(8,128)(2,1)S(1)} collective-permute-done((bf16[256,256]{1,0:T(8,128)(2,1)S(1)}, bf16[256,256]{1,0:T(8,128)(2,1)S(1)}, u32[]{:S(2)}, u32[]{:S(2)}) %collective-permute-start) | collective-permute-done | bytes 131104 | tf_op jit(solution)/shard_map/ppermute | solution.py:21
  11.1 1.9 %collective-permute-start.6 = (bf16[256,256]{1,0:T(8,128)(2,1)S(1)}, bf16[256,256]{1,0:T(8,128)(2,1)S(1)}, u32[]{:S(2)}, u32[]{:S(2)}) collective-permute-start(bf16[256,256]{1,0:T(8,128)(2,1)S(1)} %collective-permute-done.1), channel_id=1, source_target_pairs={{0,8},{4,12},{8,0},{12,4},{16,24},{20,28},{24,16},{28,20},{1,9},{5... | collective-permute-start | bytes 393224 | tf_op jit(solution)/shard_map/ppermute | solution.py:21
  14.1 1.8 %collective-permute-done.5 = bf16[256,256]{1,0:T(8,128)(2,1)S(1)} collective-permute-done((bf16[256,256]{1,0:T(8,128)(2,1)S(1)}, bf16[256,256]{1,0:T(8,128)(2,1)S(1)}, u32[]{:S(2)}, u32[]{:S(2)}) %collective-permute-start.5) | collective-permute-done | bytes 131104 | tf_op jit(solution)/shard_map/ppermute | solution.py:21
  17.6 2.0 %collective-permute-start.9 = (bf16[512,256]{1,0:T(8,128)(2,1)S(1)}, bf16[512,256]{1,0:T(8,128)(2,1)S(1)}, u32[]{:S(2)}, u32[]{:S(2)}) collective-permute-start(bf16[512,256]{1,0:T(8,128)(2,1)S(1)} %slice.40), channel_id=1, source_target_pairs={{0,16},{4,20},{8,24},{12,28},{16,0},{20,4},{24,8},{28,12},{1,17},{... | collective-permute-start | bytes 786440 | tf_op jit(solution)/shard_map/ppermute | solution.py:21
  22.7 1.6 %collective-permute-start.17 = (bf16[512,256]{1,0:T(8,128)(2,1)S(1)}, bf16[512,256]{1,0:T(8,128)(2,1)S(1)}, u32[]{:S(2)}, u32[]{:S(2)}) collective-permute-start(bf16[512,256]{1,0:T(8,128)(2,1)S(1)} %get-tuple-element.44), channel_id=1, source_target_pairs={{0,1},{1,0},{2,3},{3,2},{4,5},{5,4},{6,7},{7,6},{8,9},{9,8},{10,11... | collective-permute-start | bytes 786440 | tf_op jit(solution)/shard_map/ppermute | solution.py:21
  24.5 2.1 %collective-permute-done.9.refs_4_ = bf16[512,256]{1,0:T(8,128)(2,1)S(1)} collective-permute-done((bf16[512,256]{1,0:T(8,128)(2,1)S(1)}, bf16[512,256]{1,0:T(8,128)(2,1)S(1)}, u32[]{:S(2)}, u32[]{:S(2)}) %collective-permute-start.9) | collective-permute-done | bytes 262176 | tf_op jit(solution)/shard_map/ppermute | solution.py:21
  26.6 2.2 %collective-permute-done.7.refs_2_ = bf16[512,256]{1,0:T(8,128)(2,1)S(1)} collective-permute-done((bf16[512,256]{1,0:T(8,128)(2,1)S(1)}, bf16[512,256]{1,0:T(8,128)(2,1)S(1)}, u32[]{:S(2)}, u32[]{:S(2)}) %collective-permute-start.7) | collective-permute-done | bytes 262176 | tf_op jit(solution)/shard_map/ppermute | solution.py:21
  28.8 2.1 %collective-permute-done.17 = bf16[512,256]{1,0:T(8,128)(2,1)S(1)} collective-permute-done((bf16[512,256]{1,0:T(8,128)(2,1)S(1)}, bf16[512,256]{1,0:T(8,128)(2,1)S(1)}, u32[]{:S(2)}, u32[]{:S(2)}) %collective-permute-start.17) | collective-permute-done | bytes 262176 | tf_op jit(solution)/shard_map/ppermute | solution.py:21
  30.9 1.6 %collective-permute-start.19 = (bf16[512,256]{1,0:T(8,128)(2,1)S(1)}, bf16[512,256]{1,0:T(8,128)(2,1)S(1)}, u32[]{:S(2)}, u32[]{:S(2)}) collective-permute-start(bf16[512,256]{1,0:T(8,128)(2,1)S(1)} %get-tuple-element.46), channel_id=1, source_target_pairs={{0,1},{1,0},{2,3},{3,2},{4,5},{5,4},{6,7},{7,6},{8,9},{9,8},{10,11... | collective-permute-start | bytes 786440 | tf_op jit(solution)/shard_map/ppermute | solution.py:21
  32.6 2.7 %collective-permute-start.18 = (bf16[512,256]{1,0:T(8,128)(2,1)S(1)}, bf16[512,256]{1,0:T(8,128)(2,1)S(1)}, u32[]{:S(2)}, u32[]{:S(2)}) collective-permute-start(bf16[512,256]{1,0:T(8,128)(2,1)S(1)} %add_convert_fusion), channel_id=1, source_target_pairs={{0,2},{1,3},{2,0},{3,1},{4,6},{5,7},{6,4},{7,5},{8,10},{9,11},{10,... | collective-permute-start | bytes 786440 | tf_op jit(solution)/shard_map/ppermute | solution.py:21
  38.8 6.8 %collective-permute-done.19.refs_2_ = bf16[512,256]{1,0:T(8,128)(2,1)S(1)} collective-permute-done((bf16[512,256]{1,0:T(8,128)(2,1)S(1)}, bf16[512,256]{1,0:T(8,128)(2,1)S(1)}, u32[]{:S(2)}, u32[]{:S(2)}) %collective-permute-start.19) | collective-permute-done | bytes 262176 | tf_op jit(solution)/shard_map/ppermute | solution.py:21
  45.9 3.5 %collective-permute-done.16 = bf16[512,256]{1,0:T(8,128)(2,1)S(1)} collective-permute-done((bf16[512,256]{1,0:T(8,128)(2,1)S(1)}, bf16[512,256]{1,0:T(8,128)(2,1)S(1)}, u32[]{:S(2)}, u32[]{:S(2)}) %collective-permute-start.16) | collective-permute-done | bytes 262176 | tf_op jit(solution)/shard_map/ppermute | solution.py:21
  49.5 2.7 %collective-permute-start.20 = (bf16[512,256]{1,0:T(8,128)(2,1)S(1)}, bf16[512,256]{1,0:T(8,128)(2,1)S(1)}, u32[]{:S(2)}, u32[]{:S(2)}) collective-permute-start(bf16[512,256]{1,0:T(8,128)(2,1)S(1)} %add_convert_fusion.1), channel_id=1, source_target_pairs={{0,2},{1,3},{2,0},{3,1},{4,6},{5,7},{6,4},{7,5},{8,10},{9,11},{10,... | collective-permute-start | bytes 786440 | tf_op jit(solution)/shard_map/ppermute | solution.py:21
  52.3 1.6 %collective-permute-start.21 = (bf16[256,256]{1,0:T(8,128)(2,1)S(1)}, bf16[256,256]{1,0:T(8,128)(2,1)S(1)}, u32[]{:S(2)}, u32[]{:S(2)}) collective-permute-start(bf16[256,256]{1,0:T(8,128)(2,1)S(1)} %get-tuple-element.65), channel_id=1, source_target_pairs={{0,1},{1,0},{2,3},{3,2},{4,5},{5,4},{6,7},{7,6},{8,9},{9,8},{10,11... | collective-permute-start | bytes 393224 | tf_op jit(solution)/shard_map/ppermute | solution.py:21
  54.4 6.0 %collective-permute-done.21 = bf16[256,256]{1,0:T(8,128)(2,1)S(1)} collective-permute-done((bf16[256,256]{1,0:T(8,128)(2,1)S(1)}, bf16[256,256]{1,0:T(8,128)(2,1)S(1)}, u32[]{:S(2)}, u32[]{:S(2)}) %collective-permute-start.21) | collective-permute-done | bytes 131104 | tf_op jit(solution)/shard_map/ppermute | solution.py:21
  60.4 2.6 %collective-permute-done.22 = bf16[256,256]{1,0:T(8,128)(2,1)S(1)} collective-permute-done((bf16[256,256]{1,0:T(8,128)(2,1)S(1)}, bf16[256,256]{1,0:T(8,128)(2,1)S(1)}, u32[]{:S(2)}, u32[]{:S(2)}) %collective-permute-start.22) | collective-permute-done | bytes 131104 | tf_op jit(solution)/shard_map/ppermute | solution.py:21
  68.1 1.6 %collective-permute-start.25 = (bf16[64,512]{1,0:T(8,128)(2,1)S(1)}, bf16[64,512]{1,0:T(8,128)(2,1)S(1)}, u32[]{:S(2)}, u32[]{:S(2)}) collective-permute-start(bf16[64,512]{1,0:T(8,128)(2,1)S(1)} %get-tuple-element.64), channel_id=1, source_target_pairs={{0,16},{4,20},{8,24},{12,28},{16,0},{20,4},{24,8},{28,12},{1,17},{... | collective-permute-start | bytes 196616 | tf_op jit(solution)/shard_map/ppermute | solution.py:21
  73.2 3.0 %collective-permute-start.29 = (bf16[64,512]{1,0:T(8,128)(2,1)S(1)}, bf16[64,512]{1,0:T(8,128)(2,1)S(1)}, u32[]{:S(2)}, u32[]{:S(2)}) collective-permute-start(bf16[64,512]{1,0:T(8,128)(2,1)S(1)} %fusion.2), channel_id=1, source_target_pairs={{0,3},{1,2},{2,1},{3,0},{4,7},{5,6},{6,5},{7,4},{8,11},{9,10},{10,... | collective-permute-start | bytes 196616 | tf_op jit(solution)/shard_map/ppermute | solution.py:21
  77.6 2.0 %collective-permute-done.29 = bf16[64,512]{1,0:T(8,128)(2,1)S(1)} collective-permute-done((bf16[64,512]{1,0:T(8,128)(2,1)S(1)}, bf16[64,512]{1,0:T(8,128)(2,1)S(1)}, u32[]{:S(2)}, u32[]{:S(2)}) %collective-permute-start.29) | collective-permute-done | bytes 65568 | tf_op jit(solution)/shard_map/ppermute | solution.py:21
  79.6 2.4 %collective-permute-done.28 = bf16[64,512]{1,0:T(8,128)(2,1)S(1)} collective-permute-done((bf16[64,512]{1,0:T(8,128)(2,1)S(1)}, bf16[64,512]{1,0:T(8,128)(2,1)S(1)}, u32[]{:S(2)}, u32[]{:S(2)}) %collective-permute-start.28) | collective-permute-done | bytes 65568 | tf_op jit(solution)/shard_map/ppermute | solution.py:21
  82.1 1.6 %collective-permute-start.35 = (bf16[64,512]{1,0:T(8,128)(2,1)S(1)}, bf16[64,512]{1,0:T(8,128)(2,1)S(1)}, u32[]{:S(2)}, u32[]{:S(2)}) collective-permute-start(bf16[64,512]{1,0:T(8,128)(2,1)S(1)} %add_convert_fusion.2.refs_0_), channel_id=1, source_target_pairs={{0,24},{4,28},{8,16},{12,20},{16,8},{20,12},{24,0},{28,4},{1,25},{... | collective-permute-start | bytes 196616 | tf_op jit(solution)/shard_map/ppermute | solution.py:21
  85.6 2.3 %collective-permute-done.35.refs_6_ = bf16[64,512]{1,0:T(8,128)(2,1)S(1)} collective-permute-done((bf16[64,512]{1,0:T(8,128)(2,1)S(1)}, bf16[64,512]{1,0:T(8,128)(2,1)S(1)}, u32[]{:S(2)}, u32[]{:S(2)}) %collective-permute-start.35) | collective-permute-done | bytes 65568 | tf_op jit(solution)/shard_map/ppermute | solution.py:21
  (87 shorter events, 28.0 us)
Async XLA Ops:
  1.6 6.9 %collective-permute-start.1 = (bf16[256,256]{1,0:T(8,128)(2,1)S(1)}, bf16[256,256]{1,0:T(8,128)(2,1)S(1)}, u32[]{:S(2)}, u32[]{:S(2)}) collective-permute-start(bf16[256,256]{1,0:T(8,128)(2,1)S(1)} %get-tuple-element.60), channel_id=1, source_target_pairs={{0,16},{4,20},{8,24},{12,28},{16,0},{20,4},{24,8},{28,12},{1,17},{... | collective-permute-start | bytes 393224 | tf_op jit(solution)/shard_map/ppermute | solution.py:21
  4.7 6.3 %collective-permute-start = (bf16[256,256]{1,0:T(8,128)(2,1)S(1)}, bf16[256,256]{1,0:T(8,128)(2,1)S(1)}, u32[]{:S(2)}, u32[]{:S(2)}) collective-permute-start(bf16[256,256]{1,0:T(8,128)(2,1)S(1)} %get-tuple-element.61), channel_id=1, source_target_pairs={{0,8},{4,12},{8,0},{12,4},{16,24},{20,28},{24,16},{28,20},{1,9},{5... | collective-permute-start | bytes 393224 | tf_op jit(solution)/shard_map/ppermute | solution.py:21
  6.2 6.8 %collective-permute-start.4 = (bf16[256,256]{1,0:T(8,128)(2,1)S(1)}, bf16[256,256]{1,0:T(8,128)(2,1)S(1)}, u32[]{:S(2)}, u32[]{:S(2)}) collective-permute-start(bf16[256,256]{1,0:T(8,128)(2,1)S(1)} %get-tuple-element.61), channel_id=1, source_target_pairs={{0,16},{4,20},{8,24},{12,28},{16,0},{20,4},{24,8},{28,12},{1,17},{... | collective-permute-start | bytes 393224 | tf_op jit(solution)/shard_map/ppermute | solution.py:21
  6.7 6.9 %collective-permute-start.3 = (bf16[256,256]{1,0:T(8,128)(2,1)S(1)}, bf16[256,256]{1,0:T(8,128)(2,1)S(1)}, u32[]{:S(2)}, u32[]{:S(2)}) collective-permute-start(bf16[256,256]{1,0:T(8,128)(2,1)S(1)} %get-tuple-element.60), channel_id=1, source_target_pairs={{0,8},{4,12},{8,0},{12,4},{16,24},{20,28},{24,16},{28,20},{1,9},{5... | collective-permute-start | bytes 393224 | tf_op jit(solution)/shard_map/ppermute | solution.py:21
  13.0 8.1 %collective-permute-start.2 = (bf16[512,512]{1,0:T(8,128)(2,1)S(1)}, bf16[512,512]{1,0:T(8,128)(2,1)S(1)}, u32[]{:S(2)}, u32[]{:S(2)}) collective-permute-start(bf16[512,512]{1,0:T(8,128)(2,1)S(1)} %copy-done), channel_id=1, source_target_pairs={{0,4},{4,0},{8,12},{12,8},{16,20},{20,16},{24,28},{28,24},{1,5},{5... | collective-permute-start | bytes 1572872 | tf_op jit(solution)/shard_map/ppermute | solution.py:21
  13.6 6.1 %collective-permute-start.11 = (bf16[512,256]{1,0:T(8,128)(2,1)S(1)}, bf16[512,256]{1,0:T(8,128)(2,1)S(1)}, u32[]{:S(2)}, u32[]{:S(2)}) collective-permute-start(bf16[512,256]{1,0:T(8,128)(2,1)S(1)} %constant_dynamic-update-slice_fusion.refs_2_), channel_id=1, source_target_pairs={{0,4},{4,0},{8,12},{12,8},{16,20},{20,16},{24,28},{28,24},{1,5},{5... | collective-permute-start | bytes 786440 | tf_op jit(solution)/shard_map/ppermute | solution.py:21
  13.7 7.5 %collective-permute-start.12 = (bf16[512,256]{1,0:T(8,128)(2,1)S(1)}, bf16[512,256]{1,0:T(8,128)(2,1)S(1)}, u32[]{:S(2)}, u32[]{:S(2)}) collective-permute-start(bf16[512,256]{1,0:T(8,128)(2,1)S(1)} %constant_dynamic-update-slice_fusion.2.refs_4_), channel_id=1, source_target_pairs={{0,4},{4,0},{8,12},{12,8},{16,20},{20,16},{24,28},{28,24},{1,5},{5... | collective-permute-start | bytes 786440 | tf_op jit(solution)/shard_map/ppermute | solution.py:21
  17.6 9.0 %collective-permute-start.9 = (bf16[512,256]{1,0:T(8,128)(2,1)S(1)}, bf16[512,256]{1,0:T(8,128)(2,1)S(1)}, u32[]{:S(2)}, u32[]{:S(2)}) collective-permute-start(bf16[512,256]{1,0:T(8,128)(2,1)S(1)} %slice.40), channel_id=1, source_target_pairs={{0,16},{4,20},{8,24},{12,28},{16,0},{20,4},{24,8},{28,12},{1,17},{... | collective-permute-start | bytes 786440 | tf_op jit(solution)/shard_map/ppermute | solution.py:21
  19.6 9.1 %collective-permute-start.7 = (bf16[512,256]{1,0:T(8,128)(2,1)S(1)}, bf16[512,256]{1,0:T(8,128)(2,1)S(1)}, u32[]{:S(2)}, u32[]{:S(2)}) collective-permute-start(bf16[512,256]{1,0:T(8,128)(2,1)S(1)} %slice.40), channel_id=1, source_target_pairs={{0,8},{4,12},{8,0},{12,4},{16,24},{20,28},{24,16},{28,20},{1,9},{5... | collective-permute-start | bytes 786440 | tf_op jit(solution)/shard_map/ppermute | solution.py:21
  22.7 8.2 %collective-permute-start.17 = (bf16[512,256]{1,0:T(8,128)(2,1)S(1)}, bf16[512,256]{1,0:T(8,128)(2,1)S(1)}, u32[]{:S(2)}, u32[]{:S(2)}) collective-permute-start(bf16[512,256]{1,0:T(8,128)(2,1)S(1)} %get-tuple-element.44), channel_id=1, source_target_pairs={{0,1},{1,0},{2,3},{3,2},{4,5},{5,4},{6,7},{7,6},{8,9},{9,8},{10,11... | collective-permute-start | bytes 786440 | tf_op jit(solution)/shard_map/ppermute | solution.py:21
  24.4 10.9 %collective-permute-start.14 = (bf16[512,256]{1,0:T(8,128)(2,1)S(1)}, bf16[512,256]{1,0:T(8,128)(2,1)S(1)}, u32[]{:S(2)}, u32[]{:S(2)}) collective-permute-start(bf16[512,256]{1,0:T(8,128)(2,1)S(1)} %slice.41), channel_id=1, source_target_pairs={{0,24},{4,28},{8,16},{12,20},{16,8},{20,12},{24,0},{28,4},{1,25},{... | collective-permute-start | bytes 786440 | tf_op jit(solution)/shard_map/ppermute | solution.py:21
  26.6 8.7 %collective-permute-start.10 = (bf16[512,256]{1,0:T(8,128)(2,1)S(1)}, bf16[512,256]{1,0:T(8,128)(2,1)S(1)}, u32[]{:S(2)}, u32[]{:S(2)}) collective-permute-start(bf16[512,256]{1,0:T(8,128)(2,1)S(1)} %collective-permute-done.9.refs_4_), channel_id=1, source_target_pairs={{0,4},{4,0},{8,12},{12,8},{16,20},{20,16},{24,28},{28,24},{1,5},{5... | collective-permute-start | bytes 786440 | tf_op jit(solution)/shard_map/ppermute | solution.py:21
  28.8 6.5 %collective-permute-start.8 = (bf16[512,256]{1,0:T(8,128)(2,1)S(1)}, bf16[512,256]{1,0:T(8,128)(2,1)S(1)}, u32[]{:S(2)}, u32[]{:S(2)}) collective-permute-start(bf16[512,256]{1,0:T(8,128)(2,1)S(1)} %collective-permute-done.7.refs_2_), channel_id=1, source_target_pairs={{0,4},{4,0},{8,12},{12,8},{16,20},{20,16},{24,28},{28,24},{1,5},{5... | collective-permute-start | bytes 786440 | tf_op jit(solution)/shard_map/ppermute | solution.py:21
  30.9 14.7 %collective-permute-start.19 = (bf16[512,256]{1,0:T(8,128)(2,1)S(1)}, bf16[512,256]{1,0:T(8,128)(2,1)S(1)}, u32[]{:S(2)}, u32[]{:S(2)}) collective-permute-start(bf16[512,256]{1,0:T(8,128)(2,1)S(1)} %get-tuple-element.46), channel_id=1, source_target_pairs={{0,1},{1,0},{2,3},{3,2},{4,5},{5,4},{6,7},{7,6},{8,9},{9,8},{10,11... | collective-permute-start | bytes 786440 | tf_op jit(solution)/shard_map/ppermute | solution.py:21
  32.6 13.0 %collective-permute-start.18 = (bf16[512,256]{1,0:T(8,128)(2,1)S(1)}, bf16[512,256]{1,0:T(8,128)(2,1)S(1)}, u32[]{:S(2)}, u32[]{:S(2)}) collective-permute-start(bf16[512,256]{1,0:T(8,128)(2,1)S(1)} %add_convert_fusion), channel_id=1, source_target_pairs={{0,2},{1,3},{2,0},{3,1},{4,6},{5,7},{6,4},{7,5},{8,10},{9,11},{10,... | collective-permute-start | bytes 786440 | tf_op jit(solution)/shard_map/ppermute | solution.py:21
  38.3 11.1 %collective-permute-start.16 = (bf16[512,256]{1,0:T(8,128)(2,1)S(1)}, bf16[512,256]{1,0:T(8,128)(2,1)S(1)}, u32[]{:S(2)}, u32[]{:S(2)}) collective-permute-start(bf16[512,256]{1,0:T(8,128)(2,1)S(1)} %get-tuple-element.42), channel_id=1, source_target_pairs={{0,1},{1,0},{2,3},{3,2},{4,5},{5,4},{6,7},{7,6},{8,9},{9,8},{10,11... | collective-permute-start | bytes 786440 | tf_op jit(solution)/shard_map/ppermute | solution.py:21
  49.5 13.5 %collective-permute-start.20 = (bf16[512,256]{1,0:T(8,128)(2,1)S(1)}, bf16[512,256]{1,0:T(8,128)(2,1)S(1)}, u32[]{:S(2)}, u32[]{:S(2)}) collective-permute-start(bf16[512,256]{1,0:T(8,128)(2,1)S(1)} %add_convert_fusion.1), channel_id=1, source_target_pairs={{0,2},{1,3},{2,0},{3,1},{4,6},{5,7},{6,4},{7,5},{8,10},{9,11},{10,... | collective-permute-start | bytes 786440 | tf_op jit(solution)/shard_map/ppermute | solution.py:21
  52.3 8.1 %collective-permute-start.21 = (bf16[256,256]{1,0:T(8,128)(2,1)S(1)}, bf16[256,256]{1,0:T(8,128)(2,1)S(1)}, u32[]{:S(2)}, u32[]{:S(2)}) collective-permute-start(bf16[256,256]{1,0:T(8,128)(2,1)S(1)} %get-tuple-element.65), channel_id=1, source_target_pairs={{0,1},{1,0},{2,3},{3,2},{4,5},{5,4},{6,7},{7,6},{8,9},{9,8},{10,11... | collective-permute-start | bytes 393224 | tf_op jit(solution)/shard_map/ppermute | solution.py:21
  53.9 9.1 %collective-permute-start.22 = (bf16[256,256]{1,0:T(8,128)(2,1)S(1)}, bf16[256,256]{1,0:T(8,128)(2,1)S(1)}, u32[]{:S(2)}, u32[]{:S(2)}) collective-permute-start(bf16[256,256]{1,0:T(8,128)(2,1)S(1)} %get-tuple-element.66), channel_id=1, source_target_pairs={{0,1},{1,0},{2,3},{3,2},{4,5},{5,4},{6,7},{7,6},{8,9},{9,8},{10,11... | collective-permute-start | bytes 393224 | tf_op jit(solution)/shard_map/ppermute | solution.py:21
  67.1 5.2 %collective-permute-start.26 = (bf16[64,512]{1,0:T(8,128)(2,1)S(1)}, bf16[64,512]{1,0:T(8,128)(2,1)S(1)}, u32[]{:S(2)}, u32[]{:S(2)}) collective-permute-start(bf16[64,512]{1,0:T(8,128)(2,1)S(1)} %get-tuple-element.63), channel_id=1, source_target_pairs={{0,24},{4,28},{8,16},{12,20},{16,8},{20,12},{24,0},{28,4},{1,25},{... | collective-permute-start | bytes 196616 | tf_op jit(solution)/shard_map/ppermute | solution.py:21
  73.2 6.5 %collective-permute-start.29 = (bf16[64,512]{1,0:T(8,128)(2,1)S(1)}, bf16[64,512]{1,0:T(8,128)(2,1)S(1)}, u32[]{:S(2)}, u32[]{:S(2)}) collective-permute-start(bf16[64,512]{1,0:T(8,128)(2,1)S(1)} %fusion.2), channel_id=1, source_target_pairs={{0,3},{1,2},{2,1},{3,0},{4,7},{5,6},{6,5},{7,4},{8,11},{9,10},{10,... | collective-permute-start | bytes 196616 | tf_op jit(solution)/shard_map/ppermute | solution.py:21
  76.2 5.8 %collective-permute-start.28 = (bf16[64,512]{1,0:T(8,128)(2,1)S(1)}, bf16[64,512]{1,0:T(8,128)(2,1)S(1)}, u32[]{:S(2)}, u32[]{:S(2)}) collective-permute-start(bf16[64,512]{1,0:T(8,128)(2,1)S(1)} %fusion.2), channel_id=1, source_target_pairs={{0,2},{1,3},{2,0},{3,1},{4,6},{5,7},{6,4},{7,5},{8,10},{9,11},{10,... | collective-permute-start | bytes 196616 | tf_op jit(solution)/shard_map/ppermute | solution.py:21
  76.2 5.8 %collective-permute-start.27 = (bf16[64,512]{1,0:T(8,128)(2,1)S(1)}, bf16[64,512]{1,0:T(8,128)(2,1)S(1)}, u32[]{:S(2)}, u32[]{:S(2)}) collective-permute-start(bf16[64,512]{1,0:T(8,128)(2,1)S(1)} %fusion.2), channel_id=1, source_target_pairs={{0,1},{1,0},{2,3},{3,2},{4,5},{5,4},{6,7},{7,6},{8,9},{9,8},{10,11... | collective-permute-start | bytes 196616 | tf_op jit(solution)/shard_map/ppermute | solution.py:21
  82.1 5.8 %collective-permute-start.35 = (bf16[64,512]{1,0:T(8,128)(2,1)S(1)}, bf16[64,512]{1,0:T(8,128)(2,1)S(1)}, u32[]{:S(2)}, u32[]{:S(2)}) collective-permute-start(bf16[64,512]{1,0:T(8,128)(2,1)S(1)} %add_convert_fusion.2.refs_0_), channel_id=1, source_target_pairs={{0,24},{4,28},{8,16},{12,20},{16,8},{20,12},{24,0},{28,4},{1,25},{... | collective-permute-start | bytes 196616 | tf_op jit(solution)/shard_map/ppermute | solution.py:21
  (18 other events, 85.5 us)

commit v5 on v4

--- a/solution.py
+++ b/solution.py
@@ -211,25 +211,32 @@
     )(weight, cotangent, pre, *early, *terms)
 
 
-def join(pieces):
-    n = len(pieces)
+def join(pieces, core, whole=None):
+    n = 2 * len(pieces)
     part, f = pieces[0].shape
 
     def kernel(*refs):
-        out_ref = refs[-1]
+        *refs, out_ref, buffer, sems = refs
         me_row = lax.axis_index("row")
-        for k in range(n):
-            at = pl.multiple_of((me_row ^ k) * part, part)
-            out_ref[pl.ds(at, part), :] = refs[k][...].astype(F32)
-
-    vmem = pl.BlockSpec(memory_space=pltpu.VMEM)
+        copies = []
+        for k, ref in enumerate(refs[:n // 2]):
+            buffer[k] = ref[...].astype(F32)
+            at = pl.multiple_of((me_row ^ (2 * k + core)) * part, part)
+            copies.append(pltpu.make_async_copy(buffer.at[k], out_ref.at[pl.ds(at, part), :], sems.at[k]))
+            copies[k].start()
+        for copy in copies:
+            copy.wait()
+
+    vmem, any_space = pl.BlockSpec(memory_space=pltpu.VMEM), pl.BlockSpec(memory_space=pl.ANY)
     return pl.pallas_call(
         kernel,
         out_shape=jax.ShapeDtypeStruct((n * part, f), F32),
-        in_specs=[vmem] * n,
-        out_specs=vmem,
-        compiler_params=pltpu.CompilerParams(vmem_limit_bytes=VMEM_LIMIT),
-    )(*pieces)
+        in_specs=[vmem] * (n // 2) + ([] if whole is None else [any_space]),
+        out_specs=any_space,
+        scratch_shapes=[pltpu.VMEM((n // 2, part, f), F32), pltpu.SemaphoreType.DMA((n // 2,))],
+        input_output_aliases={} if whole is None else {n // 2: 0},
+        compiler_params=pltpu.CompilerParams(vmem_limit_bytes=VMEM_LIMIT),
+    )(*pieces, *([] if whole is None else [whole]))
 
 
 def reduce_gradient(keep, send):
@@ -248,11 +255,9 @@
         else:
             rounded = plus(rounded, swap(rounded, "col", bit))
             bit *= 2
-    pieces = []
-    for k in range(0, n_row, 2):
-        piece = swap(rounded, "row", k) if k else rounded
-        pieces += [piece, swap(piece, "row", 1)]
-    return join(pieces)
+    even = [swap(rounded, "row", k) if k else rounded for k in range(0, n_row, 2)]
+    odd = [swap(piece, "row", 1) for piece in even]
+    return join(odd, 1, join(even, 0))
 
 
 def plus(*terms):

time: 91.3 us -> 91 us (level)
  transfers between devices with their start and end apart: 37 -> 37, of which waited for: 24 -> 22; matrix products, arithmetic and copies ran while one was open for 0% -> 0% of each run, Pallas kernels for 4% -> 5%
where the time goes in v5:
time: 91 us; the launch traced here: 90.8 us
  waiting for transfers between devices  46.1 us (51%)
  starting transfers between devices  34.4 us (38%)
  Pallas kernels  6.53 us (7%)
  local copies, waits for them, and re-layouts  1.8 us (2%)
  between operations  1.6 us (2%)
    ppermute x37, waiting for transfers between devices, swap(): lax.ppermute(x, axis, [(i, i ^ mask) for i in range(lax.axis_size(axis))])  46.1 us
    ppermute x37, starting transfers between devices, swap(): lax.ppermute(x, axis, [(i, i ^ mask) for i in range(lax.axis_size(axis))])  34.4 us
    pallas_call x2, Pallas kernels, tile_products(): pl.pallas_call(functools.partial(tiles_kernel, at=at, n_row=n_row, part=m...  3.08 us
  transfers between devices with their start and end apart: 37, of which 22 were waited for; matrix products, arithmetic and copies ran while one was open for 0% of the time, Pallas kernels for 5%

profile of v5, /device:TPU:0, one launch (start us, length us, event | category | flops | bytes accessed | tf_op | source)
XLA Modules:
  0.0 90.8 jit_solution(6513402325088922087)
XLA Ops:
  1.6 3.0 %collective-permute-start.1 = (bf16[256,256]{1,0:T(8,128)(2,1)S(1)}, bf16[256,256]{1,0:T(8,128)(2,1)S(1)}, u32[]{:S(2)}, u32[]{:S(2)}) collective-permute-start(bf16[256,256]{1,0:T(8,128)(2,1)S(1)} %get-tuple-element.60), channel_id=1, source_target_pairs={{0,16},{4,20},{8,24},{12,28},{16,0},{20,4},{24,8},{28,12},{1,17},{... | collective-permute-start | bytes 393224 | tf_op jit(solution)/shard_map/ppermute | solution.py:21
  6.8 1.8 %collective-permute-done.1 = bf16[256,256]{1,0:T(8,128)(2,1)S(1)} collective-permute-done((bf16[256,256]{1,0:T(8,128)(2,1)S(1)}, bf16[256,256]{1,0:T(8,128)(2,1)S(1)}, u32[]{:S(2)}, u32[]{:S(2)}) %collective-permute-start.1) | collective-permute-done | bytes 131104 | tf_op jit(solution)/shard_map/ppermute | solution.py:21
  8.6 2.4 %collective-permute-done = bf16[256,256]{1,0:T(8,128)(2,1)S(1)} collective-permute-done((bf16[256,256]{1,0:T(8,128)(2,1)S(1)}, bf16[256,256]{1,0:T(8,128)(2,1)S(1)}, u32[]{:S(2)}, u32[]{:S(2)}) %collective-permute-start) | collective-permute-done | bytes 131104 | tf_op jit(solution)/shard_map/ppermute | solution.py:21
  11.1 1.9 %collective-permute-start.6 = (bf16[256,256]{1,0:T(8,128)(2,1)S(1)}, bf16[256,256]{1,0:T(8,128)(2,1)S(1)}, u32[]{:S(2)}, u32[]{:S(2)}) collective-permute-start(bf16[256,256]{1,0:T(8,128)(2,1)S(1)} %collective-permute-done.1), channel_id=1, source_target_pairs={{0,8},{4,12},{8,0},{12,4},{16,24},{20,28},{24,16},{28,20},{1,9},{5... | collective-permute-start | bytes 393224 | tf_op jit(solution)/shard_map/ppermute | solution.py:21
  14.1 1.8 %collective-permute-done.5 = bf16[256,256]{1,0:T(8,128)(2,1)S(1)} collective-permute-done((bf16[256,256]{1,0:T(8,128)(2,1)S(1)}, bf16[256,256]{1,0:T(8,128)(2,1)S(1)}, u32[]{:S(2)}, u32[]{:S(2)}) %collective-permute-start.5) | collective-permute-done | bytes 131104 | tf_op jit(solution)/shard_map/ppermute | solution.py:21
  17.6 2.0 %collective-permute-start.9 = (bf16[512,256]{1,0:T(8,128)(2,1)S(1)}, bf16[512,256]{1,0:T(8,128)(2,1)S(1)}, u32[]{:S(2)}, u32[]{:S(2)}) collective-permute-start(bf16[512,256]{1,0:T(8,128)(2,1)S(1)} %slice.40), channel_id=1, source_target_pairs={{0,16},{4,20},{8,24},{12,28},{16,0},{20,4},{24,8},{28,12},{1,17},{... | collective-permute-start | bytes 786440 | tf_op jit(solution)/shard_map/ppermute | solution.py:21
  22.7 1.6 %collective-permute-start.17 = (bf16[512,256]{1,0:T(8,128)(2,1)S(1)}, bf16[512,256]{1,0:T(8,128)(2,1)S(1)}, u32[]{:S(2)}, u32[]{:S(2)}) collective-permute-start(bf16[512,256]{1,0:T(8,128)(2,1)S(1)} %get-tuple-element.44), channel_id=1, source_target_pairs={{0,1},{1,0},{2,3},{3,2},{4,5},{5,4},{6,7},{7,6},{8,9},{9,8},{10,11... | collective-permute-start | bytes 786440 | tf_op jit(solution)/shard_map/ppermute | solution.py:21
  24.5 2.1 %collective-permute-done.9.refs_4_ = bf16[512,256]{1,0:T(8,128)(2,1)S(1)} collective-permute-done((bf16[512,256]{1,0:T(8,128)(2,1)S(1)}, bf16[512,256]{1,0:T(8,128)(2,1)S(1)}, u32[]{:S(2)}, u32[]{:S(2)}) %collective-permute-start.9) | collective-permute-done | bytes 262176 | tf_op jit(solution)/shard_map/ppermute | solution.py:21
  26.6 2.2 %collective-permute-done.7.refs_2_ = bf16[512,256]{1,0:T(8,128)(2,1)S(1)} collective-permute-done((bf16[512,256]{1,0:T(8,128)(2,1)S(1)}, bf16[512,256]{1,0:T(8,128)(2,1)S(1)}, u32[]{:S(2)}, u32[]{:S(2)}) %collective-permute-start.7) | collective-permute-done | bytes 262176 | tf_op jit(solution)/shard_map/ppermute | solution.py:21
  28.8 2.1 %collective-permute-done.17 = bf16[512,256]{1,0:T(8,128)(2,1)S(1)} collective-permute-done((bf16[512,256]{1,0:T(8,128)(2,1)S(1)}, bf16[512,256]{1,0:T(8,128)(2,1)S(1)}, u32[]{:S(2)}, u32[]{:S(2)}) %collective-permute-start.17) | collective-permute-done | bytes 262176 | tf_op jit(solution)/shard_map/ppermute | solution.py:21
  30.9 1.6 %collective-permute-start.19 = (bf16[512,256]{1,0:T(8,128)(2,1)S(1)}, bf16[512,256]{1,0:T(8,128)(2,1)S(1)}, u32[]{:S(2)}, u32[]{:S(2)}) collective-permute-start(bf16[512,256]{1,0:T(8,128)(2,1)S(1)} %get-tuple-element.46), channel_id=1, source_target_pairs={{0,1},{1,0},{2,3},{3,2},{4,5},{5,4},{6,7},{7,6},{8,9},{9,8},{10,11... | collective-permute-start | bytes 786440 | tf_op jit(solution)/shard_map/ppermute | solution.py:21
  32.6 2.7 %collective-permute-start.18 = (bf16[512,256]{1,0:T(8,128)(2,1)S(1)}, bf16[512,256]{1,0:T(8,128)(2,1)S(1)}, u32[]{:S(2)}, u32[]{:S(2)}) collective-permute-start(bf16[512,256]{1,0:T(8,128)(2,1)S(1)} %add_convert_fusion), channel_id=1, source_target_pairs={{0,2},{1,3},{2,0},{3,1},{4,6},{5,7},{6,4},{7,5},{8,10},{9,11},{10,... | collective-permute-start | bytes 786440 | tf_op jit(solution)/shard_map/ppermute | solution.py:21
  38.8 6.8 %collective-permute-done.19.refs_2_ = bf16[512,256]{1,0:T(8,128)(2,1)S(1)} collective-permute-done((bf16[512,256]{1,0:T(8,128)(2,1)S(1)}, bf16[512,256]{1,0:T(8,128)(2,1)S(1)}, u32[]{:S(2)}, u32[]{:S(2)}) %collective-permute-start.19) | collective-permute-done | bytes 262176 | tf_op jit(solution)/shard_map/ppermute | solution.py:21
  45.9 3.5 %collective-permute-done.16 = bf16[512,256]{1,0:T(8,128)(2,1)S(1)} collective-permute-done((bf16[512,256]{1,0:T(8,128)(2,1)S(1)}, bf16[512,256]{1,0:T(8,128)(2,1)S(1)}, u32[]{:S(2)}, u32[]{:S(2)}) %collective-permute-start.16) | collective-permute-done | bytes 262176 | tf_op jit(solution)/shard_map/ppermute | solution.py:21
  49.5 2.7 %collective-permute-start.20 = (bf16[512,256]{1,0:T(8,128)(2,1)S(1)}, bf16[512,256]{1,0:T(8,128)(2,1)S(1)}, u32[]{:S(2)}, u32[]{:S(2)}) collective-permute-start(bf16[512,256]{1,0:T(8,128)(2,1)S(1)} %add_convert_fusion.1), channel_id=1, source_target_pairs={{0,2},{1,3},{2,0},{3,1},{4,6},{5,7},{6,4},{7,5},{8,10},{9,11},{10,... | collective-permute-start | bytes 786440 | tf_op jit(solution)/shard_map/ppermute | solution.py:21
  52.3 1.6 %collective-permute-start.21 = (bf16[256,256]{1,0:T(8,128)(2,1)S(1)}, bf16[256,256]{1,0:T(8,128)(2,1)S(1)}, u32[]{:S(2)}, u32[]{:S(2)}) collective-permute-start(bf16[256,256]{1,0:T(8,128)(2,1)S(1)} %get-tuple-element.65), channel_id=1, source_target_pairs={{0,1},{1,0},{2,3},{3,2},{4,5},{5,4},{6,7},{7,6},{8,9},{9,8},{10,11... | collective-permute-start | bytes 393224 | tf_op jit(solution)/shard_map/ppermute | solution.py:21
  54.4 6.0 %collective-permute-done.21 = bf16[256,256]{1,0:T(8,128)(2,1)S(1)} collective-permute-done((bf16[256,256]{1,0:T(8,128)(2,1)S(1)}, bf16[256,256]{1,0:T(8,128)(2,1)S(1)}, u32[]{:S(2)}, u32[]{:S(2)}) %collective-permute-start.21) | collective-permute-done | bytes 131104 | tf_op jit(solution)/shard_map/ppermute | solution.py:21
  60.4 2.6 %collective-permute-done.22 = bf16[256,256]{1,0:T(8,128)(2,1)S(1)} collective-permute-done((bf16[256,256]{1,0:T(8,128)(2,1)S(1)}, bf16[256,256]{1,0:T(8,128)(2,1)S(1)}, u32[]{:S(2)}, u32[]{:S(2)}) %collective-permute-start.22) | collective-permute-done | bytes 131104 | tf_op jit(solution)/shard_map/ppermute | solution.py:21
  68.1 1.6 %collective-permute-start.25 = (bf16[64,512]{1,0:T(8,128)(2,1)S(1)}, bf16[64,512]{1,0:T(8,128)(2,1)S(1)}, u32[]{:S(2)}, u32[]{:S(2)}) collective-permute-start(bf16[64,512]{1,0:T(8,128)(2,1)S(1)} %get-tuple-element.64), channel_id=1, source_target_pairs={{0,16},{4,20},{8,24},{12,28},{16,0},{20,4},{24,8},{28,12},{1,17},{... | collective-permute-start | bytes 196616 | tf_op jit(solution)/shard_map/ppermute | solution.py:21
  73.1 3.0 %collective-permute-start.29 = (bf16[64,512]{1,0:T(8,128)(2,1)S(1)}, bf16[64,512]{1,0:T(8,128)(2,1)S(1)}, u32[]{:S(2)}, u32[]{:S(2)}) collective-permute-start(bf16[64,512]{1,0:T(8,128)(2,1)S(1)} %fusion.2), channel_id=1, source_target_pairs={{0,3},{1,2},{2,1},{3,0},{4,7},{5,6},{6,5},{7,4},{8,11},{9,10},{10,... | collective-permute-start | bytes 196616 | tf_op jit(solution)/shard_map/ppermute | solution.py:21
  77.6 2.0 %collective-permute-done.29 = bf16[64,512]{1,0:T(8,128)(2,1)S(1)} collective-permute-done((bf16[64,512]{1,0:T(8,128)(2,1)S(1)}, bf16[64,512]{1,0:T(8,128)(2,1)S(1)}, u32[]{:S(2)}, u32[]{:S(2)}) %collective-permute-start.29) | collective-permute-done | bytes 65568 | tf_op jit(solution)/shard_map/ppermute | solution.py:21
  79.6 2.4 %collective-permute-done.28 = bf16[64,512]{1,0:T(8,128)(2,1)S(1)} collective-permute-done((bf16[64,512]{1,0:T(8,128)(2,1)S(1)}, bf16[64,512]{1,0:T(8,128)(2,1)S(1)}, u32[]{:S(2)}, u32[]{:S(2)}) %collective-permute-start.28) | collective-permute-done | bytes 65568 | tf_op jit(solution)/shard_map/ppermute | solution.py:21
  82.0 1.6 %collective-permute-start.35 = (bf16[64,512]{1,0:T(8,128)(2,1)S(1)}, bf16[64,512]{1,0:T(8,128)(2,1)S(1)}, u32[]{:S(2)}, u32[]{:S(2)}) collective-permute-start(bf16[64,512]{1,0:T(8,128)(2,1)S(1)} %add_convert_fusion.2.refs_0_), channel_id=1, source_target_pairs={{0,24},{4,28},{8,16},{12,20},{16,8},{20,12},{24,0},{28,4},{1,25},{... | collective-permute-start | bytes 196616 | tf_op jit(solution)/shard_map/ppermute | solution.py:21
  85.6 2.3 %collective-permute-done.35.refs_3_ = bf16[64,512]{1,0:T(8,128)(2,1)S(1)} collective-permute-done((bf16[64,512]{1,0:T(8,128)(2,1)S(1)}, bf16[64,512]{1,0:T(8,128)(2,1)S(1)}, u32[]{:S(2)}, u32[]{:S(2)}) %collective-permute-start.35) | collective-permute-done | bytes 65568 | tf_op jit(solution)/shard_map/ppermute | solution.py:21
  (88 shorter events, 27.7 us)
Async XLA Ops:
  1.6 6.9 %collective-permute-start.1 = (bf16[256,256]{1,0:T(8,128)(2,1)S(1)}, bf16[256,256]{1,0:T(8,128)(2,1)S(1)}, u32[]{:S(2)}, u32[]{:S(2)}) collective-permute-start(bf16[256,256]{1,0:T(8,128)(2,1)S(1)} %get-tuple-element.60), channel_id=1, source_target_pairs={{0,16},{4,20},{8,24},{12,28},{16,0},{20,4},{24,8},{28,12},{1,17},{... | collective-permute-start | bytes 393224 | tf_op jit(solution)/shard_map/ppermute | solution.py:21
  4.7 6.3 %collective-permute-start = (bf16[256,256]{1,0:T(8,128)(2,1)S(1)}, bf16[256,256]{1,0:T(8,128)(2,1)S(1)}, u32[]{:S(2)}, u32[]{:S(2)}) collective-permute-start(bf16[256,256]{1,0:T(8,128)(2,1)S(1)} %get-tuple-element.61), channel_id=1, source_target_pairs={{0,8},{4,12},{8,0},{12,4},{16,24},{20,28},{24,16},{28,20},{1,9},{5... | collective-permute-start | bytes 393224 | tf_op jit(solution)/shard_map/ppermute | solution.py:21
  6.2 6.8 %collective-permute-start.4 = (bf16[256,256]{1,0:T(8,128)(2,1)S(1)}, bf16[256,256]{1,0:T(8,128)(2,1)S(1)}, u32[]{:S(2)}, u32[]{:S(2)}) collective-permute-start(bf16[256,256]{1,0:T(8,128)(2,1)S(1)} %get-tuple-element.61), channel_id=1, source_target_pairs={{0,16},{4,20},{8,24},{12,28},{16,0},{20,4},{24,8},{28,12},{1,17},{... | collective-permute-start | bytes 393224 | tf_op jit(solution)/shard_map/ppermute | solution.py:21
  6.7 6.9 %collective-permute-start.3 = (bf16[256,256]{1,0:T(8,128)(2,1)S(1)}, bf16[256,256]{1,0:T(8,128)(2,1)S(1)}, u32[]{:S(2)}, u32[]{:S(2)}) collective-permute-start(bf16[256,256]{1,0:T(8,128)(2,1)S(1)} %get-tuple-element.60), channel_id=1, source_target_pairs={{0,8},{4,12},{8,0},{12,4},{16,24},{20,28},{24,16},{28,20},{1,9},{5... | collective-permute-start | bytes 393224 | tf_op jit(solution)/shard_map/ppermute | solution.py:21
  13.0 8.1 %collective-permute-start.2 = (bf16[512,512]{1,0:T(8,128)(2,1)S(1)}, bf16[512,512]{1,0:T(8,128)(2,1)S(1)}, u32[]{:S(2)}, u32[]{:S(2)}) collective-permute-start(bf16[512,512]{1,0:T(8,128)(2,1)S(1)} %copy-done), channel_id=1, source_target_pairs={{0,4},{4,0},{8,12},{12,8},{16,20},{20,16},{24,28},{28,24},{1,5},{5... | collective-permute-start | bytes 1572872 | tf_op jit(solution)/shard_map/ppermute | solution.py:21
  13.6 6.1 %collective-permute-start.11 = (bf16[512,256]{1,0:T(8,128)(2,1)S(1)}, bf16[512,256]{1,0:T(8,128)(2,1)S(1)}, u32[]{:S(2)}, u32[]{:S(2)}) collective-permute-start(bf16[512,256]{1,0:T(8,128)(2,1)S(1)} %constant_dynamic-update-slice_fusion.refs_2_), channel_id=1, source_target_pairs={{0,4},{4,0},{8,12},{12,8},{16,20},{20,16},{24,28},{28,24},{1,5},{5... | collective-permute-start | bytes 786440 | tf_op jit(solution)/shard_map/ppermute | solution.py:21
  13.7 7.5 %collective-permute-start.12 = (bf16[512,256]{1,0:T(8,128)(2,1)S(1)}, bf16[512,256]{1,0:T(8,128)(2,1)S(1)}, u32[]{:S(2)}, u32[]{:S(2)}) collective-permute-start(bf16[512,256]{1,0:T(8,128)(2,1)S(1)} %constant_dynamic-update-slice_fusion.2.refs_4_), channel_id=1, source_target_pairs={{0,4},{4,0},{8,12},{12,8},{16,20},{20,16},{24,28},{28,24},{1,5},{5... | collective-permute-start | bytes 786440 | tf_op jit(solution)/shard_map/ppermute | solution.py:21
  17.6 9.0 %collective-permute-start.9 = (bf16[512,256]{1,0:T(8,128)(2,1)S(1)}, bf16[512,256]{1,0:T(8,128)(2,1)S(1)}, u32[]{:S(2)}, u32[]{:S(2)}) collective-permute-start(bf16[512,256]{1,0:T(8,128)(2,1)S(1)} %slice.40), channel_id=1, source_target_pairs={{0,16},{4,20},{8,24},{12,28},{16,0},{20,4},{24,8},{28,12},{1,17},{... | collective-permute-start | bytes 786440 | tf_op jit(solution)/shard_map/ppermute | solution.py:21
  19.6 9.1 %collective-permute-start.7 = (bf16[512,256]{1,0:T(8,128)(2,1)S(1)}, bf16[512,256]{1,0:T(8,128)(2,1)S(1)}, u32[]{:S(2)}, u32[]{:S(2)}) collective-permute-start(bf16[512,256]{1,0:T(8,128)(2,1)S(1)} %slice.40), channel_id=1, source_target_pairs={{0,8},{4,12},{8,0},{12,4},{16,24},{20,28},{24,16},{28,20},{1,9},{5... | collective-permute-start | bytes 786440 | tf_op jit(solution)/shard_map/ppermute | solution.py:21
  22.7 8.2 %collective-permute-start.17 = (bf16[512,256]{1,0:T(8,128)(2,1)S(1)}, bf16[512,256]{1,0:T(8,128)(2,1)S(1)}, u32[]{:S(2)}, u32[]{:S(2)}) collective-permute-start(bf16[512,256]{1,0:T(8,128)(2,1)S(1)} %get-tuple-element.44), channel_id=1, source_target_pairs={{0,1},{1,0},{2,3},{3,2},{4,5},{5,4},{6,7},{7,6},{8,9},{9,8},{10,11... | collective-permute-start | bytes 786440 | tf_op jit(solution)/shard_map/ppermute | solution.py:21
  24.4 10.9 %collective-permute-start.14 = (bf16[512,256]{1,0:T(8,128)(2,1)S(1)}, bf16[512,256]{1,0:T(8,128)(2,1)S(1)}, u32[]{:S(2)}, u32[]{:S(2)}) collective-permute-start(bf16[512,256]{1,0:T(8,128)(2,1)S(1)} %slice.41), channel_id=1, source_target_pairs={{0,24},{4,28},{8,16},{12,20},{16,8},{20,12},{24,0},{28,4},{1,25},{... | collective-permute-start | bytes 786440 | tf_op jit(solution)/shard_map/ppermute | solution.py:21
  26.6 8.7 %collective-permute-start.10 = (bf16[512,256]{1,0:T(8,128)(2,1)S(1)}, bf16[512,256]{1,0:T(8,128)(2,1)S(1)}, u32[]{:S(2)}, u32[]{:S(2)}) collective-permute-start(bf16[512,256]{1,0:T(8,128)(2,1)S(1)} %collective-permute-done.9.refs_4_), channel_id=1, source_target_pairs={{0,4},{4,0},{8,12},{12,8},{16,20},{20,16},{24,28},{28,24},{1,5},{5... | collective-permute-start | bytes 786440 | tf_op jit(solution)/shard_map/ppermute | solution.py:21
  28.8 6.5 %collective-permute-start.8 = (bf16[512,256]{1,0:T(8,128)(2,1)S(1)}, bf16[512,256]{1,0:T(8,128)(2,1)S(1)}, u32[]{:S(2)}, u32[]{:S(2)}) collective-permute-start(bf16[512,256]{1,0:T(8,128)(2,1)S(1)} %collective-permute-done.7.refs_2_), channel_id=1, source_target_pairs={{0,4},{4,0},{8,12},{12,8},{16,20},{20,16},{24,28},{28,24},{1,5},{5... | collective-permute-start | bytes 786440 | tf_op jit(solution)/shard_map/ppermute | solution.py:21
  30.9 14.7 %collective-permute-start.19 = (bf16[512,256]{1,0:T(8,128)(2,1)S(1)}, bf16[512,256]{1,0:T(8,128)(2,1)S(1)}, u32[]{:S(2)}, u32[]{:S(2)}) collective-permute-start(bf16[512,256]{1,0:T(8,128)(2,1)S(1)} %get-tuple-element.46), channel_id=1, source_target_pairs={{0,1},{1,0},{2,3},{3,2},{4,5},{5,4},{6,7},{7,6},{8,9},{9,8},{10,11... | collective-permute-start | bytes 786440 | tf_op jit(solution)/shard_map/ppermute | solution.py:21
  32.6 13.0 %collective-permute-start.18 = (bf16[512,256]{1,0:T(8,128)(2,1)S(1)}, bf16[512,256]{1,0:T(8,128)(2,1)S(1)}, u32[]{:S(2)}, u32[]{:S(2)}) collective-permute-start(bf16[512,256]{1,0:T(8,128)(2,1)S(1)} %add_convert_fusion), channel_id=1, source_target_pairs={{0,2},{1,3},{2,0},{3,1},{4,6},{5,7},{6,4},{7,5},{8,10},{9,11},{10,... | collective-permute-start | bytes 786440 | tf_op jit(solution)/shard_map/ppermute | solution.py:21
  38.3 11.1 %collective-permute-start.16 = (bf16[512,256]{1,0:T(8,128)(2,1)S(1)}, bf16[512,256]{1,0:T(8,128)(2,1)S(1)}, u32[]{:S(2)}, u32[]{:S(2)}) collective-permute-start(bf16[512,256]{1,0:T(8,128)(2,1)S(1)} %get-tuple-element.42), channel_id=1, source_target_pairs={{0,1},{1,0},{2,3},{3,2},{4,5},{5,4},{6,7},{7,6},{8,9},{9,8},{10,11... | collective-permute-start | bytes 786440 | tf_op jit(solution)/shard_map/ppermute | solution.py:21
  49.5 13.5 %collective-permute-start.20 = (bf16[512,256]{1,0:T(8,128)(2,1)S(1)}, bf16[512,256]{1,0:T(8,128)(2,1)S(1)}, u32[]{:S(2)}, u32[]{:S(2)}) collective-permute-start(bf16[512,256]{1,0:T(8,128)(2,1)S(1)} %add_convert_fusion.1), channel_id=1, source_target_pairs={{0,2},{1,3},{2,0},{3,1},{4,6},{5,7},{6,4},{7,5},{8,10},{9,11},{10,... | collective-permute-start | bytes 786440 | tf_op jit(solution)/shard_map/ppermute | solution.py:21
  52.3 8.1 %collective-permute-start.21 = (bf16[256,256]{1,0:T(8,128)(2,1)S(1)}, bf16[256,256]{1,0:T(8,128)(2,1)S(1)}, u32[]{:S(2)}, u32[]{:S(2)}) collective-permute-start(bf16[256,256]{1,0:T(8,128)(2,1)S(1)} %get-tuple-element.65), channel_id=1, source_target_pairs={{0,1},{1,0},{2,3},{3,2},{4,5},{5,4},{6,7},{7,6},{8,9},{9,8},{10,11... | collective-permute-start | bytes 393224 | tf_op jit(solution)/shard_map/ppermute | solution.py:21
  53.9 9.1 %collective-permute-start.22 = (bf16[256,256]{1,0:T(8,128)(2,1)S(1)}, bf16[256,256]{1,0:T(8,128)(2,1)S(1)}, u32[]{:S(2)}, u32[]{:S(2)}) collective-permute-start(bf16[256,256]{1,0:T(8,128)(2,1)S(1)} %get-tuple-element.66), channel_id=1, source_target_pairs={{0,1},{1,0},{2,3},{3,2},{4,5},{5,4},{6,7},{7,6},{8,9},{9,8},{10,11... | collective-permute-start | bytes 393224 | tf_op jit(solution)/shard_map/ppermute | solution.py:21
  67.1 5.2 %collective-permute-start.26 = (bf16[64,512]{1,0:T(8,128)(2,1)S(1)}, bf16[64,512]{1,0:T(8,128)(2,1)S(1)}, u32[]{:S(2)}, u32[]{:S(2)}) collective-permute-start(bf16[64,512]{1,0:T(8,128)(2,1)S(1)} %get-tuple-element.63), channel_id=1, source_target_pairs={{0,24},{4,28},{8,16},{12,20},{16,8},{20,12},{24,0},{28,4},{1,25},{... | collective-permute-start | bytes 196616 | tf_op jit(solution)/shard_map/ppermute | solution.py:21
  73.1 6.5 %collective-permute-start.29 = (bf16[64,512]{1,0:T(8,128)(2,1)S(1)}, bf16[64,512]{1,0:T(8,128)(2,1)S(1)}, u32[]{:S(2)}, u32[]{:S(2)}) collective-permute-start(bf16[64,512]{1,0:T(8,128)(2,1)S(1)} %fusion.2), channel_id=1, source_target_pairs={{0,3},{1,2},{2,1},{3,0},{4,7},{5,6},{6,5},{7,4},{8,11},{9,10},{10,... | collective-permute-start | bytes 196616 | tf_op jit(solution)/shard_map/ppermute | solution.py:21
  76.2 5.8 %collective-permute-start.28 = (bf16[64,512]{1,0:T(8,128)(2,1)S(1)}, bf16[64,512]{1,0:T(8,128)(2,1)S(1)}, u32[]{:S(2)}, u32[]{:S(2)}) collective-permute-start(bf16[64,512]{1,0:T(8,128)(2,1)S(1)} %fusion.2), channel_id=1, source_target_pairs={{0,2},{1,3},{2,0},{3,1},{4,6},{5,7},{6,4},{7,5},{8,10},{9,11},{10,... | collective-permute-start | bytes 196616 | tf_op jit(solution)/shard_map/ppermute | solution.py:21
  76.2 5.8 %collective-permute-start.27 = (bf16[64,512]{1,0:T(8,128)(2,1)S(1)}, bf16[64,512]{1,0:T(8,128)(2,1)S(1)}, u32[]{:S(2)}, u32[]{:S(2)}) collective-permute-start(bf16[64,512]{1,0:T(8,128)(2,1)S(1)} %fusion.2), channel_id=1, source_target_pairs={{0,1},{1,0},{2,3},{3,2},{4,5},{5,4},{6,7},{7,6},{8,9},{9,8},{10,11... | collective-permute-start | bytes 196616 | tf_op jit(solution)/shard_map/ppermute | solution.py:21
  82.0 5.8 %collective-permute-start.35 = (bf16[64,512]{1,0:T(8,128)(2,1)S(1)}, bf16[64,512]{1,0:T(8,128)(2,1)S(1)}, u32[]{:S(2)}, u32[]{:S(2)}) collective-permute-start(bf16[64,512]{1,0:T(8,128)(2,1)S(1)} %add_convert_fusion.2.refs_0_), channel_id=1, source_target_pairs={{0,24},{4,28},{8,16},{12,20},{16,8},{20,12},{24,0},{28,4},{1,25},{... | collective-permute-start | bytes 196616 | tf_op jit(solution)/shard_map/ppermute | solution.py:21
  (18 other events, 87.0 us)

commit v6 on v5

--- a/solution.py
+++ b/solution.py
@@ -301,7 +301,7 @@
     for at, wide in zip(starts, CHUNKS):
         final = at + wide == features.shape[1]
         if at:
-            early, *blocks = lax.optimization_barrier((features, *blocks))
+            early, blocks[0] = lax.optimization_barrier((features, blocks[0]))
             late, *keep = lax.optimization_barrier((features, *keep))
             blocks = gather_chips(early[:, at:at + wide], late[:, at:at + wide])
         pieces = [own, core]
@@ -317,7 +317,7 @@
             send, aggregated, pre = lax.optimization_barrier((send, aggregated, pre))
             summed.append(aggregated)
         near, got = lax.optimization_barrier((near, got))
-        cut = near.shape[0] // (2 if final else 1)
+        cut = near.shape[0] // (4 if final else 1)
         arrived = [swap(near[i:i + cut], "col", 1) for i in range(0, near.shape[0], cut)]
         terms, done = [keep[0], swap(send, "col", 2), jnp.concatenate(arrived)], at
     scale = 1.0 / math.sqrt(cotangent.shape[0] * n_row * n_col)

time: 91 us -> 91.1 us (level)
  starting transfers between devices: 34.4 us -> 36.6 us
  waiting for transfers between devices: 46.1 us -> 44.1 us
    ppermute x37 -> x39, starting transfers between devices: 34.4 us -> 36.6 us  [swap(): lax.ppermute(x, axis, [(i, i ^ mask) for i in range(lax.axis_size(axis))])]
    ppermute x37 -> x39, waiting for transfers between devices: 46.1 us -> 44.1 us  [swap(): lax.ppermute(x, axis, [(i, i ^ mask) for i in range(lax.axis_size(axis))])]
  transfers between devices with their start and end apart: 37 -> 39, of which waited for: 22 -> 24; matrix products, arithmetic and copies ran while one was open for 0% -> 0% of each run, Pallas kernels for 5% -> 5%
where the time goes in v6:
time: 91.1 us; the launch traced here: 91 us
  waiting for transfers between devices  44.1 us (48%)
  starting transfers between devices  36.6 us (40%)
  Pallas kernels  6.52 us (7%)
  local copies, waits for them, and re-layouts  1.8 us (2%)
  between operations  1.61 us (2%)
    ppermute x39, waiting for transfers between devices, swap(): lax.ppermute(x, axis, [(i, i ^ mask) for i in range(lax.axis_size(axis))])  44.1 us
    ppermute x39, starting transfers between devices, swap(): lax.ppermute(x, axis, [(i, i ^ mask) for i in range(lax.axis_size(axis))])  36.6 us
    pallas_call x2, Pallas kernels, tile_products(): pl.pallas_call(functools.partial(tiles_kernel, at=at, n_row=n_row, part=m...  3.08 us
  transfers between devices with their start and end apart: 39, of which 24 were waited for; matrix products, arithmetic and copies ran while one was open for 0% of the time, Pallas kernels for 5%

profile of v6, /device:TPU:0, one launch (start us, length us, event | category | flops | bytes accessed | tf_op | source)
XLA Modules:
  0.0 91.0 jit_solution(7366553907193179182)
XLA Ops:
  1.6 3.0 %collective-permute-start.1 = (bf16[256,256]{1,0:T(8,128)(2,1)S(1)}, bf16[256,256]{1,0:T(8,128)(2,1)S(1)}, u32[]{:S(2)}, u32[]{:S(2)}) collective-permute-start(bf16[256,256]{1,0:T(8,128)(2,1)S(1)} %get-tuple-element.60), channel_id=1, source_target_pairs={{0,16},{4,20},{8,24},{12,28},{16,0},{20,4},{24,8},{28,12},{1,17},{... | collective-permute-start | bytes 393224 | tf_op jit(solution)/shard_map/ppermute | solution.py:21
  6.8 1.8 %collective-permute-done.1 = bf16[256,256]{1,0:T(8,128)(2,1)S(1)} collective-permute-done((bf16[256,256]{1,0:T(8,128)(2,1)S(1)}, bf16[256,256]{1,0:T(8,128)(2,1)S(1)}, u32[]{:S(2)}, u32[]{:S(2)}) %collective-permute-start.1) | collective-permute-done | bytes 131104 | tf_op jit(solution)/shard_map/ppermute | solution.py:21
  8.6 2.4 %collective-permute-done = bf16[256,256]{1,0:T(8,128)(2,1)S(1)} collective-permute-done((bf16[256,256]{1,0:T(8,128)(2,1)S(1)}, bf16[256,256]{1,0:T(8,128)(2,1)S(1)}, u32[]{:S(2)}, u32[]{:S(2)}) %collective-permute-start) | collective-permute-done | bytes 131104 | tf_op jit(solution)/shard_map/ppermute | solution.py:21
  11.1 1.9 %collective-permute-start.12 = (bf16[256,256]{1,0:T(8,128)(2,1)S(1)}, bf16[256,256]{1,0:T(8,128)(2,1)S(1)}, u32[]{:S(2)}, u32[]{:S(2)}) collective-permute-start(bf16[256,256]{1,0:T(8,128)(2,1)S(1)} %collective-permute-done.1), channel_id=1, source_target_pairs={{0,8},{4,12},{8,0},{12,4},{16,24},{20,28},{24,16},{28,20},{1,9},{5... | collective-permute-start | bytes 393224 | tf_op jit(solution)/shard_map/ppermute | solution.py:21
  14.1 1.8 %collective-permute-done.11 = bf16[256,256]{1,0:T(8,128)(2,1)S(1)} collective-permute-done((bf16[256,256]{1,0:T(8,128)(2,1)S(1)}, bf16[256,256]{1,0:T(8,128)(2,1)S(1)}, u32[]{:S(2)}, u32[]{:S(2)}) %collective-permute-start.11) | collective-permute-done | bytes 131104 | tf_op jit(solution)/shard_map/ppermute | solution.py:21
  16.8 2.0 %collective-permute-start.6 = (bf16[512,256]{1,0:T(8,128)(2,1)S(1)}, bf16[512,256]{1,0:T(8,128)(2,1)S(1)}, u32[]{:S(2)}, u32[]{:S(2)}) collective-permute-start(bf16[512,256]{1,0:T(8,128)(2,1)S(1)} %slice.46), channel_id=1, source_target_pairs={{0,16},{4,20},{8,24},{12,28},{16,0},{20,4},{24,8},{28,12},{1,17},{... | collective-permute-start | bytes 786440 | tf_op jit(solution)/shard_map/ppermute | solution.py:21
  22.8 1.6 %collective-permute-start.17 = (bf16[512,256]{1,0:T(8,128)(2,1)S(1)}, bf16[512,256]{1,0:T(8,128)(2,1)S(1)}, u32[]{:S(2)}, u32[]{:S(2)}) collective-permute-start(bf16[512,256]{1,0:T(8,128)(2,1)S(1)} %get-tuple-element.44), channel_id=1, source_target_pairs={{0,1},{1,0},{2,3},{3,2},{4,5},{5,4},{6,7},{7,6},{8,9},{9,8},{10,11... | collective-permute-start | bytes 786440 | tf_op jit(solution)/shard_map/ppermute | solution.py:21
  25.8 3.0 %collective-permute-done.4.refs_2_ = bf16[512,256]{1,0:T(8,128)(2,1)S(1)} collective-permute-done((bf16[512,256]{1,0:T(8,128)(2,1)S(1)}, bf16[512,256]{1,0:T(8,128)(2,1)S(1)}, u32[]{:S(2)}, u32[]{:S(2)}) %collective-permute-start.4) | collective-permute-done | bytes 262176 | tf_op jit(solution)/shard_map/ppermute | solution.py:21
  28.8 2.1 %collective-permute-done.17 = bf16[512,256]{1,0:T(8,128)(2,1)S(1)} collective-permute-done((bf16[512,256]{1,0:T(8,128)(2,1)S(1)}, bf16[512,256]{1,0:T(8,128)(2,1)S(1)}, u32[]{:S(2)}, u32[]{:S(2)}) %collective-permute-start.17) | collective-permute-done | bytes 262176 | tf_op jit(solution)/shard_map/ppermute | solution.py:21
  31.0 1.6 %collective-permute-start.19 = (bf16[512,256]{1,0:T(8,128)(2,1)S(1)}, bf16[512,256]{1,0:T(8,128)(2,1)S(1)}, u32[]{:S(2)}, u32[]{:S(2)}) collective-permute-start(bf16[512,256]{1,0:T(8,128)(2,1)S(1)} %get-tuple-element.46), channel_id=1, source_target_pairs={{0,1},{1,0},{2,3},{3,2},{4,5},{5,4},{6,7},{7,6},{8,9},{9,8},{10,11... | collective-permute-start | bytes 786440 | tf_op jit(solution)/shard_map/ppermute | solution.py:21
  32.6 2.7 %collective-permute-start.18 = (bf16[512,256]{1,0:T(8,128)(2,1)S(1)}, bf16[512,256]{1,0:T(8,128)(2,1)S(1)}, u32[]{:S(2)}, u32[]{:S(2)}) collective-permute-start(bf16[512,256]{1,0:T(8,128)(2,1)S(1)} %add_convert_fusion), channel_id=1, source_target_pairs={{0,2},{1,3},{2,0},{3,1},{4,6},{5,7},{6,4},{7,5},{8,10},{9,11},{10,... | collective-permute-start | bytes 786440 | tf_op jit(solution)/shard_map/ppermute | solution.py:21
  38.9 6.8 %collective-permute-done.19.refs_2_ = bf16[512,256]{1,0:T(8,128)(2,1)S(1)} collective-permute-done((bf16[512,256]{1,0:T(8,128)(2,1)S(1)}, bf16[512,256]{1,0:T(8,128)(2,1)S(1)}, u32[]{:S(2)}, u32[]{:S(2)}) %collective-permute-start.19) | collective-permute-done | bytes 262176 | tf_op jit(solution)/shard_map/ppermute | solution.py:21
  46.0 3.5 %collective-permute-done.16 = bf16[512,256]{1,0:T(8,128)(2,1)S(1)} collective-permute-done((bf16[512,256]{1,0:T(8,128)(2,1)S(1)}, bf16[512,256]{1,0:T(8,128)(2,1)S(1)}, u32[]{:S(2)}, u32[]{:S(2)}) %collective-permute-start.16) | collective-permute-done | bytes 262176 | tf_op jit(solution)/shard_map/ppermute | solution.py:21
  49.6 2.7 %collective-permute-start.20 = (bf16[512,256]{1,0:T(8,128)(2,1)S(1)}, bf16[512,256]{1,0:T(8,128)(2,1)S(1)}, u32[]{:S(2)}, u32[]{:S(2)}) collective-permute-start(bf16[512,256]{1,0:T(8,128)(2,1)S(1)} %add_convert_fusion.1), channel_id=1, source_target_pairs={{0,2},{1,3},{2,0},{3,1},{4,6},{5,7},{6,4},{7,5},{8,10},{9,11},{10,... | collective-permute-start | bytes 786440 | tf_op jit(solution)/shard_map/ppermute | solution.py:21
  52.3 1.6 %collective-permute-start.21 = (bf16[128,256]{1,0:T(8,128)(2,1)S(1)}, bf16[128,256]{1,0:T(8,128)(2,1)S(1)}, u32[]{:S(2)}, u32[]{:S(2)}) collective-permute-start(bf16[128,256]{1,0:T(8,128)(2,1)S(1)} %get-tuple-element.65), channel_id=1, source_target_pairs={{0,1},{1,0},{2,3},{3,2},{4,5},{5,4},{6,7},{7,6},{8,9},{9,8},{10,11... | collective-permute-start | bytes 196616 | tf_op jit(solution)/shard_map/ppermute | solution.py:21
  56.4 3.3 %collective-permute-done.21 = bf16[128,256]{1,0:T(8,128)(2,1)S(1)} collective-permute-done((bf16[128,256]{1,0:T(8,128)(2,1)S(1)}, bf16[128,256]{1,0:T(8,128)(2,1)S(1)}, u32[]{:S(2)}, u32[]{:S(2)}) %collective-permute-start.21) | collective-permute-done | bytes 65568 | tf_op jit(solution)/shard_map/ppermute | solution.py:21
  60.4 2.6 %collective-permute-done.23 = bf16[128,256]{1,0:T(8,128)(2,1)S(1)} collective-permute-done((bf16[128,256]{1,0:T(8,128)(2,1)S(1)}, bf16[128,256]{1,0:T(8,128)(2,1)S(1)}, u32[]{:S(2)}, u32[]{:S(2)}) %collective-permute-start.23) | collective-permute-done | bytes 65568 | tf_op jit(solution)/shard_map/ppermute | solution.py:21
  68.9 1.6 %collective-permute-start.27 = (bf16[64,512]{1,0:T(8,128)(2,1)S(1)}, bf16[64,512]{1,0:T(8,128)(2,1)S(1)}, u32[]{:S(2)}, u32[]{:S(2)}) collective-permute-start(bf16[64,512]{1,0:T(8,128)(2,1)S(1)} %get-tuple-element.64), channel_id=1, source_target_pairs={{0,16},{4,20},{8,24},{12,28},{16,0},{20,4},{24,8},{28,12},{1,17},{... | collective-permute-start | bytes 196616 | tf_op jit(solution)/shard_map/ppermute | solution.py:21
  73.9 2.4 %collective-permute-start.31 = (bf16[64,512]{1,0:T(8,128)(2,1)S(1)}, bf16[64,512]{1,0:T(8,128)(2,1)S(1)}, u32[]{:S(2)}, u32[]{:S(2)}) collective-permute-start(bf16[64,512]{1,0:T(8,128)(2,1)S(1)} %fusion.2), channel_id=1, source_target_pairs={{0,3},{1,2},{2,1},{3,0},{4,7},{5,6},{6,5},{7,4},{8,11},{9,10},{10,... | collective-permute-start | bytes 196616 | tf_op jit(solution)/shard_map/ppermute | solution.py:21
  76.3 2.1 %collective-permute-start.29 = (bf16[64,512]{1,0:T(8,128)(2,1)S(1)}, bf16[64,512]{1,0:T(8,128)(2,1)S(1)}, u32[]{:S(2)}, u32[]{:S(2)}) collective-permute-start(bf16[64,512]{1,0:T(8,128)(2,1)S(1)} %fusion.2), channel_id=1, source_target_pairs={{0,1},{1,0},{2,3},{3,2},{4,5},{5,4},{6,7},{7,6},{8,9},{9,8},{10,11... | collective-permute-start | bytes 196616 | tf_op jit(solution)/shard_map/ppermute | solution.py:21
  78.3 2.3 %collective-permute-done.31 = bf16[64,512]{1,0:T(8,128)(2,1)S(1)} collective-permute-done((bf16[64,512]{1,0:T(8,128)(2,1)S(1)}, bf16[64,512]{1,0:T(8,128)(2,1)S(1)}, u32[]{:S(2)}, u32[]{:S(2)}) %collective-permute-start.31) | collective-permute-done | bytes 65568 | tf_op jit(solution)/shard_map/ppermute | solution.py:21
  80.7 1.8 %collective-permute-done.30 = bf16[64,512]{1,0:T(8,128)(2,1)S(1)} collective-permute-done((bf16[64,512]{1,0:T(8,128)(2,1)S(1)}, bf16[64,512]{1,0:T(8,128)(2,1)S(1)}, u32[]{:S(2)}, u32[]{:S(2)}) %collective-permute-start.30) | collective-permute-done | bytes 65568 | tf_op jit(solution)/shard_map/ppermute | solution.py:21
  82.5 1.7 %collective-permute-start.37 = (bf16[64,512]{1,0:T(8,128)(2,1)S(1)}, bf16[64,512]{1,0:T(8,128)(2,1)S(1)}, u32[]{:S(2)}, u32[]{:S(2)}) collective-permute-start(bf16[64,512]{1,0:T(8,128)(2,1)S(1)} %add_convert_fusion.2.refs_0_), channel_id=1, source_target_pairs={{0,24},{4,28},{8,16},{12,20},{16,8},{20,12},{24,0},{28,4},{1,25},{... | collective-permute-start | bytes 196616 | tf_op jit(solution)/shard_map/ppermute | solution.py:21
  86.1 2.0 %collective-permute-done.37.refs_3_ = bf16[64,512]{1,0:T(8,128)(2,1)S(1)} collective-permute-done((bf16[64,512]{1,0:T(8,128)(2,1)S(1)}, bf16[64,512]{1,0:T(8,128)(2,1)S(1)}, u32[]{:S(2)}, u32[]{:S(2)}) %collective-permute-start.37) | collective-permute-done | bytes 65568 | tf_op jit(solution)/shard_map/ppermute | solution.py:21
  (92 shorter events, 30.8 us)
Async XLA Ops:
  1.6 6.9 %collective-permute-start.1 = (bf16[256,256]{1,0:T(8,128)(2,1)S(1)}, bf16[256,256]{1,0:T(8,128)(2,1)S(1)}, u32[]{:S(2)}, u32[]{:S(2)}) collective-permute-start(bf16[256,256]{1,0:T(8,128)(2,1)S(1)} %get-tuple-element.60), channel_id=1, source_target_pairs={{0,16},{4,20},{8,24},{12,28},{16,0},{20,4},{24,8},{28,12},{1,17},{... | collective-permute-start | bytes 393224 | tf_op jit(solution)/shard_map/ppermute | solution.py:21
  4.7 6.3 %collective-permute-start = (bf16[256,256]{1,0:T(8,128)(2,1)S(1)}, bf16[256,256]{1,0:T(8,128)(2,1)S(1)}, u32[]{:S(2)}, u32[]{:S(2)}) collective-permute-start(bf16[256,256]{1,0:T(8,128)(2,1)S(1)} %get-tuple-element.61), channel_id=1, source_target_pairs={{0,8},{4,12},{8,0},{12,4},{16,24},{20,28},{24,16},{28,20},{1,9},{5... | collective-permute-start | bytes 393224 | tf_op jit(solution)/shard_map/ppermute | solution.py:21
  6.2 6.8 %collective-permute-start.9 = (bf16[256,256]{1,0:T(8,128)(2,1)S(1)}, bf16[256,256]{1,0:T(8,128)(2,1)S(1)}, u32[]{:S(2)}, u32[]{:S(2)}) collective-permute-start(bf16[256,256]{1,0:T(8,128)(2,1)S(1)} %get-tuple-element.61), channel_id=1, source_target_pairs={{0,16},{4,20},{8,24},{12,28},{16,0},{20,4},{24,8},{28,12},{1,17},{... | collective-permute-start | bytes 393224 | tf_op jit(solution)/shard_map/ppermute | solution.py:21
  6.7 6.9 %collective-permute-start.3 = (bf16[256,256]{1,0:T(8,128)(2,1)S(1)}, bf16[256,256]{1,0:T(8,128)(2,1)S(1)}, u32[]{:S(2)}, u32[]{:S(2)}) collective-permute-start(bf16[256,256]{1,0:T(8,128)(2,1)S(1)} %get-tuple-element.60), channel_id=1, source_target_pairs={{0,8},{4,12},{8,0},{12,4},{16,24},{20,28},{24,16},{28,20},{1,9},{5... | collective-permute-start | bytes 393224 | tf_op jit(solution)/shard_map/ppermute | solution.py:21
  13.0 8.2 %collective-permute-start.2 = (bf16[512,512]{1,0:T(8,128)(2,1)S(1)}, bf16[512,512]{1,0:T(8,128)(2,1)S(1)}, u32[]{:S(2)}, u32[]{:S(2)}) collective-permute-start(bf16[512,512]{1,0:T(8,128)(2,1)S(1)} %copy-done), channel_id=1, source_target_pairs={{0,4},{4,0},{8,12},{12,8},{16,20},{20,16},{24,28},{28,24},{1,5},{5... | collective-permute-start | bytes 1572872 | tf_op jit(solution)/shard_map/ppermute | solution.py:21
  13.6 6.1 %collective-permute-start.8 = (bf16[512,256]{1,0:T(8,128)(2,1)S(1)}, bf16[512,256]{1,0:T(8,128)(2,1)S(1)}, u32[]{:S(2)}, u32[]{:S(2)}) collective-permute-start(bf16[512,256]{1,0:T(8,128)(2,1)S(1)} %constant_dynamic-update-slice_fusion.refs_2_), channel_id=1, source_target_pairs={{0,4},{4,0},{8,12},{12,8},{16,20},{20,16},{24,28},{28,24},{1,5},{5... | collective-permute-start | bytes 786440 | tf_op jit(solution)/shard_map/ppermute | solution.py:21
  13.7 7.5 %collective-permute-start.10 = (bf16[512,256]{1,0:T(8,128)(2,1)S(1)}, bf16[512,256]{1,0:T(8,128)(2,1)S(1)}, u32[]{:S(2)}, u32[]{:S(2)}) collective-permute-start(bf16[512,256]{1,0:T(8,128)(2,1)S(1)} %constant_dynamic-update-slice_fusion.2.refs_4_), channel_id=1, source_target_pairs={{0,4},{4,0},{8,12},{12,8},{16,20},{20,16},{24,28},{28,24},{1,5},{5... | collective-permute-start | bytes 786440 | tf_op jit(solution)/shard_map/ppermute | solution.py:21
  16.8 9.0 %collective-permute-start.6 = (bf16[512,256]{1,0:T(8,128)(2,1)S(1)}, bf16[512,256]{1,0:T(8,128)(2,1)S(1)}, u32[]{:S(2)}, u32[]{:S(2)}) collective-permute-start(bf16[512,256]{1,0:T(8,128)(2,1)S(1)} %slice.46), channel_id=1, source_target_pairs={{0,16},{4,20},{8,24},{12,28},{16,0},{20,4},{24,8},{28,12},{1,17},{... | collective-permute-start | bytes 786440 | tf_op jit(solution)/shard_map/ppermute | solution.py:21
  19.6 9.2 %collective-permute-start.4 = (bf16[512,256]{1,0:T(8,128)(2,1)S(1)}, bf16[512,256]{1,0:T(8,128)(2,1)S(1)}, u32[]{:S(2)}, u32[]{:S(2)}) collective-permute-start(bf16[512,256]{1,0:T(8,128)(2,1)S(1)} %slice.46), channel_id=1, source_target_pairs={{0,8},{4,12},{8,0},{12,4},{16,24},{20,28},{24,16},{28,20},{1,9},{5... | collective-permute-start | bytes 786440 | tf_op jit(solution)/shard_map/ppermute | solution.py:21
  22.8 8.2 %collective-permute-start.17 = (bf16[512,256]{1,0:T(8,128)(2,1)S(1)}, bf16[512,256]{1,0:T(8,128)(2,1)S(1)}, u32[]{:S(2)}, u32[]{:S(2)}) collective-permute-start(bf16[512,256]{1,0:T(8,128)(2,1)S(1)} %get-tuple-element.44), channel_id=1, source_target_pairs={{0,1},{1,0},{2,3},{3,2},{4,5},{5,4},{6,7},{7,6},{8,9},{9,8},{10,11... | collective-permute-start | bytes 786440 | tf_op jit(solution)/shard_map/ppermute | solution.py:21
  24.4 10.9 %collective-permute-start.14 = (bf16[512,256]{1,0:T(8,128)(2,1)S(1)}, bf16[512,256]{1,0:T(8,128)(2,1)S(1)}, u32[]{:S(2)}, u32[]{:S(2)}) collective-permute-start(bf16[512,256]{1,0:T(8,128)(2,1)S(1)} %slice.47), channel_id=1, source_target_pairs={{0,24},{4,28},{8,16},{12,20},{16,8},{20,12},{24,0},{28,4},{1,25},{... | collective-permute-start | bytes 786440 | tf_op jit(solution)/shard_map/ppermute | solution.py:21
  25.8 9.5 %collective-permute-start.7 = (bf16[512,256]{1,0:T(8,128)(2,1)S(1)}, bf16[512,256]{1,0:T(8,128)(2,1)S(1)}, u32[]{:S(2)}, u32[]{:S(2)}) collective-permute-start(bf16[512,256]{1,0:T(8,128)(2,1)S(1)} %collective-permute-done.6.refs_4_), channel_id=1, source_target_pairs={{0,4},{4,0},{8,12},{12,8},{16,20},{20,16},{24,28},{28,24},{1,5},{5... | collective-permute-start | bytes 786440 | tf_op jit(solution)/shard_map/ppermute | solution.py:21
  28.8 6.5 %collective-permute-start.5 = (bf16[512,256]{1,0:T(8,128)(2,1)S(1)}, bf16[512,256]{1,0:T(8,128)(2,1)S(1)}, u32[]{:S(2)}, u32[]{:S(2)}) collective-permute-start(bf16[512,256]{1,0:T(8,128)(2,1)S(1)} %collective-permute-done.4.refs_2_), channel_id=1, source_target_pairs={{0,4},{4,0},{8,12},{12,8},{16,20},{20,16},{24,28},{28,24},{1,5},{5... | collective-permute-start | bytes 786440 | tf_op jit(solution)/shard_map/ppermute | solution.py:21
  31.0 14.7 %collective-permute-start.19 = (bf16[512,256]{1,0:T(8,128)(2,1)S(1)}, bf16[512,256]{1,0:T(8,128)(2,1)S(1)}, u32[]{:S(2)}, u32[]{:S(2)}) collective-permute-start(bf16[512,256]{1,0:T(8,128)(2,1)S(1)} %get-tuple-element.46), channel_id=1, source_target_pairs={{0,1},{1,0},{2,3},{3,2},{4,5},{5,4},{6,7},{7,6},{8,9},{9,8},{10,11... | collective-permute-start | bytes 786440 | tf_op jit(solution)/shard_map/ppermute | solution.py:21
  32.6 13.0 %collective-permute-start.18 = (bf16[512,256]{1,0:T(8,128)(2,1)S(1)}, bf16[512,256]{1,0:T(8,128)(2,1)S(1)}, u32[]{:S(2)}, u32[]{:S(2)}) collective-permute-start(bf16[512,256]{1,0:T(8,128)(2,1)S(1)} %add_convert_fusion), channel_id=1, source_target_pairs={{0,2},{1,3},{2,0},{3,1},{4,6},{5,7},{6,4},{7,5},{8,10},{9,11},{10,... | collective-permute-start | bytes 786440 | tf_op jit(solution)/shard_map/ppermute | solution.py:21
  38.4 11.1 %collective-permute-start.16 = (bf16[512,256]{1,0:T(8,128)(2,1)S(1)}, bf16[512,256]{1,0:T(8,128)(2,1)S(1)}, u32[]{:S(2)}, u32[]{:S(2)}) collective-permute-start(bf16[512,256]{1,0:T(8,128)(2,1)S(1)} %get-tuple-element.42), channel_id=1, source_target_pairs={{0,1},{1,0},{2,3},{3,2},{4,5},{5,4},{6,7},{7,6},{8,9},{9,8},{10,11... | collective-permute-start | bytes 786440 | tf_op jit(solution)/shard_map/ppermute | solution.py:21
  49.6 14.2 %collective-permute-start.20 = (bf16[512,256]{1,0:T(8,128)(2,1)S(1)}, bf16[512,256]{1,0:T(8,128)(2,1)S(1)}, u32[]{:S(2)}, u32[]{:S(2)}) collective-permute-start(bf16[512,256]{1,0:T(8,128)(2,1)S(1)} %add_convert_fusion.1), channel_id=1, source_target_pairs={{0,2},{1,3},{2,0},{3,1},{4,6},{5,7},{6,4},{7,5},{8,10},{9,11},{10,... | collective-permute-start | bytes 786440 | tf_op jit(solution)/shard_map/ppermute | solution.py:21
  52.3 7.4 %collective-permute-start.21 = (bf16[128,256]{1,0:T(8,128)(2,1)S(1)}, bf16[128,256]{1,0:T(8,128)(2,1)S(1)}, u32[]{:S(2)}, u32[]{:S(2)}) collective-permute-start(bf16[128,256]{1,0:T(8,128)(2,1)S(1)} %get-tuple-element.65), channel_id=1, source_target_pairs={{0,1},{1,0},{2,3},{3,2},{4,5},{5,4},{6,7},{7,6},{8,9},{9,8},{10,11... | collective-permute-start | bytes 196616 | tf_op jit(solution)/shard_map/ppermute | solution.py:21
  53.9 6.5 %collective-permute-start.24 = (bf16[128,256]{1,0:T(8,128)(2,1)S(1)}, bf16[128,256]{1,0:T(8,128)(2,1)S(1)}, u32[]{:S(2)}, u32[]{:S(2)}) collective-permute-start(bf16[128,256]{1,0:T(8,128)(2,1)S(1)} %get-tuple-element.66), channel_id=1, source_target_pairs={{0,1},{1,0},{2,3},{3,2},{4,5},{5,4},{6,7},{7,6},{8,9},{9,8},{10,11... | collective-permute-start | bytes 196616 | tf_op jit(solution)/shard_map/ppermute | solution.py:21
  54.4 8.6 %collective-permute-start.23 = (bf16[128,256]{1,0:T(8,128)(2,1)S(1)}, bf16[128,256]{1,0:T(8,128)(2,1)S(1)}, u32[]{:S(2)}, u32[]{:S(2)}) collective-permute-start(bf16[128,256]{1,0:T(8,128)(2,1)S(1)} %get-tuple-element.67), channel_id=1, source_target_pairs={{0,1},{1,0},{2,3},{3,2},{4,5},{5,4},{6,7},{7,6},{8,9},{9,8},{10,11... | collective-permute-start | bytes 196616 | tf_op jit(solution)/shard_map/ppermute | solution.py:21
  55.9 7.8 %collective-permute-start.22 = (bf16[128,256]{1,0:T(8,128)(2,1)S(1)}, bf16[128,256]{1,0:T(8,128)(2,1)S(1)}, u32[]{:S(2)}, u32[]{:S(2)}) collective-permute-start(bf16[128,256]{1,0:T(8,128)(2,1)S(1)} %get-tuple-element.68), channel_id=1, source_target_pairs={{0,1},{1,0},{2,3},{3,2},{4,5},{5,4},{6,7},{7,6},{8,9},{9,8},{10,11... | collective-permute-start | bytes 196616 | tf_op jit(solution)/shard_map/ppermute | solution.py:21
  73.9 6.8 %collective-permute-start.31 = (bf16[64,512]{1,0:T(8,128)(2,1)S(1)}, bf16[64,512]{1,0:T(8,128)(2,1)S(1)}, u32[]{:S(2)}, u32[]{:S(2)}) collective-permute-start(bf16[64,512]{1,0:T(8,128)(2,1)S(1)} %fusion.2), channel_id=1, source_target_pairs={{0,3},{1,2},{2,1},{3,0},{4,7},{5,6},{6,5},{7,4},{8,11},{9,10},{10,... | collective-permute-start | bytes 196616 | tf_op jit(solution)/shard_map/ppermute | solution.py:21
  76.3 6.2 %collective-permute-start.30 = (bf16[64,512]{1,0:T(8,128)(2,1)S(1)}, bf16[64,512]{1,0:T(8,128)(2,1)S(1)}, u32[]{:S(2)}, u32[]{:S(2)}) collective-permute-start(bf16[64,512]{1,0:T(8,128)(2,1)S(1)} %fusion.2), channel_id=1, source_target_pairs={{0,2},{1,3},{2,0},{3,1},{4,6},{5,7},{6,4},{7,5},{8,10},{9,11},{10,... | collective-permute-start | bytes 196616 | tf_op jit(solution)/shard_map/ppermute | solution.py:21
  76.3 6.2 %collective-permute-start.29 = (bf16[64,512]{1,0:T(8,128)(2,1)S(1)}, bf16[64,512]{1,0:T(8,128)(2,1)S(1)}, u32[]{:S(2)}, u32[]{:S(2)}) collective-permute-start(bf16[64,512]{1,0:T(8,128)(2,1)S(1)} %fusion.2), channel_id=1, source_target_pairs={{0,1},{1,0},{2,3},{3,2},{4,5},{5,4},{6,7},{7,6},{8,9},{9,8},{10,11... | collective-permute-start | bytes 196616 | tf_op jit(solution)/shard_map/ppermute | solution.py:21
  (20 other events, 98.6 us)
